TPU v7x, 512 devices: a whole 4x4x16 slice. The times are simulated.
512 devices in a mesh: dp: 64 (over z_lo, y, core), feat: 8 (over z_hi, x).
Axes of the slice: x: 4, y: 4, z: 16 (z_hi: 2, z_lo: 8; z = z_hi * 8 + z_lo), core: 2. Of those that a mesh axis runs over, the one named last changes fastest.
Arguments:
- view_a: bfloat16 [512, 16384], P('dp', 'feat'), may hold values from -100 to 100
- view_b: bfloat16 [512, 16384], P('dp'), may hold values from -100 to 100
Outputs:
- correlation: float32 [16384, 16384], P('feat', 'dp')
- grad_a: float32 [512, 16384], P('dp', 'feat')
- grad_b: float32 [512, 16384], P(None, 'dp')
All inputs are finite; a program needn't handle non-finite values.
Results may differ from a plain program's by a relative error of at most 0.0065.
Values may be sent and summed in bfloat16 or wider, within the bound.
No kernel may reach another device: no remote copies, remote signals or barrier semaphores. Data moves between devices by JAX's collectives and lax.ppermute only.
A program may use at most 64 MiB of HBM per device.

v0:
```python
import jax
import jax.numpy as jnp
from jax import lax
from jax.sharding import PartitionSpec as P

epsilon = 1e-05
off_weight = 0.005


def split_halves(values):
    upper = values.astype(jnp.bfloat16)
    lower = (values - upper.astype(jnp.float32)).astype(jnp.bfloat16)
    return (upper, lower)


def paired_product(left, halves, dims):
    first = lax.dot_general(left, halves[0], dims, preferred_element_type=jnp.float32)
    return first + lax.dot_general(left, halves[1], dims, preferred_element_type=jnp.float32)


def local(view_a, view_b):
    images_dev = view_a.shape[0]
    cols_a = view_a.shape[1]
    width = view_b.shape[1]
    groups = lax.axis_size("dp")
    all_images = images_dev * groups
    cols_b = width // groups
    feat_index = lax.axis_index("feat")
    dp_index = lax.axis_index("dp")
    float_a = view_a.astype(jnp.float32)
    float_b = view_b.astype(jnp.float32)
    sum_a, square_a, sum_b, square_b = lax.psum(
        (
            jnp.sum(float_a, 0),
            jnp.sum(float_a * float_a, 0),
            jnp.sum(float_b, 0),
            jnp.sum(float_b * float_b, 0),
        ),
        "dp",
    )
    mean_a = sum_a / all_images
    inverse_a = lax.rsqrt(square_a / all_images - mean_a * mean_a + epsilon)
    mean_b = sum_b / all_images
    inverse_b = lax.rsqrt(square_b / all_images - mean_b * mean_b + epsilon)
    norm_a = ((float_a - mean_a) * inverse_a).astype(jnp.bfloat16)
    norm_b = ((float_b - mean_b) * inverse_b).astype(jnp.bfloat16)
    whole_a = lax.all_gather(norm_a, "dp", axis=0, tiled=True)
    column_b = lax.all_to_all(norm_b, "dp", split_axis=1, concat_axis=0, tiled=True)
    correlation = (
        lax.dot_general(
            whole_a, column_b, (((0,), (0,)), ((), ())), preferred_element_type=jnp.float32
        )
        / all_images
    )
    row_ids = feat_index * cols_a + lax.iota(jnp.int32, cols_a)
    col_ids = dp_index * cols_b + lax.iota(jnp.int32, cols_b)
    on_diag = row_ids[:, None] == col_ids[None, :]
    column_f = column_b.astype(jnp.float32)
    squares = jnp.sum(correlation * correlation, 1)
    diag_part = jnp.sum(jnp.where(on_diag, correlation, 0.0), 1)
    squares, diagonal = lax.psum((squares, diag_part), "dp")
    shift = -2.0 * (1.0 - diagonal) - 2.0 * off_weight * diagonal
    grad_tile = 2.0 * off_weight * correlation + jnp.where(on_diag, shift[:, None], 0.0)
    tile_halves = split_halves(grad_tile)
    projected = 2.0 * off_weight * squares + shift * diagonal
    grad_a_n = lax.psum_scatter(
        paired_product(column_b, tile_halves, (((1,), (1,)), ((), ()))),
        "dp",
        scatter_dimension=0,
        tiled=True,
    )
    grad_a = (grad_a_n - norm_a.astype(jnp.float32) * projected) * inverse_a
    part_b = paired_product(whole_a, tile_halves, (((1,), (0,)), ((), ())))
    grad_b_n = lax.psum(part_b, "feat")
    inverse_cols = lax.dynamic_slice_in_dim(inverse_b, dp_index * cols_b, cols_b, 0)
    grad_b = (grad_b_n - column_f * jnp.mean(grad_b_n * column_f, 0)) * inverse_cols
    return (correlation, grad_a, grad_b)


def solution(mesh):
    in_specs = (P("dp", "feat"), P("dp", None))
    out_specs = (P("feat", "dp"), P("dp", "feat"), P(None, "dp"))
    return jax.shard_map(local, mesh=mesh, in_specs=in_specs, out_specs=out_specs, check_vma=False)
```

profile of v0, /device:TPU:4, one launch (start us, length us, event | category | flops | bytes accessed | tf_op | source)
XLA Modules:
  0.0 1927.5 jit_solution(18349858759989907964)
XLA Ops:
  7.2 0.0 all-reduce.8.cloned.1.call-start
  7.2 1.9 convert_reduce_fusion
  9.1 0.0 all-reduce.8.cloned.1.call-update
  9.2 0.0 all-gather.2.cloned.1.call-start
  9.2 0.8 convert_reduce_fusion.1
  10.0 431.8 %all-reduce.1 = (f32[2048]{0:T(1024)S(1)}, f32[2048]{0:T(1024)S(1)}) all-reduce(f32[2048]{0:T(1024)S(1)} %get-tuple-element.11, f32[2048]{0:T(1024)S(1)} %get-tuple-element.10), channel_id=1, replica_groups=mesh['dp'=64,'feat'=8] {'dp'}, use_global_device_ids=true, to_apply=%region_3.0 | all-reduce | flops 4096 | bytes 32768 | tf_op jit(solution)/shard_map/psum | solution.py:32
  441.9 1.4 fusion.15
  443.2 0.0 all-gather.2.cloned.1.call-update
  443.3 335.8 %all-reduce.8.cloned.1.call-done = (f32[16384]{0:T(1024)}, f32[16384]{0:T(1024)}) async-done(((f32[16384]{0:T(1024)}, f32[16384]{0:T(1024)}), (f32[16384]{0:T(1024)}, f32[16384]{0:T(1024)})) %all-reduce.8.cloned.1.call-update) | async-done | bytes 131088 | tf_op jit(solution)/shard_map/psum | solution.py:32
  779.1 0.9 broadcast_multiply_fusion.1
  780.0 1.7 fusion.7
  781.7 10.1 all-to-all-start
  791.8 0.0 all-reduce.6.cloned.1.call-start
  791.9 20.3 %all-to-all-done = bf16[8,64,256]{2,0,1:T(8,128)(2,1)S(1)} async-done(((bf16[8,64,256]{2,0,1:T(8,128)(2,1)}), bf16[8,64,256]{2,0,1:T(8,128)(2,1)S(1)}, u32[]{:S(2)}, u32[]{:S(2)}) %all-to-all-start) | async-done | bytes 262176 | tf_op jit(solution)/shard_map/all_to_all | solution.py:48
  812.2 89.8 %all-gather.2.cloned.1.call-done = bf16[512,2048]{1,0:T(8,128)(2,1)} async-done(((bf16[8,2048]{1,0:T(8,128)(2,1)}), bf16[512,2048]{1,0:T(8,128)(2,1)}) %all-gather.2.cloned.1.call-update) | async-done | bytes 2097168 | tf_op jit(solution)/shard_map/all_gather | solution.py:47
  902.0 3.9 multiply_reduce_fusion
  905.9 423.3 %all-reduce = (f32[2048]{0:T(1024)S(1)}, f32[2048]{0:T(1024)S(1)}) all-reduce(f32[2048]{0:T(1024)S(1)} %get-tuple-element.7, f32[2048]{0:T(1024)S(1)} %get-tuple-element.6), channel_id=1, replica_groups=mesh['dp'=64,'feat'=8] {'dp'}, use_global_device_ids=true, to_apply=%region_9.10 | all-reduce | flops 4096 | bytes 32768 | tf_op jit(solution)/shard_map/psum | solution.py:61
  1329.2 0.0 copy-start.2
  1329.2 2.6 fusion.17
  1331.8 0.0 copy-done.2
  1331.8 1.7 convolution_add_fusion.1
  1333.6 0.0 all-reduce.6.cloned.1.call-update
  1333.6 0.0 reduce-scatter.2.cloned.1.call-start
  1333.7 0.9 fusion.10
  1334.5 2.8 convolution_add_fusion
  1337.4 0.0 copy-start
  1337.4 0.0 reduce-scatter.2.cloned.1.call-update
  1337.4 0.1 dynamic_slice.3
  1337.5 1.5 copy-done
  1339.0 1.8 copy.5
  1340.8 0.0 copy-start.1
  1340.8 131.5 %all-reduce.6.cloned.1.call-done = f32[512,256]{1,0:T(8,128)} async-done(((f32[512,256]{1,0:T(8,128)}), f32[512,256]{1,0:T(8,128)}) %all-reduce.6.cloned.1.call-update) | async-done | bytes 524304 | tf_op jit(solution)/shard_map/psum | solution.py:74
  1472.2 1.1 fusion.3
  1473.4 1.9 fusion.5
  1475.3 444.2 %reduce-scatter.2.cloned.1.call-done = f32[8,2048]{1,0:T(8,128)} async-done(((f32[512,2048]{1,0:T(8,128)}), f32[8,2048]{1,0:T(8,128)}) %reduce-scatter.2.cloned.1.call-update) | async-done | bytes 65552 | tf_op jit(solution)/shard_map/reduce_scatter | solution.py:66
  1919.5 0.0 copy-done.1
  1919.5 1.5 subtract_multiply_fusion
  (5 shorter events, 0.0 us)
Async XLA Ops:
  7.2 771.9 %all-reduce.8.cloned.1.call-start = ((), (), s32[]{:S(2)}) async-start(), calls=%async_computation.5 | async-start | bytes 262144 | tf_op jit(solution)/shard_map/psum | solution.py:32
  9.2 892.8 %all-gather.2.cloned.1.call-start = ((), (), s32[]{:S(2)}) async-start(), calls=%async_computation.2 | async-start | bytes 2129920 | tf_op jit(solution)/shard_map/all_gather | solution.py:47
  781.7 30.5 %all-to-all-start = ((bf16[8,64,256]{2,0,1:T(8,128)(2,1)}), bf16[8,64,256]{2,0,1:T(8,128)(2,1)S(1)}, u32[]{:S(2)}, u32[]{:S(2)}) async-start(bf16[8,64,256]{2,0,1:T(8,128)(2,1)} %bitcast), calls=%async_computation | async-start | bytes 524288 | tf_op jit(solution)/shard_map/all_to_all | solution.py:48
  791.8 680.4 %all-reduce.6.cloned.1.call-start = ((), (), s32[]{:S(2)}) async-start(), calls=%async_computation.4 | async-start | bytes 1048576 | tf_op jit(solution)/shard_map/psum | solution.py:74
  1329.2 2.6 copy-start.2
  1333.6 585.9 %reduce-scatter.2.cloned.1.call-start = ((), (), s32[]{:S(2)}) async-start(), calls=%async_computation.3 | async-start | bytes 4259840 | tf_op jit(solution)/shard_map/reduce_scatter | solution.py:66
  1337.4 1.6 copy-start
  1340.8 578.8 %copy-start.1 = (bf16[8,2048]{1,0:T(8,128)(2,1)S(1)}, bf16[8,2048]{1,0:T(8,128)(2,1)}, u32[]{:S(2)}) copy-start(bf16[8,2048]{1,0:T(8,128)(2,1)} %param.2) | copy-start | bytes 98308
Sparse Core Ops, SparseCore 0:
  11.6 767.4 all-reduce.7
  782.0 119.9 all-gather.1
  1333.7 138.4 all-reduce.5
  1474.9 444.5 reduce-scatter.1
where the time goes:
time: 1930 us
  waiting for transfers between devices  1020 us (53%)
  blocking collectives  855 us (44%)
    reduce_scatter x1, waiting for transfers between devices, local(): lax.psum_scatter(paired_product(column_b, tile_halves, (((1,), (1,)), (()...  444 us
    psum x1, blocking collectives, local(): lax.psum((jnp.sum(float_a, 0), jnp.sum(float_a * float_a, 0), jnp.sum(flo...  432 us
    psum x1, blocking collectives, local(): squares, diagonal = lax.psum((squares, diag_part), 'dp')  423 us
    psum x1, waiting for transfers between devices, local(): lax.psum((jnp.sum(float_a, 0), jnp.sum(float_a * float_a, 0), jnp.sum(flo...  336 us
    psum x1, waiting for transfers between devices, local(): grad_b_n = lax.psum(part_b, 'feat')  131 us
    all_gather x1, waiting for transfers between devices, local(): whole_a = lax.all_gather(norm_a, 'dp', axis=0, tiled=True)  89.8 us
  transfers between devices with their start and end apart: 5, of which 5 were waited for; matrix products, arithmetic and copies ran while one was open for 1% of the time, Pallas kernels for 0%

commit v1 on v0

v1 whole, which is shorter than its diff:
```python
import jax
import jax.numpy as jnp
from jax import lax
from jax.sharding import Mesh, PartitionSpec as P

epsilon = 1e-05
off_weight = 0.005
f32 = jnp.float32
bf16 = jnp.bfloat16
AXES = ("zl", "y", "c", "zh", "x")
DP = ("zl", "y", "c")
FEAT = ("zh", "x")


def exchange(values, axis):
    return lax.all_to_all(values, axis, split_axis=0, concat_axis=0, tiled=False)


def split_halves(values):
    upper = values.astype(bf16)
    lower = (values - upper.astype(f32)).astype(bf16)
    return upper, lower


def dot(left, right, contract):
    return lax.dot_general(left, right, (contract, ((), ())), preferred_element_type=f32)


def standardize(values):
    images = values.shape[0]
    as_float = values.astype(f32)
    mean = jnp.sum(as_float, 0) / images
    inverse = lax.rsqrt(jnp.sum(as_float * as_float, 0) / images - mean * mean + epsilon)
    return ((as_float - mean) * inverse).astype(bf16), mean, inverse


def local(view_a, view_b):
    nz, ny, nc = (lax.axis_size(a) for a in DP)
    nh, nx = (lax.axis_size(a) for a in FEAT)
    rows, cols_a = view_a.shape
    width = view_b.shape[1]
    cols_b = width // (nz * ny * nc)
    images = rows * nz * ny * nc
    iz, iy, ic = (lax.axis_index(a) for a in DP)
    ih, ix = (lax.axis_index(a) for a in FEAT)
    feat = ih * nx + ix

    with jax.named_scope("gather_z"):
        part = width // nz
        send = jnp.concatenate(
            [
                jnp.broadcast_to(view_a[None], (nz, rows, cols_a)),
                view_b.reshape(rows, nz, part).transpose(1, 0, 2),
            ],
            2,
        )
        got = exchange(send, "zl").reshape(nz * rows, cols_a + part)
    with jax.named_scope("gather_y"):
        part = part // ny
        send = jnp.concatenate(
            [
                jnp.broadcast_to(got[None, :, :cols_a], (ny, nz * rows, cols_a)),
                got[:, cols_a:].reshape(nz * rows, ny, part).transpose(1, 0, 2),
            ],
            2,
        )
        got = exchange(send, "y").reshape(ny * nz * rows, cols_a + part)
    with jax.named_scope("gather_core"):
        part = part // nc
        send = jnp.concatenate(
            [
                jnp.broadcast_to(got[None, :, :cols_a], (nc, images // nc, cols_a)),
                got[:, cols_a:].reshape(images // nc, nc, part).transpose(1, 0, 2),
            ],
            2,
        )
        got = exchange(send, "c").reshape(images, cols_a + part)

    with jax.named_scope("tile"):
        norm_a, mean_a, inverse_a = standardize(got[:, :cols_a])
        norm_b, mean_b, inverse_b = standardize(got[:, cols_a:])
        correlation = dot(norm_a, norm_b, ((0,), (0,))) / images
        on_block = (feat == iz).astype(f32)
        first = (iy * nc + ic) * cols_b
        block = lax.dynamic_slice_in_dim(correlation, first, cols_b, 0)
        eye = jnp.eye(cols_b, dtype=f32)
        diagonal = jnp.sum(block * eye, 0)
        shift = -2.0 * (1.0 - diagonal) - 2.0 * off_weight * diagonal
        squares = jnp.sum(correlation * correlation, 1)

    with jax.named_scope("partial_b"):
        upper, lower = split_halves(2.0 * off_weight * correlation)
        part_b = dot(norm_a, upper, ((1,), (0,))) + dot(norm_a, lower, ((1,), (0,)))
        own_a = lax.dynamic_slice_in_dim(norm_a, first, cols_b, 1).astype(f32)
        part_b = part_b + own_a * (shift * on_block)
        float_b = norm_b.astype(f32)
        part_b = (part_b - float_b * jnp.mean(part_b * float_b, 0)) * inverse_b

    with jax.named_scope("sum_b_x"):
        send = part_b.astype(bf16).reshape(nx, images // nx, cols_b)
        sum_b = jnp.sum(exchange(send, "x").astype(f32), 0)

    with jax.named_scope("gram"):
        blocks = nc * ny * nz
        picked = lax.dynamic_index_in_dim(norm_b.reshape(blocks, rows, cols_b), feat, 1, False)
        gram = dot(picked, norm_b, ((1,), (1,)))
        pad = jnp.zeros((cols_b,), f32)
        aux = jnp.concatenate([mean_b, inverse_b, diagonal, pad]).reshape(2, images)
        squares = squares.reshape(-1, images)
        n_sq = squares.shape[0]
    with jax.named_scope("reduce_z"):
        send = jnp.concatenate(
            [
                gram.reshape(nc, ny, nz, images).transpose(2, 1, 0, 3).reshape(nz, ny * nc, images),
                jnp.broadcast_to(squares[None], (nz, n_sq, images)),
                jnp.broadcast_to(aux[None], (nz, 2, images)),
            ],
            1,
        )
        got = exchange(send, "zl")
        total = jnp.sum(got[:, : ny * nc + n_sq], 0)
        aux = lax.dynamic_index_in_dim(got[:, ny * nc + n_sq :], feat, 0, False)
    with jax.named_scope("reduce_yc"):
        send = jnp.concatenate(
            [
                total[: ny * nc, None],
                jnp.broadcast_to(total[None, ny * nc :], (ny * nc, n_sq, images)),
                jnp.broadcast_to(aux[None], (ny * nc, 2, images)),
            ],
            1,
        )
        got = exchange(send, ("y", "c"))
        total = jnp.sum(got[:, : 1 + n_sq], 0)
        gram = total[0]
        squares = total[1:].reshape(cols_a)
        aux = got[:, 1 + n_sq :].reshape(ny * nc, 4, cols_b).transpose(1, 0, 2).reshape(4, cols_a)
        mean_f, inverse_f, diag_f = aux[0], aux[1], aux[2]

    with jax.named_scope("sum_b_zh"):
        upper, lower = split_halves(gram.reshape(2, cols_b))
        own = jnp.concatenate([sum_b.astype(bf16), upper, lower], 0)
        n_rows = images // nx
        got = exchange(jnp.broadcast_to(own[None], (nh,) + own.shape), "zh")
        sum_b = jnp.sum(got[:, :n_rows].astype(f32), 0).astype(bf16)
        gram = got[:, n_rows:].reshape(nh * 4, cols_b)
    with jax.named_scope("gather_b_x"):
        own = jnp.concatenate([sum_b, gram], 0)
        got = exchange(jnp.broadcast_to(own[None], (nx,) + own.shape), "x")
        grad_b = got[:, :n_rows].reshape(nc, ny, nz, rows, cols_b).transpose(2, 1, 0, 3, 4)
        grad_b = grad_b.reshape(images, cols_b).astype(f32)
        gram = got[:, n_rows:].reshape(nx, nh, 2, images).transpose(2, 1, 0, 3).reshape(2, nh * nx, images)

    with jax.named_scope("grad_a"):
        shift = -2.0 * (1.0 - diag_f) - 2.0 * off_weight * diag_f
        projected = 2.0 * off_weight * squares + shift * diag_f
        both = dot(gram.reshape(2 * nh * nx, images), norm_a, ((1,), (0,)))
        scale = 2.0 * off_weight / images
        start_b = view_b_columns(view_b, feat, cols_a)
        own_b = ((start_b - mean_f) * inverse_f).astype(bf16).astype(f32)
        own_a = ((view_a.astype(f32) - mean_a) * inverse_a).astype(bf16).astype(f32)
        grad_a_n = (both[:rows] + both[rows:]) * scale + own_b * shift
        grad_a = (grad_a_n - own_a * projected) * inverse_a
    return correlation, grad_a, grad_b


def view_b_columns(view_b, feat, cols_a):
    return lax.dynamic_slice_in_dim(view_b, feat * cols_a, cols_a, 1).astype(f32)


def solution(mesh):
    sizes = (8, 4, 2, 2, 4)
    fine = Mesh(mesh.devices.reshape(sizes), AXES)
    in_specs = (P(DP, FEAT), P(DP, None))
    out_specs = (P(FEAT, DP), P(DP, FEAT), P(None, DP))
    return jax.shard_map(local, mesh=fine, in_specs=in_specs, out_specs=out_specs, check_vma=False)
```

time: 1930 us -> 159 us (0.08)
  the two profiles are of different devices: /device:TPU:4 before, /device:TPU:32 now
where the time goes in v1:
time: 159 us
  blocking collectives  68.5 us (43%)
  waiting for transfers between devices  50.9 us (32%)
  starting transfers between devices  23.2 us (15%)
  other arithmetic  6.84 us (4%)
  local copies, waits for them, and re-layouts  5.15 us (3%)
  matrix products  3.03 us (2%)
    all_to_all x3, blocking collectives, exchange(): lax.all_to_all(values, axis, split_axis=0, concat_axis=0, tiled=False)  68.5 us
    all_to_all x5, waiting for transfers between devices, exchange(): lax.all_to_all(values, axis, split_axis=0, concat_axis=0, tiled=False)  50.9 us
    all_to_all x5, starting transfers between devices, exchange(): lax.all_to_all(values, axis, split_axis=0, concat_axis=0, tiled=False)  23.2 us
  transfers between devices with their start and end apart: 5, of which 5 were waited for; matrix products, arithmetic and copies ran while one was open for 1% of the time, Pallas kernels for 0%

profile of v1, /device:TPU:32, one launch (start us, length us, event | category | flops | bytes accessed | tf_op | source)
XLA Modules:
  0.0 158.6 jit_solution(9849443223876002668)
XLA Ops:
  0.6 0.8 broadcast_in_dim.28
  1.4 1.0 pad_maximum_fusion.2
  2.4 39.3 %all_to_all.40 = bf16[8,8,4096]{2,1,0:T(8,128)(2,1)S(1)} all-to-all(bf16[8,8,4096]{2,1,0:T(8,128)(2,1)S(1)} %pad_maximum_fusion.2), channel_id=1, replica_groups=mesh['zl'=8,'y'=4,'c'=2,'zh'=2,'x'=4] {'zl'}, dimensions={0} | all-to-all | bytes 1048576 | tf_op jit(solution)/shard_map/gather_z/all_to_all | solution.py:16
  41.8 0.2 reshape.136
  42.0 0.1 broadcast_in_dim.29
  42.2 1.1 pad_maximum_fusion.1
  43.3 4.5 %all-to-all-start.1 = ((bf16[4,64,2560]{2,1,0:T(8,128)(2,1)}), bf16[4,64,2560]{2,1,0:T(8,128)(2,1)S(1)}, u32[]{:S(2)}, u32[]{:S(2)}) async-start(bf16[4,64,2560]{2,1,0:T(8,128)(2,1)} %pad_maximum_fusion.1), calls=%async_computation.1 | async-start | bytes 2621440 | tf_op jit(solution)/shard_map/gather_y/all_to_all | solution.py:16
  47.8 16.4 %all-to-all-done.1 = bf16[4,64,2560]{2,1,0:T(8,128)(2,1)S(1)} async-done(((bf16[4,64,2560]{2,1,0:T(8,128)(2,1)}), bf16[4,64,2560]{2,1,0:T(8,128)(2,1)S(1)}, u32[]{:S(2)}, u32[]{:S(2)}) %all-to-all-start.1) | async-done | bytes 1310752 | tf_op jit(solution)/shard_map/gather_y/all_to_all | solution.py:16
  64.1 0.1 slice.97
  64.3 0.1 copy.40
  64.4 0.1 copy.41
  64.6 0.2 broadcast_in_dim.30
  64.8 0.2 pad_maximum_fusion
  65.0 5.6 %all_to_all.41 = bf16[2,256,2304]{2,1,0:T(8,128)(2,1)S(1)} all-to-all(bf16[2,256,2304]{2,1,0:T(8,128)(2,1)S(1)} %pad_maximum_fusion), channel_id=1, replica_groups=mesh['zl'=8,'y'=4,'c'=2,'zh'=2,'x'=4] {'c'}, dimensions={0} | all-to-all | bytes 4718592 | tf_op jit(solution)/shard_map/gather_core/all_to_all | solution.py:16
  70.7 0.6 convert_reduce_fusion
  71.3 0.1 convert_reduce_fusion.1
  71.4 0.6 fusion.1
  72.0 0.9 multiply_reduce_fusion
  72.9 0.0 copy-start
  72.9 0.7 fusion.3
  73.7 0.6 copy-done
  74.3 0.8 fusion.7
  75.1 0.8 fusion.10
  75.9 0.1 constant_dynamic-slice_fusion
  76.0 0.2 convolution_bitcast_fusion
  76.3 0.1 copy.44
  76.5 23.5 %all_to_all.42 = f32[8,14,512]{2,1,0:T(8,128)S(1)} all-to-all(f32[8,14,512]{2,1,0:T(8,128)S(1)} %copy.44), channel_id=1, replica_groups=mesh['zl'=8,'y'=4,'c'=2,'zh'=2,'x'=4] {'zl'}, dimensions={0} | all-to-all | bytes 458752 | tf_op jit(solution)/shard_map/reduce_z/all_to_all | solution.py:16
  100.0 4.3 %all-to-all-start.3 = ((bf16[4,128,256]{2,1,0:T(8,128)(2,1)}), bf16[4,128,256]{2,1,0:T(8,128)(2,1)S(1)}, u32[]{:S(2)}, u32[]{:S(2)}) async-start(bf16[4,128,256]{2,1,0:T(8,128)(2,1)} %bitcast.8), calls=%async_computation.3 | async-start | bytes 524288 | tf_op jit(solution)/shard_map/sum_b_x/all_to_all | solution.py:16
  104.4 0.7 pad_maximum_fusion.4
  105.1 5.9 %all-to-all-done.3 = bf16[4,128,256]{2,1,0:T(8,128)(2,1)S(1)} async-done(((bf16[4,128,256]{2,1,0:T(8,128)(2,1)}), bf16[4,128,256]{2,1,0:T(8,128)(2,1)S(1)}, u32[]{:S(2)}, u32[]{:S(2)}) %all-to-all-start.3) | async-done | bytes 262176 | tf_op jit(solution)/shard_map/sum_b_x/all_to_all | solution.py:16
  111.0 3.4 %all-to-all-start.5 = ((f32[8,7,512]{2,1,0:T(8,128)}), f32[8,7,512]{2,1,0:T(8,128)S(1)}, u32[]{:S(2)}, u32[]{:S(2)}) async-start(f32[8,7,512]{2,1,0:T(8,128)} %pad_maximum_fusion.4), calls=%async_computation.5 | async-start | bytes 262144 | tf_op jit(solution)/shard_map/reduce_yc/all_to_all | solution.py:16
  114.4 6.0 %all-to-all-done.5 = f32[8,7,512]{2,1,0:T(8,128)S(1)} async-done(((f32[8,7,512]{2,1,0:T(8,128)}), f32[8,7,512]{2,1,0:T(8,128)S(1)}, u32[]{:S(2)}, u32[]{:S(2)}) %all-to-all-start.5) | async-done | bytes 114720 | tf_op jit(solution)/shard_map/reduce_yc/all_to_all | solution.py:16
  120.5 0.7 broadcast_in_dim.40
  121.1 7.6 %all-to-all-start.6 = ((bf16[2,132,256]{2,1,0:T(8,128)(2,1)}), bf16[2,132,256]{2,1,0:T(8,128)(2,1)S(1)}, u32[]{:S(2)}, u32[]{:S(2)}) async-start(bf16[2,132,256]{2,1,0:T(8,128)(2,1)} %broadcast_in_dim.40), calls=%async_computation.6 | async-start | bytes 278528 | tf_op jit(solution)/shard_map/sum_b_zh/all_to_all | solution.py:16
  128.8 15.4 %all-to-all-done.6 = bf16[2,132,256]{2,1,0:T(8,128)(2,1)S(1)} async-done(((bf16[2,132,256]{2,1,0:T(8,128)(2,1)}), bf16[2,132,256]{2,1,0:T(8,128)(2,1)S(1)}, u32[]{:S(2)}, u32[]{:S(2)}) %all-to-all-start.6) | async-done | bytes 135200 | tf_op jit(solution)/shard_map/sum_b_zh/all_to_all | solution.py:16
  144.3 0.7 broadcast_in_dim.41
  145.0 3.5 %all-to-all-start.7 = ((bf16[4,136,256]{2,1,0:T(8,128)(2,1)}), bf16[4,136,256]{2,1,0:T(8,128)(2,1)S(1)}, u32[]{:S(2)}, u32[]{:S(2)}) async-start(bf16[4,136,256]{2,1,0:T(8,128)(2,1)} %broadcast_in_dim.41), calls=%async_computation.7 | async-start | bytes 557056 | tf_op jit(solution)/shard_map/gather_b_x/all_to_all | solution.py:16
  148.5 7.3 %all-to-all-done.7 = bf16[4,136,256]{2,1,0:T(8,128)(2,1)S(1)} async-done(((bf16[4,136,256]{2,1,0:T(8,128)(2,1)}), bf16[4,136,256]{2,1,0:T(8,128)(2,1)S(1)}, u32[]{:S(2)}, u32[]{:S(2)}) %all-to-all-start.7) | async-done | bytes 278560 | tf_op jit(solution)/shard_map/gather_b_x/all_to_all | solution.py:16
  155.8 0.0 copy-start.1
  155.8 0.9 copy.47
  156.7 0.4 fusion.28
  157.1 0.0 copy-done.1
  157.1 1.4 fusion.18
  (47 shorter events, 0.7 us)
Async XLA Ops:
  43.3 20.8 %all-to-all-start.1 = ((bf16[4,64,2560]{2,1,0:T(8,128)(2,1)}), bf16[4,64,2560]{2,1,0:T(8,128)(2,1)S(1)}, u32[]{:S(2)}, u32[]{:S(2)}) async-start(bf16[4,64,2560]{2,1,0:T(8,128)(2,1)} %pad_maximum_fusion.1), calls=%async_computation.1 | async-start | bytes 2621440 | tf_op jit(solution)/shard_map/gather_y/all_to_all | solution.py:16
  72.9 1.3 copy-start
  100.0 11.0 %all-to-all-start.3 = ((bf16[4,128,256]{2,1,0:T(8,128)(2,1)}), bf16[4,128,256]{2,1,0:T(8,128)(2,1)S(1)}, u32[]{:S(2)}, u32[]{:S(2)}) async-start(bf16[4,128,256]{2,1,0:T(8,128)(2,1)} %bitcast.8), calls=%async_computation.3 | async-start | bytes 524288 | tf_op jit(solution)/shard_map/sum_b_x/all_to_all | solution.py:16
  111.0 9.4 %all-to-all-start.5 = ((f32[8,7,512]{2,1,0:T(8,128)}), f32[8,7,512]{2,1,0:T(8,128)S(1)}, u32[]{:S(2)}, u32[]{:S(2)}) async-start(f32[8,7,512]{2,1,0:T(8,128)} %pad_maximum_fusion.4), calls=%async_computation.5 | async-start | bytes 262144 | tf_op jit(solution)/shard_map/reduce_yc/all_to_all | solution.py:16
  121.1 23.1 %all-to-all-start.6 = ((bf16[2,132,256]{2,1,0:T(8,128)(2,1)}), bf16[2,132,256]{2,1,0:T(8,128)(2,1)S(1)}, u32[]{:S(2)}, u32[]{:S(2)}) async-start(bf16[2,132,256]{2,1,0:T(8,128)(2,1)} %broadcast_in_dim.40), calls=%async_computation.6 | async-start | bytes 278528 | tf_op jit(solution)/shard_map/sum_b_zh/all_to_all | solution.py:16
  145.0 10.7 %all-to-all-start.7 = ((bf16[4,136,256]{2,1,0:T(8,128)(2,1)}), bf16[4,136,256]{2,1,0:T(8,128)(2,1)S(1)}, u32[]{:S(2)}, u32[]{:S(2)}) async-start(bf16[4,136,256]{2,1,0:T(8,128)(2,1)} %broadcast_in_dim.41), calls=%async_computation.7 | async-start | bytes 557056 | tf_op jit(solution)/shard_map/gather_b_x/all_to_all | solution.py:16
  155.8 1.4 copy-start.1

commit v2 on v1

--- a/solution.py
+++ b/solution.py
@@ -17,9 +17,16 @@
 
 
 def split_halves(values):
-    upper = values.astype(bf16)
-    lower = (values - upper.astype(f32)).astype(bf16)
-    return upper, lower
+    return terms(values, 2)
+
+
+def terms(values, count):
+    parts = []
+    for _ in range(count):
+        rounded = lax.reduce_precision(values, 8, 7)
+        parts.append(rounded.astype(bf16))
+        values = values - rounded
+    return parts
 
 
 def dot(left, right, contract):
@@ -97,63 +104,68 @@
         part_b = (part_b - float_b * jnp.mean(part_b * float_b, 0)) * inverse_b
 
     with jax.named_scope("sum_b_x"):
-        send = part_b.astype(bf16).reshape(nx, images // nx, cols_b)
-        sum_b = jnp.sum(exchange(send, "x").astype(f32), 0)
+        n_rows = images // nx
+        send = part_b.astype(bf16).reshape(nx, n_rows, cols_b)
+        sum_b = jnp.sum(exchange(send, "x").astype(f32), 0).astype(bf16)
 
     with jax.named_scope("gram"):
-        blocks = nc * ny * nz
-        picked = lax.dynamic_index_in_dim(norm_b.reshape(blocks, rows, cols_b), feat, 1, False)
-        gram = dot(picked, norm_b, ((1,), (1,)))
-        pad = jnp.zeros((cols_b,), f32)
-        aux = jnp.concatenate([mean_b, inverse_b, diagonal, pad]).reshape(2, images)
+        take = rows // nx
+        n_yc = ny * nc
+        picked = lax.dynamic_index_in_dim(norm_b.reshape(images // rows, nx, take, cols_b), ix, 1, False)
+        gram = dot(picked.reshape(-1, cols_b), norm_b, ((1,), (1,)))
+        gram = gram.reshape(nc, ny, nz, take, images).transpose(2, 1, 0, 3, 4)
+        gram = gram.reshape(nz, n_yc * take, images).astype(bf16)
+        aux = jnp.concatenate(terms(mean_b, 3) + terms(inverse_b, 3) + terms(diagonal, 2))
+        aux = aux.reshape(-1, images)
         squares = squares.reshape(-1, images)
-        n_sq = squares.shape[0]
+        n_sq, n_aux = squares.shape[0], aux.shape[0]
+        n_gram = n_yc * take
     with jax.named_scope("reduce_z"):
         send = jnp.concatenate(
             [
-                gram.reshape(nc, ny, nz, images).transpose(2, 1, 0, 3).reshape(nz, ny * nc, images),
-                jnp.broadcast_to(squares[None], (nz, n_sq, images)),
-                jnp.broadcast_to(aux[None], (nz, 2, images)),
+                gram,
+                jnp.broadcast_to(squares[None].astype(bf16), (nz, n_sq, images)),
+                jnp.broadcast_to(aux[None], (nz, n_aux, images)),
             ],
             1,
         )
+        send, sum_b = lax.optimization_barrier((send, sum_b))
+        other = lax.ppermute(sum_b, "zh", [(0, 1), (1, 0)])
         got = exchange(send, "zl")
-        total = jnp.sum(got[:, : ny * nc + n_sq], 0)
-        aux = lax.dynamic_index_in_dim(got[:, ny * nc + n_sq :], feat, 0, False)
+        total = jnp.sum(got[:, : n_gram + n_sq].astype(f32), 0)
+        aux = lax.dynamic_index_in_dim(got[:, n_gram + n_sq :], feat, 0, False)
+        aux = aux.astype(f32).reshape(-1, cols_b)
+        aux = jnp.stack([aux[0] + aux[1] + aux[2], aux[3] + aux[4] + aux[5], aux[6] + aux[7], aux[7]])
+        aux = aux.reshape(2, images)
     with jax.named_scope("reduce_yc"):
         send = jnp.concatenate(
             [
-                total[: ny * nc, None],
-                jnp.broadcast_to(total[None, ny * nc :], (ny * nc, n_sq, images)),
-                jnp.broadcast_to(aux[None], (ny * nc, 2, images)),
+                total[:n_gram].reshape(n_yc, take, images),
+                jnp.broadcast_to(total[None, n_gram:], (n_yc, n_sq, images)),
+                jnp.broadcast_to(aux[None], (n_yc, 2, images)),
             ],
             1,
         )
         got = exchange(send, ("y", "c"))
-        total = jnp.sum(got[:, : 1 + n_sq], 0)
-        gram = total[0]
-        squares = total[1:].reshape(cols_a)
-        aux = got[:, 1 + n_sq :].reshape(ny * nc, 4, cols_b).transpose(1, 0, 2).reshape(4, cols_a)
+        total = jnp.sum(got[:, : take + n_sq], 0)
+        gram = total[:take]
+        squares = total[take:].reshape(cols_a)
+        aux = got[:, take + n_sq :].reshape(n_yc, 4, cols_b).transpose(1, 0, 2).reshape(4, cols_a)
         mean_f, inverse_f, diag_f = aux[0], aux[1], aux[2]
 
-    with jax.named_scope("sum_b_zh"):
-        upper, lower = split_halves(gram.reshape(2, cols_b))
-        own = jnp.concatenate([sum_b.astype(bf16), upper, lower], 0)
-        n_rows = images // nx
-        got = exchange(jnp.broadcast_to(own[None], (nh,) + own.shape), "zh")
-        sum_b = jnp.sum(got[:, :n_rows].astype(f32), 0).astype(bf16)
-        gram = got[:, n_rows:].reshape(nh * 4, cols_b)
     with jax.named_scope("gather_b_x"):
-        own = jnp.concatenate([sum_b, gram], 0)
+        sum_b = (sum_b.astype(f32) + other.astype(f32)).astype(bf16)
+        upper, lower = split_halves(gram)
+        own = jnp.concatenate([sum_b, upper.reshape(-1, cols_b), lower.reshape(-1, cols_b)], 0)
         got = exchange(jnp.broadcast_to(own[None], (nx,) + own.shape), "x")
         grad_b = got[:, :n_rows].reshape(nc, ny, nz, rows, cols_b).transpose(2, 1, 0, 3, 4)
         grad_b = grad_b.reshape(images, cols_b).astype(f32)
-        gram = got[:, n_rows:].reshape(nx, nh, 2, images).transpose(2, 1, 0, 3).reshape(2, nh * nx, images)
+        gram = got[:, n_rows:].reshape(nx, 2, take, images).transpose(1, 0, 2, 3).reshape(2 * rows, images)
 
     with jax.named_scope("grad_a"):
         shift = -2.0 * (1.0 - diag_f) - 2.0 * off_weight * diag_f
         projected = 2.0 * off_weight * squares + shift * diag_f
-        both = dot(gram.reshape(2 * nh * nx, images), norm_a, ((1,), (0,)))
+        both = dot(gram, norm_a, ((1,), (0,)))
         scale = 2.0 * off_weight / images
         start_b = view_b_columns(view_b, feat, cols_a)
         own_b = ((start_b - mean_f) * inverse_f).astype(bf16).astype(f32)

time: 159 us -> 138 us (0.87)
  blocking collectives: 68.5 us -> 45 us
  waiting for transfers between devices: 50.9 us -> 39.6 us
  starting transfers between devices: 23.2 us -> 31 us
  other arithmetic: 6.84 us -> 9.56 us
  local copies, waits for them, and re-layouts: 5.15 us -> 7.47 us
    all_to_all x3 -> x2, blocking collectives: 68.5 us -> 45 us  [exchange(): lax.all_to_all(values, axis, split_axis=0, concat_axis=0, tiled=False)]
    all_to_all x5, waiting for transfers between devices: 50.9 us -> 39.6 us  [exchange(): lax.all_to_all(values, axis, split_axis=0, concat_axis=0, tiled=False)]
    ppermute x0 -> x1, starting transfers between devices: none -> 8.21 us  [local(): other = lax.ppermute(sum_b, 'zh', [(0, 1), (1, 0)])]
    unnamed x6 -> x15, local copies, waits for them, and re-layouts: 0.58 us -> 2.69 us
    convert_element_type x1 -> x2, other arithmetic: 0.56 us -> 2.27 us  [standardize(): return (((as_float - mean) * inverse).astype(bf16), mean, inverse)]
  transfers between devices with their start and end apart: 5 -> 6, of which waited for: 5 -> 5; matrix products, arithmetic and copies ran while one was open for 1% -> 2% of each run, Pallas kernels for 0% -> 0%
where the time goes in v2:
time: 138 us; the launch traced here: 137 us
  blocking collectives  45 us (33%)
  waiting for transfers between devices  39.6 us (29%)
  starting transfers between devices  31 us (22%)
  other arithmetic  9.56 us (7%)
  local copies, waits for them, and re-layouts  7.47 us (5%)
  matrix products  3.08 us (2%)
    all_to_all x2, blocking collectives, exchange(): lax.all_to_all(values, axis, split_axis=0, concat_axis=0, tiled=False)  45 us
    all_to_all x5, waiting for transfers between devices, exchange(): lax.all_to_all(values, axis, split_axis=0, concat_axis=0, tiled=False)  39.6 us
    all_to_all x5, starting transfers between devices, exchange(): lax.all_to_all(values, axis, split_axis=0, concat_axis=0, tiled=False)  22.8 us
    ppermute x1, starting transfers between devices, local(): other = lax.ppermute(sum_b, 'zh', [(0, 1), (1, 0)])  8.21 us
    dot_general x5, matrix products, dot(): lax.dot_general(left, right, (contract, ((), ())), preferred_element_type...  3.08 us
  transfers between devices with their start and end apart: 6, of which 5 were waited for; matrix products, arithmetic and copies ran while one was open for 2% of the time, Pallas kernels for 0%

profile of v2, /device:TPU:32, one launch (start us, length us, event | category | flops | bytes accessed | tf_op | source)
XLA Modules:
  0.0 136.7 jit_solution(4629847135637695886)
XLA Ops:
  0.6 0.8 broadcast_in_dim.20
  1.4 1.0 pad_maximum_fusion.2
  2.4 39.3 %all_to_all.35 = bf16[8,8,4096]{2,1,0:T(8,128)(2,1)S(1)} all-to-all(bf16[8,8,4096]{2,1,0:T(8,128)(2,1)S(1)} %pad_maximum_fusion.2), channel_id=1, replica_groups=mesh['zl'=8,'y'=4,'c'=2,'zh'=2,'x'=4] {'zl'}, dimensions={0} | all-to-all | bytes 1048576 | tf_op jit(solution)/shard_map/gather_z/all_to_all | solution.py:16
  41.8 0.2 reshape.155
  42.0 0.1 broadcast_in_dim.21
  42.2 1.2 pad_maximum_fusion.1
  43.3 4.5 %all-to-all-start.1 = ((bf16[4,64,2560]{2,1,0:T(8,128)(2,1)}), bf16[4,64,2560]{2,1,0:T(8,128)(2,1)S(1)}, u32[]{:S(2)}, u32[]{:S(2)}) async-start(bf16[4,64,2560]{2,1,0:T(8,128)(2,1)} %pad_maximum_fusion.1), calls=%async_computation.1 | async-start | bytes 2621440 | tf_op jit(solution)/shard_map/gather_y/all_to_all | solution.py:16
  47.8 16.4 %all-to-all-done.1 = bf16[4,64,2560]{2,1,0:T(8,128)(2,1)S(1)} async-done(((bf16[4,64,2560]{2,1,0:T(8,128)(2,1)}), bf16[4,64,2560]{2,1,0:T(8,128)(2,1)S(1)}, u32[]{:S(2)}, u32[]{:S(2)}) %all-to-all-start.1) | async-done | bytes 1310752 | tf_op jit(solution)/shard_map/gather_y/all_to_all | solution.py:16
  64.2 0.1 slice.122
  64.3 0.1 copy.40
  64.5 0.1 copy.41
  64.6 0.2 broadcast_in_dim.22
  64.8 0.2 pad_maximum_fusion
  65.0 5.6 %all_to_all.36 = bf16[2,256,2304]{2,1,0:T(8,128)(2,1)S(1)} all-to-all(bf16[2,256,2304]{2,1,0:T(8,128)(2,1)S(1)} %pad_maximum_fusion), channel_id=1, replica_groups=mesh['zl'=8,'y'=4,'c'=2,'zh'=2,'x'=4] {'c'}, dimensions={0} | all-to-all | bytes 4718592 | tf_op jit(solution)/shard_map/gather_core/all_to_all | solution.py:16
  70.7 0.1 convert_reduce_fusion.1
  70.8 0.6 convert_reduce_fusion
  71.4 0.7 copy-done
  72.1 0.1 reshape.159
  72.3 2.2 %fusion.1 = bf16[512,2048]{1,0:T(8,128)(2,1)S(1)} fusion(f32[2048]{0:T(1024)S(1)} %get-tuple-element.29, f32[2048]{0:T(1024)S(1)} %get-tuple-element.28, bf16[512,2304]{1,0:T(8,128)(2,1)} %bitcast.44), kind=kLoop, calls=%fused_computation.4 | loop fusion | flops 4194304 | bytes 4210688 | tf_op jit(solution)/shard_map/tile/convert_element_type | solution.py:41
  74.5 0.9 multiply_reduce_fusion
  75.4 0.7 fusion.8
  76.2 0.6 copy-done.1
  76.8 0.8 fusion.11
  77.6 1.8 %fusion.14 = bf16[512,256]{1,0:T(8,128)(2,1)} fusion(f32[512,256]{1,0:T(8,128)S(1)} %get-tuple-element.41, f32[256]{0:T(256)S(1)} %broadcast_multiply_fusion.2, f32[256]{0:T(256)S(1)} %get-tuple-element.14, f32[256]{0:T(256)S(1)} %get-tuple-element.38, bf16[512,2304]{1,0:T(8,128)(2,1)} %bitcast.45), kind=kLoop, calls=%fused_computation.29 | loop fusion | flops 1179648 | bytes 1051648 | tf_op jit(solution)/shard_map/sum_b_x/convert_element_type | solution.py:108
  79.4 4.3 %all-to-all-start.3 = ((bf16[4,128,256]{2,1,0:T(8,128)(2,1)}), bf16[4,128,256]{2,1,0:T(8,128)(2,1)S(1)}, u32[]{:S(2)}, u32[]{:S(2)}) async-start(bf16[4,128,256]{2,1,0:T(8,128)(2,1)} %bitcast.13), calls=%async_computation.3 | async-start | bytes 524288 | tf_op jit(solution)/shard_map/sum_b_x/all_to_all | solution.py:16
  83.7 0.2 fusion.6
  84.0 0.2 dynamic-update-slice
  84.2 0.2 dynamic-update-slice.1
  84.4 0.2 dynamic-update-slice.2
  84.6 0.2 dynamic-update-slice.3
  84.9 0.2 dynamic-update-slice.4
  85.0 0.2 dynamic-update-slice.5
  85.2 0.2 dynamic-update-slice.6
  85.4 0.2 dynamic-update-slice.7
  85.7 4.9 %all-to-all-done.3 = bf16[4,128,256]{2,1,0:T(8,128)(2,1)S(1)} async-done(((bf16[4,128,256]{2,1,0:T(8,128)(2,1)}), bf16[4,128,256]{2,1,0:T(8,128)(2,1)S(1)}, u32[]{:S(2)}, u32[]{:S(2)}) %all-to-all-start.3) | async-done | bytes 262176 | tf_op jit(solution)/shard_map/sum_b_x/all_to_all | solution.py:16
  90.7 0.7 copy.45
  91.4 7.2 %all-to-all-start.4 = ((bf16[8,24,512]{2,1,0:T(8,128)(2,1)}), bf16[8,24,512]{2,1,0:T(8,128)(2,1)S(1)}, u32[]{:S(2)}, u32[]{:S(2)}) async-start(bf16[8,24,512]{2,1,0:T(8,128)(2,1)} %copy.45), calls=%async_computation.4 | async-start | bytes 393216 | tf_op jit(solution)/shard_map/reduce_z/all_to_all | solution.py:16
  98.6 8.2 %collective-permute-start = (bf16[128,256]{1,0:T(8,128)(2,1)S(1)}, bf16[128,256]{1,0:T(8,128)(2,1)S(1)}, u32[]{:S(2)}, u32[]{:S(2)}) collective-permute-start(bf16[128,256]{1,0:T(8,128)(2,1)S(1)} %reduce_sum.100), channel_id=1, source_target_pairs={{0,4},{4,0},{1,5},{5,1},{2,6},{6,2},{3,7},{7,3},{8,12},{12,8},{9,1... | collective-permute-start | bytes 196616 | tf_op jit(solution)/shard_map/reduce_z/ppermute | solution.py:133
  106.8 5.5 %all-to-all-done.4 = bf16[8,24,512]{2,1,0:T(8,128)(2,1)S(1)} async-done(((bf16[8,24,512]{2,1,0:T(8,128)(2,1)}), bf16[8,24,512]{2,1,0:T(8,128)(2,1)S(1)}, u32[]{:S(2)}, u32[]{:S(2)}) %all-to-all-start.4) | async-done | bytes 196640 | tf_op jit(solution)/shard_map/reduce_z/all_to_all | solution.py:16
  112.6 0.7 pad_maximum_fusion.4
  113.3 3.4 %all-to-all-start.5 = ((f32[8,8,512]{2,1,0:T(8,128)}), f32[8,8,512]{2,1,0:T(8,128)S(1)}, u32[]{:S(2)}, u32[]{:S(2)}) async-start(f32[8,8,512]{2,1,0:T(8,128)} %pad_maximum_fusion.4), calls=%async_computation.5 | async-start | bytes 262144 | tf_op jit(solution)/shard_map/reduce_yc/all_to_all | solution.py:16
  116.7 6.0 %all-to-all-done.5 = f32[8,8,512]{2,1,0:T(8,128)S(1)} async-done(((f32[8,8,512]{2,1,0:T(8,128)}), f32[8,8,512]{2,1,0:T(8,128)S(1)}, u32[]{:S(2)}, u32[]{:S(2)}) %all-to-all-start.5) | async-done | bytes 131104 | tf_op jit(solution)/shard_map/reduce_yc/all_to_all | solution.py:16
  122.8 0.7 broadcast_in_dim.29
  123.5 3.5 %all-to-all-start.6 = ((bf16[4,136,256]{2,1,0:T(8,128)(2,1)}), bf16[4,136,256]{2,1,0:T(8,128)(2,1)S(1)}, u32[]{:S(2)}, u32[]{:S(2)}) async-start(bf16[4,136,256]{2,1,0:T(8,128)(2,1)} %broadcast_in_dim.29), calls=%async_computation.6 | async-start | bytes 557056 | tf_op jit(solution)/shard_map/gather_b_x/all_to_all | solution.py:16
  127.1 6.8 %all-to-all-done.6 = bf16[4,136,256]{2,1,0:T(8,128)(2,1)S(1)} async-done(((bf16[4,136,256]{2,1,0:T(8,128)(2,1)}), bf16[4,136,256]{2,1,0:T(8,128)(2,1)S(1)}, u32[]{:S(2)}, u32[]{:S(2)}) %all-to-all-start.6) | async-done | bytes 278560 | tf_op jit(solution)/shard_map/gather_b_x/all_to_all | solution.py:16
  134.0 0.9 copy.48
  134.9 0.4 fusion.37
  135.3 1.4 %fusion.22 = f32[8,2048]{1,0:T(8,128)} fusion(f32[16,2048]{1,0:T(8,128)S(1)} %fusion.37, bf16[8,2048]{1,0:T(8,128)(2,1)S(1)} %copy-done.2, f32[2048]{0:T(1024)S(1)} %get-tuple-element.23, f32[2048]{0:T(1024)S(1)} %get-tuple-element.29, f32[2048]{0:T(1024)S(1)} %get-tuple-element.28, f32[2048]{0:T(1024)S(1)} %get-tuple-element.22, f32[2048]{0:T(1024)S(1)} %bitcast.59, ...), kind=kLoop, calls=%fused_computation.48 | loop fusion | flops 278528 | bytes 311300 | tf_op jit(solution)/shard_map/grad_a/mul | solution.py:174
  (55 shorter events, 0.9 us)
Async XLA Ops:
  43.3 20.8 %all-to-all-start.1 = ((bf16[4,64,2560]{2,1,0:T(8,128)(2,1)}), bf16[4,64,2560]{2,1,0:T(8,128)(2,1)S(1)}, u32[]{:S(2)}, u32[]{:S(2)}) async-start(bf16[4,64,2560]{2,1,0:T(8,128)(2,1)} %pad_maximum_fusion.1), calls=%async_computation.1 | async-start | bytes 2621440 | tf_op jit(solution)/shard_map/gather_y/all_to_all | solution.py:16
  70.7 1.4 %copy-start = (bf16[2,256,2304]{2,1,0:T(8,128)(2,1)}, bf16[2,256,2304]{2,1,0:T(8,128)(2,1)S(1)}, u32[]{:S(2)}) copy-start(bf16[2,256,2304]{2,1,0:T(8,128)(2,1)S(1)} %all_to_all.36) | copy-start | bytes 7077892
  75.4 1.3 copy-start.1
  79.4 11.3 %all-to-all-start.3 = ((bf16[4,128,256]{2,1,0:T(8,128)(2,1)}), bf16[4,128,256]{2,1,0:T(8,128)(2,1)S(1)}, u32[]{:S(2)}, u32[]{:S(2)}) async-start(bf16[4,128,256]{2,1,0:T(8,128)(2,1)} %bitcast.13), calls=%async_computation.3 | async-start | bytes 524288 | tf_op jit(solution)/shard_map/sum_b_x/all_to_all | solution.py:16
  91.4 20.9 %all-to-all-start.4 = ((bf16[8,24,512]{2,1,0:T(8,128)(2,1)}), bf16[8,24,512]{2,1,0:T(8,128)(2,1)S(1)}, u32[]{:S(2)}, u32[]{:S(2)}) async-start(bf16[8,24,512]{2,1,0:T(8,128)(2,1)} %copy.45), calls=%async_computation.4 | async-start | bytes 393216 | tf_op jit(solution)/shard_map/reduce_z/all_to_all | solution.py:16
  98.6 18.1 %collective-permute-start = (bf16[128,256]{1,0:T(8,128)(2,1)S(1)}, bf16[128,256]{1,0:T(8,128)(2,1)S(1)}, u32[]{:S(2)}, u32[]{:S(2)}) collective-permute-start(bf16[128,256]{1,0:T(8,128)(2,1)S(1)} %reduce_sum.100), channel_id=1, source_target_pairs={{0,4},{4,0},{1,5},{5,1},{2,6},{6,2},{3,7},{7,3},{8,12},{12,8},{9,1... | collective-permute-start | bytes 196616 | tf_op jit(solution)/shard_map/reduce_z/ppermute | solution.py:133
  113.3 9.4 %all-to-all-start.5 = ((f32[8,8,512]{2,1,0:T(8,128)}), f32[8,8,512]{2,1,0:T(8,128)S(1)}, u32[]{:S(2)}, u32[]{:S(2)}) async-start(f32[8,8,512]{2,1,0:T(8,128)} %pad_maximum_fusion.4), calls=%async_computation.5 | async-start | bytes 262144 | tf_op jit(solution)/shard_map/reduce_yc/all_to_all | solution.py:16
  123.5 10.4 %all-to-all-start.6 = ((bf16[4,136,256]{2,1,0:T(8,128)(2,1)}), bf16[4,136,256]{2,1,0:T(8,128)(2,1)S(1)}, u32[]{:S(2)}, u32[]{:S(2)}) async-start(bf16[4,136,256]{2,1,0:T(8,128)(2,1)} %broadcast_in_dim.29), calls=%async_computation.6 | async-start | bytes 557056 | tf_op jit(solution)/shard_map/gather_b_x/all_to_all | solution.py:16
  133.9 1.4 copy-start.2

commit v3 on v2

--- a/solution.py
+++ b/solution.py
@@ -53,39 +53,33 @@
     feat = ih * nx + ix
 
     with jax.named_scope("gather_z"):
-        part = width // nz
+        lanes = cols_b // (nx // nc)
+        quarter = view_b.reshape(rows, nz * ny, nx, lanes)
+        quarter = lax.dynamic_index_in_dim(quarter, ix, 2, False).reshape(rows, nz, ny * lanes)
+        send = jnp.concatenate(
+            [jnp.broadcast_to(view_a[None], (nz, rows, cols_a)), quarter.transpose(1, 0, 2)], 2
+        )
+        got = exchange(send, "zl").reshape(nz * rows, cols_a + ny * lanes)
+    with jax.named_scope("gather_y"):
         send = jnp.concatenate(
             [
-                jnp.broadcast_to(view_a[None], (nz, rows, cols_a)),
-                view_b.reshape(rows, nz, part).transpose(1, 0, 2),
+                jnp.broadcast_to(got[None, :, :cols_a], (ny, nz * rows, cols_a)),
+                got[:, cols_a:].reshape(nz * rows, ny, lanes).transpose(1, 0, 2),
             ],
             2,
         )
-        got = exchange(send, "zl").reshape(nz * rows, cols_a + part)
-    with jax.named_scope("gather_y"):
-        part = part // ny
-        send = jnp.concatenate(
-            [
-                jnp.broadcast_to(got[None, :, :cols_a], (ny, nz * rows, cols_a)),
-                got[:, cols_a:].reshape(nz * rows, ny, part).transpose(1, 0, 2),
-            ],
-            2,
-        )
-        got = exchange(send, "y").reshape(ny * nz * rows, cols_a + part)
+        got = exchange(send, "y").reshape(ny * nz * rows, cols_a + lanes)
     with jax.named_scope("gather_core"):
-        part = part // nc
-        send = jnp.concatenate(
-            [
-                jnp.broadcast_to(got[None, :, :cols_a], (nc, images // nc, cols_a)),
-                got[:, cols_a:].reshape(images // nc, nc, part).transpose(1, 0, 2),
-            ],
-            2,
-        )
-        got = exchange(send, "c").reshape(images, cols_a + part)
+        got = exchange(jnp.broadcast_to(got[None], (nc,) + got.shape), "c")
+        got = got.reshape(images, cols_a + lanes)
+    with jax.named_scope("gather_b_x_raw"):
+        part = exchange(jnp.broadcast_to(got[None, :, cols_a:], (nx, images, lanes)), "x")
+        part = lax.dynamic_index_in_dim(part.reshape(nc, nx // nc, images, lanes), ic, 0, False)
+        raw_b = jnp.concatenate([part[k] for k in range(nx // nc)], 1)
 
     with jax.named_scope("tile"):
         norm_a, mean_a, inverse_a = standardize(got[:, :cols_a])
-        norm_b, mean_b, inverse_b = standardize(got[:, cols_a:])
+        norm_b, mean_b, inverse_b = standardize(raw_b)
         correlation = dot(norm_a, norm_b, ((0,), (0,))) / images
         on_block = (feat == iz).astype(f32)
         first = (iy * nc + ic) * cols_b
@@ -153,25 +147,25 @@
         aux = got[:, take + n_sq :].reshape(n_yc, 4, cols_b).transpose(1, 0, 2).reshape(4, cols_a)
         mean_f, inverse_f, diag_f = aux[0], aux[1], aux[2]
 
+    with jax.named_scope("shift_a"):
+        shift = -2.0 * (1.0 - diag_f) - 2.0 * off_weight * diag_f
+        projected = 2.0 * off_weight * squares + shift * diag_f
+        own_b = ((view_b_columns(view_b, feat, cols_a) - mean_f) * inverse_f).astype(bf16).astype(f32)
+        own_a = ((view_a.astype(f32) - mean_a) * inverse_a).astype(bf16).astype(f32)
+        shifted = (own_b * shift - own_a * projected) * inverse_a
+        scale = jnp.broadcast_to(2.0 * off_weight / images * inverse_a, (rows, cols_a))
     with jax.named_scope("gather_b_x"):
         sum_b = (sum_b.astype(f32) + other.astype(f32)).astype(bf16)
-        upper, lower = split_halves(gram)
+        upper, lower = terms(gram, 2)
         own = jnp.concatenate([sum_b, upper.reshape(-1, cols_b), lower.reshape(-1, cols_b)], 0)
+        own, shifted, scale = lax.optimization_barrier((own, shifted, scale))
         got = exchange(jnp.broadcast_to(own[None], (nx,) + own.shape), "x")
         grad_b = got[:, :n_rows].reshape(nc, ny, nz, rows, cols_b).transpose(2, 1, 0, 3, 4)
         grad_b = grad_b.reshape(images, cols_b).astype(f32)
         gram = got[:, n_rows:].reshape(nx, 2, take, images).transpose(1, 0, 2, 3).reshape(2 * rows, images)
-
     with jax.named_scope("grad_a"):
-        shift = -2.0 * (1.0 - diag_f) - 2.0 * off_weight * diag_f
-        projected = 2.0 * off_weight * squares + shift * diag_f
         both = dot(gram, norm_a, ((1,), (0,)))
-        scale = 2.0 * off_weight / images
-        start_b = view_b_columns(view_b, feat, cols_a)
-        own_b = ((start_b - mean_f) * inverse_f).astype(bf16).astype(f32)
-        own_a = ((view_a.astype(f32) - mean_a) * inverse_a).astype(bf16).astype(f32)
-        grad_a_n = (both[:rows] + both[rows:]) * scale + own_b * shift
-        grad_a = (grad_a_n - own_a * projected) * inverse_a
+        grad_a = (both[:rows] + both[rows:]) * scale + shifted
     return correlation, grad_a, grad_b
 
 

time: 138 us -> 136 us (0.986)
  other arithmetic: 9.56 us -> 7.42 us
  blocking collectives: 45 us -> 46.4 us
    all_to_all x2 -> x3, blocking collectives: 45 us -> 46.4 us  [exchange(): lax.all_to_all(values, axis, split_axis=0, concat_axis=0, tiled=False)]
    unnamed x15 -> x14, local copies, waits for them, and re-layouts: 2.69 us -> 3.4 us
  transfers between devices with their start and end apart: 6 -> 6, of which waited for: 5 -> 5; matrix products, arithmetic and copies ran while one was open for 2% -> 4% of each run, Pallas kernels for 0% -> 0%
where the time goes in v3:
time: 136 us; the launch traced here: 135 us
  blocking collectives  46.4 us (34%)
  waiting for transfers between devices  38.4 us (28%)
  starting transfers between devices  30.7 us (23%)
  local copies, waits for them, and re-layouts  8.38 us (6%)
  other arithmetic  7.42 us (5%)
  matrix products  3.1 us (2%)
    all_to_all x3, blocking collectives, exchange(): lax.all_to_all(values, axis, split_axis=0, concat_axis=0, tiled=False)  46.4 us
    all_to_all x5, waiting for transfers between devices, exchange(): lax.all_to_all(values, axis, split_axis=0, concat_axis=0, tiled=False)  38.4 us
    all_to_all x5, starting transfers between devices, exchange(): lax.all_to_all(values, axis, split_axis=0, concat_axis=0, tiled=False)  22.5 us
    ppermute x1, starting transfers between devices, local(): other = lax.ppermute(sum_b, 'zh', [(0, 1), (1, 0)])  8.21 us
    unnamed x14, local copies, waits for them, and re-layouts  3.4 us
    dot_general x5, matrix products, dot(): lax.dot_general(left, right, (contract, ((), ())), preferred_element_type...  3.1 us
  transfers between devices with their start and end apart: 6, of which 5 were waited for; matrix products, arithmetic and copies ran while one was open for 4% of the time, Pallas kernels for 0%

profile of v3, /device:TPU:32, one launch (start us, length us, event | category | flops | bytes accessed | tf_op | source)
XLA Modules:
  0.0 135.4 jit_solution(4253487780287438400)
XLA Ops:
  0.6 0.8 constant_dynamic-slice_fusion.2
  1.5 0.8 broadcast_in_dim.26
  2.3 31.3 %all_to_all.40 = bf16[8,8,2560]{2,1,0:T(8,128)(2,1)S(1)} all-to-all(bf16[8,8,2560]{2,1,0:T(8,128)(2,1)S(1)} %pad_maximum_fusion.1), channel_id=1, replica_groups=mesh['zl'=8,'y'=4,'c'=2,'zh'=2,'x'=4] {'zl'}, dimensions={0} | all-to-all | bytes 655360 | tf_op jit(solution)/shard_map/gather_z/all_to_all | solution.py:16
  33.7 0.1 broadcast_in_dim.27
  33.8 1.1 pad_maximum_fusion
  34.9 4.5 %all-to-all-start.1 = ((bf16[4,64,2176]{2,1,0:T(8,128)(2,1)}), bf16[4,64,2176]{2,1,0:T(8,128)(2,1)S(1)}, u32[]{:S(2)}, u32[]{:S(2)}) async-start(bf16[4,64,2176]{2,1,0:T(8,128)(2,1)} %pad_maximum_fusion), calls=%async_computation.1 | async-start | bytes 2228224 | tf_op jit(solution)/shard_map/gather_y/all_to_all | solution.py:16
  39.4 14.4 %all-to-all-done.1 = bf16[4,64,2176]{2,1,0:T(8,128)(2,1)S(1)} async-done(((bf16[4,64,2176]{2,1,0:T(8,128)(2,1)}), bf16[4,64,2176]{2,1,0:T(8,128)(2,1)S(1)}, u32[]{:S(2)}, u32[]{:S(2)}) %all-to-all-start.1) | async-done | bytes 1114144 | tf_op jit(solution)/shard_map/gather_y/all_to_all | solution.py:16
  53.8 0.2 broadcast_in_dim.29
  53.9 5.5 %all_to_all.41 = bf16[2,256,2176]{2,1,0:T(8,128)(2,1)S(1)} all-to-all(bf16[2,256,2176]{2,1,0:T(8,128)(2,1)S(1)} %broadcast_in_dim.29), channel_id=1, replica_groups=mesh['zl'=8,'y'=4,'c'=2,'zh'=2,'x'=4] {'c'}, dimensions={0} | all-to-all | bytes 4456448 | tf_op jit(solution)/shard_map/gather_core/all_to_all | solution.py:16
  59.5 1.4 %copy-done = bf16[2,256,2176]{2,1,0:T(8,128)(2,1)} copy-done((bf16[2,256,2176]{2,1,0:T(8,128)(2,1)}, bf16[2,256,2176]{2,1,0:T(8,128)(2,1)S(1)}, u32[]{:S(2)}) %copy-start) | copy-done | bytes 2228248
  60.8 0.6 convert_reduce_fusion
  61.5 0.9 broadcast_in_dim.30
  62.3 4.3 %all-to-all-start.3 = ((bf16[4,512,128]{2,1,0:T(8,128)(2,1)}), bf16[4,512,128]{2,1,0:T(8,128)(2,1)S(1)}, u32[]{:S(2)}, u32[]{:S(2)}) async-start(bf16[4,512,128]{2,1,0:T(8,128)(2,1)} %broadcast_in_dim.30), calls=%async_computation.3 | async-start | bytes 1048576 | tf_op jit(solution)/shard_map/gather_b_x_raw/all_to_all | solution.py:16
  66.6 2.2 %fusion.1 = bf16[512,2048]{1,0:T(8,128)(2,1)S(1)} fusion(f32[2048]{0:T(1024)S(1)} %get-tuple-element.27, f32[2048]{0:T(1024)S(1)} %get-tuple-element.30, bf16[512,2176]{1,0:T(8,128)(2,1)} %bitcast.45), kind=kLoop, calls=%fused_computation.4 | loop fusion | flops 4194304 | bytes 4210688 | tf_op jit(solution)/shard_map/tile/convert_element_type | solution.py:41
  68.9 7.5 %all-to-all-done.3 = bf16[4,512,128]{2,1,0:T(8,128)(2,1)S(1)} async-done(((bf16[4,512,128]{2,1,0:T(8,128)(2,1)}), bf16[4,512,128]{2,1,0:T(8,128)(2,1)S(1)}, u32[]{:S(2)}, u32[]{:S(2)}) %all-to-all-start.3) | async-done | bytes 524320 | tf_op jit(solution)/shard_map/gather_b_x_raw/all_to_all | solution.py:16
  76.4 0.1 convert_reduce_fusion.1
  76.6 0.9 multiply_reduce_fusion
  77.5 0.0 copy-start.1
  77.5 0.7 fusion.8
  78.2 0.6 copy-done.1
  78.9 0.8 fusion.11
  79.7 0.8 fusion.14
  80.5 3.4 %all-to-all-start.4 = ((bf16[4,128,256]{2,1,0:T(8,128)(2,1)}), bf16[4,128,256]{2,1,0:T(8,128)(2,1)S(1)}, u32[]{:S(2)}, u32[]{:S(2)}) async-start(bf16[4,128,256]{2,1,0:T(8,128)(2,1)} %bitcast.17), calls=%async_computation.4 | async-start | bytes 524288 | tf_op jit(solution)/shard_map/sum_b_x/all_to_all | solution.py:16
  84.0 0.2 fusion.6
  84.3 0.0 copy-start.2
  84.3 0.2 dynamic-update-slice
  84.6 0.2 dynamic-update-slice.1
  84.8 0.2 dynamic-update-slice.2
  85.0 0.2 dynamic-update-slice.3
  85.2 0.2 dynamic-update-slice.4
  85.4 0.2 dynamic-update-slice.5
  85.6 0.2 dynamic-update-slice.6
  85.8 0.2 dynamic-update-slice.7
  86.0 4.5 %all-to-all-done.4 = bf16[4,128,256]{2,1,0:T(8,128)(2,1)S(1)} async-done(((bf16[4,128,256]{2,1,0:T(8,128)(2,1)}), bf16[4,128,256]{2,1,0:T(8,128)(2,1)S(1)}, u32[]{:S(2)}, u32[]{:S(2)}) %all-to-all-start.4) | async-done | bytes 262176 | tf_op jit(solution)/shard_map/sum_b_x/all_to_all | solution.py:16
  90.6 0.7 copy.39
  91.4 6.9 %all-to-all-start.5 = ((bf16[8,24,512]{2,1,0:T(8,128)(2,1)}), bf16[8,24,512]{2,1,0:T(8,128)(2,1)S(1)}, u32[]{:S(2)}, u32[]{:S(2)}) async-start(bf16[8,24,512]{2,1,0:T(8,128)(2,1)} %copy.39), calls=%async_computation.5 | async-start | bytes 393216 | tf_op jit(solution)/shard_map/reduce_z/all_to_all | solution.py:16
  98.3 8.2 %collective-permute-start = (bf16[128,256]{1,0:T(8,128)(2,1)S(1)}, bf16[128,256]{1,0:T(8,128)(2,1)S(1)}, u32[]{:S(2)}, u32[]{:S(2)}) collective-permute-start(bf16[128,256]{1,0:T(8,128)(2,1)S(1)} %reduce_sum.100), channel_id=1, source_target_pairs={{0,4},{4,0},{1,5},{5,1},{2,6},{6,2},{3,7},{7,3},{8,12},{12,8},{9,1... | collective-permute-start | bytes 196616 | tf_op jit(solution)/shard_map/reduce_z/ppermute | solution.py:127
  106.5 5.9 %all-to-all-done.5 = bf16[8,24,512]{2,1,0:T(8,128)(2,1)S(1)} async-done(((bf16[8,24,512]{2,1,0:T(8,128)(2,1)}), bf16[8,24,512]{2,1,0:T(8,128)(2,1)S(1)}, u32[]{:S(2)}, u32[]{:S(2)}) %all-to-all-start.5) | async-done | bytes 196640 | tf_op jit(solution)/shard_map/reduce_z/all_to_all | solution.py:16
  112.7 0.7 pad_maximum_fusion.4
  113.4 3.4 %all-to-all-start.6 = ((f32[8,8,512]{2,1,0:T(8,128)}), f32[8,8,512]{2,1,0:T(8,128)S(1)}, u32[]{:S(2)}, u32[]{:S(2)}) async-start(f32[8,8,512]{2,1,0:T(8,128)} %pad_maximum_fusion.4), calls=%async_computation.6 | async-start | bytes 262144 | tf_op jit(solution)/shard_map/reduce_yc/all_to_all | solution.py:16
  116.7 0.0 collective-permute-done
  116.8 6.0 %all-to-all-done.6 = f32[8,8,512]{2,1,0:T(8,128)S(1)} async-done(((f32[8,8,512]{2,1,0:T(8,128)}), f32[8,8,512]{2,1,0:T(8,128)S(1)}, u32[]{:S(2)}, u32[]{:S(2)}) %all-to-all-start.6) | async-done | bytes 131104 | tf_op jit(solution)/shard_map/reduce_yc/all_to_all | solution.py:16
  123.0 0.0 copy-done.2
  123.0 0.8 subtract_multiply_fusion
  123.8 9.6 %all_to_all.42 = bf16[4,136,256]{2,1,0:T(8,128)(2,1)S(1)} all-to-all(bf16[4,136,256]{2,1,0:T(8,128)(2,1)S(1)} %broadcast_in_dim.38), channel_id=1, replica_groups=mesh['zl'=8,'y'=4,'c'=2,'zh'=2,'x'=4] {'x'}, dimensions={0} | all-to-all | bytes 557056 | tf_op jit(solution)/shard_map/gather_b_x/all_to_all | solution.py:16
  133.5 0.9 copy.42
  134.4 0.4 fusion.39
  134.8 0.7 fusion.21
  (57 shorter events, 0.8 us)
Async XLA Ops:
  34.9 18.8 %all-to-all-start.1 = ((bf16[4,64,2176]{2,1,0:T(8,128)(2,1)}), bf16[4,64,2176]{2,1,0:T(8,128)(2,1)S(1)}, u32[]{:S(2)}, u32[]{:S(2)}) async-start(bf16[4,64,2176]{2,1,0:T(8,128)(2,1)} %pad_maximum_fusion), calls=%async_computation.1 | async-start | bytes 2228224 | tf_op jit(solution)/shard_map/gather_y/all_to_all | solution.py:16
  59.5 1.4 %copy-start = (bf16[2,256,2176]{2,1,0:T(8,128)(2,1)}, bf16[2,256,2176]{2,1,0:T(8,128)(2,1)S(1)}, u32[]{:S(2)}) copy-start(bf16[2,256,2176]{2,1,0:T(8,128)(2,1)S(1)} %all_to_all.41) | copy-start | bytes 6684676
  62.3 14.1 %all-to-all-start.3 = ((bf16[4,512,128]{2,1,0:T(8,128)(2,1)}), bf16[4,512,128]{2,1,0:T(8,128)(2,1)S(1)}, u32[]{:S(2)}, u32[]{:S(2)}) async-start(bf16[4,512,128]{2,1,0:T(8,128)(2,1)} %broadcast_in_dim.30), calls=%async_computation.3 | async-start | bytes 1048576 | tf_op jit(solution)/shard_map/gather_b_x_raw/all_to_all | solution.py:16
  77.5 1.3 copy-start.1
  80.5 10.1 %all-to-all-start.4 = ((bf16[4,128,256]{2,1,0:T(8,128)(2,1)}), bf16[4,128,256]{2,1,0:T(8,128)(2,1)S(1)}, u32[]{:S(2)}, u32[]{:S(2)}) async-start(bf16[4,128,256]{2,1,0:T(8,128)(2,1)} %bitcast.17), calls=%async_computation.4 | async-start | bytes 524288 | tf_op jit(solution)/shard_map/sum_b_x/all_to_all | solution.py:16
  84.3 38.7 %copy-start.2 = (bf16[8,2048]{1,0:T(8,128)(2,1)S(1)}, bf16[8,2048]{1,0:T(8,128)(2,1)}, u32[]{:S(2)}) copy-start(bf16[8,2048]{1,0:T(8,128)(2,1)} %param.2) | copy-start | bytes 98308
  91.4 21.0 %all-to-all-start.5 = ((bf16[8,24,512]{2,1,0:T(8,128)(2,1)}), bf16[8,24,512]{2,1,0:T(8,128)(2,1)S(1)}, u32[]{:S(2)}, u32[]{:S(2)}) async-start(bf16[8,24,512]{2,1,0:T(8,128)(2,1)} %copy.39), calls=%async_computation.5 | async-start | bytes 393216 | tf_op jit(solution)/shard_map/reduce_z/all_to_all | solution.py:16
  98.3 18.4 %collective-permute-start = (bf16[128,256]{1,0:T(8,128)(2,1)S(1)}, bf16[128,256]{1,0:T(8,128)(2,1)S(1)}, u32[]{:S(2)}, u32[]{:S(2)}) collective-permute-start(bf16[128,256]{1,0:T(8,128)(2,1)S(1)} %reduce_sum.100), channel_id=1, source_target_pairs={{0,4},{4,0},{1,5},{5,1},{2,6},{6,2},{3,7},{7,3},{8,12},{12,8},{9,1... | collective-permute-start | bytes 196616 | tf_op jit(solution)/shard_map/reduce_z/ppermute | solution.py:127
  113.4 9.4 %all-to-all-start.6 = ((f32[8,8,512]{2,1,0:T(8,128)}), f32[8,8,512]{2,1,0:T(8,128)S(1)}, u32[]{:S(2)}, u32[]{:S(2)}) async-start(f32[8,8,512]{2,1,0:T(8,128)} %pad_maximum_fusion.4), calls=%async_computation.6 | async-start | bytes 262144 | tf_op jit(solution)/shard_map/reduce_yc/all_to_all | solution.py:16

commit v4 on v3

v4 whole, which is shorter than its diff:
```python
import functools
import jax
import jax.numpy as jnp
from jax import lax
from jax.experimental import pallas as pl
from jax.experimental.pallas import tpu as pltpu
from jax.sharding import Mesh, PartitionSpec as P

epsilon = 1e-05
off_weight = 0.005
f32 = jnp.float32
bf16 = jnp.bfloat16
AXES = ("zl", "y", "c", "zh", "x")
DP = ("zl", "y", "c")
FEAT = ("zh", "x")
SWAP = [(0, 1), (1, 0)]
VMEM_LIMIT = 40 * 1024 * 1024


def exchange(values, axis):
    return lax.all_to_all(values, axis, split_axis=0, concat_axis=0, tiled=False)


def terms(values, count):
    parts = []
    for _ in range(count):
        rounded = lax.reduce_precision(values, 8, 7)
        parts.append(rounded.astype(bf16))
        values = values - rounded
    return parts


def kernel_terms(values, count):
    parts = []
    for _ in range(count):
        parts.append(values.astype(bf16).astype(f32))
        values = values - parts[-1]
    return parts


def dot(left, right, contract):
    return lax.dot_general(left, right, (contract, ((), ())), preferred_element_type=f32)


def statistics(total, square, images):
    mean = total / images
    return mean, lax.rsqrt(square / images - mean * mean + epsilon)


def standardize_kernel(idx, own_ref, other_ref, norm_ref, stat_ref):
    half = own_ref.shape[0]
    cols = norm_ref.shape[1]
    own_place = pl.multiple_of(idx[0] * half, half)
    other_place = pl.multiple_of((1 - idx[0]) * half, half)
    block = 256
    for j in range(cols // block):
        span = slice(j * block, (j + 1) * block)
        own = own_ref[:, span].astype(f32)
        other = other_ref[:, span].astype(f32)
        total = jnp.sum(own, 0, keepdims=True) + jnp.sum(other, 0, keepdims=True)
        square = jnp.sum(own * own, 0, keepdims=True) + jnp.sum(other * other, 0, keepdims=True)
        mean, inverse = statistics(total, square, 2 * half)
        norm_ref[pl.ds(own_place, half), span] = ((own - mean) * inverse).astype(bf16)
        norm_ref[pl.ds(other_place, half), span] = ((other - mean) * inverse).astype(bf16)
        stat_ref[0:1, span] = mean
        stat_ref[1:2, span] = inverse


def in_vmem(count):
    return [pl.BlockSpec(memory_space=pltpu.VMEM)] * count


def standardize_a(idx, own, other, cols):
    half = own.shape[0]
    return pl.pallas_call(
        standardize_kernel,
        out_shape=(
            jax.ShapeDtypeStruct((2 * half, cols), bf16),
            jax.ShapeDtypeStruct((8, cols), f32),
        ),
        in_specs=[pl.BlockSpec(memory_space=pltpu.SMEM)] + in_vmem(2),
        out_specs=in_vmem(2),
        compiler_params=pltpu.CompilerParams(vmem_limit_bytes=VMEM_LIMIT),
        cost_estimate=pl.CostEstimate(
            flops=20 * half * cols, bytes_accessed=8 * half * cols, transcendentals=cols
        ),
    )(idx, own, other)


def tile_kernel(nz, ny, nc, nx, idx, a_ref, b_ref, corr_ref, part_ref, send_ref, norm_ref, high, low, tail):
    images, cols = norm_ref.shape
    cols_a = a_ref.shape[1]
    half, lanes = b_ref.shape[-2:]
    rows = images // (nz * ny * nc)
    take = rows // nx

    for h in range(cols // lanes):
        span = slice(h * lanes, (h + 1) * lanes)
        values = [b_ref[c, idx[0], h].astype(f32) for c in range(nc)]
        total = sum(jnp.sum(v, 0, keepdims=True) for v in values)
        square = sum(jnp.sum(v * v, 0, keepdims=True) for v in values)
        mean, inverse = statistics(total, square, images)
        for c in range(nc):
            norm_ref[c * half : (c + 1) * half, span] = ((values[c] - mean) * inverse).astype(bf16)
        for k, part in enumerate(kernel_terms(mean, 3) + kernel_terms(inverse, 3)):
            tail[8 + k : 9 + k, span] = part
        tail[16:17, span] = inverse

    norm = norm_ref[...]
    ones = jnp.ones((8, cols), bf16)
    for j in range(cols_a // cols):
        span = slice(j * cols, (j + 1) * cols)
        corr = dot(a_ref[:, span], norm, ((0,), (0,))) / images
        corr_ref[span, :] = corr
        upper, lower = (v.astype(bf16) for v in kernel_terms(corr * corr, 2))
        sums = dot(ones, upper, ((1,), (1,))) + dot(ones, lower, ((1,), (1,)))
        tail[j : j + 1, :] = sums[0:1]
        upper, lower = kernel_terms(2.0 * off_weight * corr, 2)
        high[span, :] = upper.astype(bf16)
        low[span, :] = lower.astype(bf16)

    picks = nz * ny * nc * take
    out = lax.broadcasted_iota(jnp.int32, (picks, images), 0)
    image = lax.broadcasted_iota(jnp.int32, (picks, images), 1)
    t, c, y, z = out & 1, (out >> 1) & 1, (out >> 2) & 3, out >> 4
    wanted = ((c * ny + y) * nz + z) * rows + idx[1] * take + t
    select = jnp.where(image == wanted, 1.0, 0.0).astype(bf16)
    picked = dot(select, norm, ((1,), (0,))).astype(bf16)
    gram = dot(picked, norm, ((1,), (1,)))
    for z in range(nz):
        send_ref[z, :, :images] = gram[z * 16 : z * 16 + 16].astype(bf16)

    place = pl.multiple_of(idx[2] * cols, cols)
    corr = corr_ref[pl.ds(place, cols), :]
    row = lax.broadcasted_iota(jnp.int32, corr.shape, 0)
    col = lax.broadcasted_iota(jnp.int32, corr.shape, 1)
    diagonal = jnp.sum(jnp.where(row == col, corr, 0.0), 0, keepdims=True)
    for k, part in enumerate(kernel_terms(diagonal, 2)):
        tail[14 + k : 15 + k, :] = part
    values = tail[0:16, :].astype(bf16)
    for z in range(nz):
        send_ref[z, :, images:] = values

    shift = -2.0 * (1.0 - diagonal) - 2.0 * off_weight * diagonal
    shift = jnp.where(idx[3] == 1, shift, 0.0)
    chunk = images // nx
    totals = []
    for k in range(nx):
        span = slice(k * chunk, (k + 1) * chunk)
        total = dot(a_ref[span, :], high[...], ((1,), (0,))) + dot(a_ref[span, :], low[...], ((1,), (0,)))
        totals.append(total + a_ref[span, pl.ds(place, cols)].astype(f32) * shift)
    along = 0.0
    for k in range(nx):
        along += jnp.sum(totals[k] * norm_ref[k * chunk : (k + 1) * chunk, :].astype(f32), 0, keepdims=True)
    along = along / images
    for k in range(nx):
        total = totals[k] - norm_ref[k * chunk : (k + 1) * chunk, :].astype(f32) * along
        to = lax.rem(k + nx - idx[1], nx)
        part_ref[pl.ds(pl.multiple_of(to * chunk, chunk), chunk), :] = (total * tail[16:17, :]).astype(bf16)


def tile(idx, norm_a, parts, sizes):
    nz, ny, nc, nx = sizes
    images, cols_a = norm_a.shape
    halves, half, lanes = parts.shape[2:]
    cols = halves * lanes
    return pl.pallas_call(
        functools.partial(tile_kernel, nz, ny, nc, nx),
        out_shape=(
            jax.ShapeDtypeStruct((cols_a, cols), f32),
            jax.ShapeDtypeStruct((images, cols), bf16),
            jax.ShapeDtypeStruct((nz, 16, images + cols), bf16),
        ),
        in_specs=[pl.BlockSpec(memory_space=pltpu.SMEM)] + in_vmem(2),
        out_specs=in_vmem(3),
        scratch_shapes=[
            pltpu.VMEM((images, cols), bf16),
            pltpu.VMEM((cols_a, cols), bf16),
            pltpu.VMEM((cols_a, cols), bf16),
            pltpu.VMEM((24, cols), f32),
        ],
        compiler_params=pltpu.CompilerParams(vmem_limit_bytes=VMEM_LIMIT),
        cost_estimate=pl.CostEstimate(
            flops=6 * images * cols_a * cols, bytes_accessed=4 * images * cols_a, transcendentals=0
        ),
    )(idx, norm_a, parts)


def local(view_a, view_b):
    nz, ny, nc = (lax.axis_size(a) for a in DP)
    nh, nx = (lax.axis_size(a) for a in FEAT)
    rows, cols_a = view_a.shape
    width = view_b.shape[1]
    cols_b = width // (nz * ny * nc)
    images = rows * nz * ny * nc
    iz, iy, ic = (lax.axis_index(a) for a in DP)
    ih, ix = (lax.axis_index(a) for a in FEAT)
    feat = ih * nx + ix
    n_yc = ny * nc

    with jax.named_scope("gather_z"):
        lanes = cols_b // (nx // nc)
        quarter = view_b.reshape(rows, nz * ny, nx, lanes)
        quarter = lax.dynamic_index_in_dim(quarter, ix, 2, False).reshape(rows, nz, ny * lanes)
        send = jnp.concatenate(
            [jnp.broadcast_to(view_a[None], (nz, rows, cols_a)), quarter.transpose(1, 0, 2)], 2
        )
        got = exchange(send, "zl").reshape(nz * rows, cols_a + ny * lanes)
    with jax.named_scope("gather_y"):
        send = jnp.concatenate(
            [
                jnp.broadcast_to(got[None, :, :cols_a], (ny, nz * rows, cols_a)),
                got[:, cols_a:].reshape(nz * rows, ny, lanes).transpose(1, 0, 2),
            ],
            2,
        )
        got = exchange(send, "y").reshape(ny * nz * rows, cols_a + lanes)
    with jax.named_scope("gather_core_x"):
        got_other = lax.ppermute(got, "c", SWAP)
        half = images // nc
        parts = exchange(jnp.broadcast_to(got[None, :, cols_a:], (nc * nx, half, lanes)), ("c", "x"))
        parts = parts.reshape(nc, nc, nx // nc, half, lanes)
    with jax.named_scope("standardize_a"):
        idx = jnp.stack([ic, ix, iy * nc + ic, (feat == iz).astype(jnp.int32)]).astype(jnp.int32)
        norm_a, stat_a = standardize_a(idx, got, got_other, cols_a)
        norm_a, parts = lax.optimization_barrier((norm_a, parts))
        mean_a, inverse_a = stat_a[0], stat_a[1]
    with jax.named_scope("tile"):
        correlation, part_b, send = tile(idx, norm_a, parts, (nz, ny, nc, nx))

    with jax.named_scope("reduce_z"):
        got = exchange(send, "zl")
    with jax.named_scope("sum_b_x"):
        n_rows = images // nx
        pieces = [part_b[:n_rows]]
        for k in range(1, nx):
            perm = [(i, (i + k) % nx) for i in range(nx)]
            pieces.append(lax.ppermute(part_b[k * n_rows : (k + 1) * n_rows], "x", perm))
        sum_b = sum(p.astype(f32) for p in pieces).astype(bf16)
        other = lax.ppermute(sum_b, "zh", SWAP)
    with jax.named_scope("reduce_yc"):
        take = rows // nx
        total = jnp.sum(got[:, :, :images].astype(f32), 0).reshape(n_yc, take * images // cols_b, cols_b)
        squares = jnp.sum(got[:, :8, images:].astype(f32), 0)
        aux = lax.dynamic_index_in_dim(got[:, 8:, images:], feat, 0, False).astype(f32)
        aux = jnp.stack([aux[0] + aux[1] + aux[2], aux[3] + aux[4] + aux[5], aux[6] + aux[7], aux[7]])
        right = jnp.concatenate([total, jnp.broadcast_to(aux[None], (n_yc, 4, cols_b))], 1)
        send = jnp.concatenate([jnp.broadcast_to(squares[None], (n_yc, 8, cols_b)), right], 2)
        got = exchange(send, ("y", "c"))
        squares = jnp.sum(got[:, :, :cols_b], 0).reshape(cols_a)
        gram = jnp.sum(got[:, :4, cols_b:], 0)
        mean_f, inverse_f, diag_f = (got[:, 4 + k, cols_b:].reshape(cols_a) for k in range(3))

    with jax.named_scope("shift_a"):
        shift = -2.0 * (1.0 - diag_f) - 2.0 * off_weight * diag_f
        projected = 2.0 * off_weight * squares + shift * diag_f
        own_b = ((view_b_columns(view_b, feat, cols_a) - mean_f) * inverse_f).astype(bf16).astype(f32)
        own_a = ((view_a.astype(f32) - mean_a) * inverse_a).astype(bf16).astype(f32)
        shifted = (own_b * shift - own_a * projected) * inverse_a
        scale = jnp.broadcast_to(2.0 * off_weight / images * inverse_a, (rows, cols_a))
    with jax.named_scope("gather_b_x"):
        sum_b = (sum_b.astype(f32) + other.astype(f32)).astype(bf16)
        upper, lower = terms(gram, 2)
        own = jnp.concatenate([sum_b, upper, lower], 0)
        shifted, scale = lax.optimization_barrier((shifted, scale))
        got = exchange(jnp.broadcast_to(own[None], (nx,) + own.shape), "x")
        grad_b = got[:, :n_rows].reshape(nc, ny, nz, rows, cols_b).transpose(2, 1, 0, 3, 4)
        grad_b = grad_b.reshape(images, cols_b).astype(f32)
        gram = got[:, n_rows:].reshape(nx, 2, take, images).transpose(1, 0, 2, 3).reshape(2 * rows, images)
    with jax.named_scope("grad_a"):
        both = dot(gram, norm_a, ((1,), (0,)))
        grad_a = (both[:rows] + both[rows:]) * scale + shifted
    return correlation, grad_a, grad_b


def view_b_columns(view_b, feat, cols_a):
    return lax.dynamic_slice_in_dim(view_b, feat * cols_a, cols_a, 1).astype(f32)


def solution(mesh):
    sizes = (8, 4, 2, 2, 4)
    fine = Mesh(mesh.devices.reshape(sizes), AXES)
    in_specs = (P(DP, FEAT), P(DP, None))
    out_specs = (P(FEAT, DP), P(DP, FEAT), P(None, DP))
    return jax.shard_map(local, mesh=fine, in_specs=in_specs, out_specs=out_specs, check_vma=False)
```

time: 136 us -> 129 us (0.949)
  waiting for transfers between devices: 38.4 us -> 23.2 us
  Pallas kernels: 0 us -> 7.02 us
  starting transfers between devices: 30.7 us -> 36.9 us
  other arithmetic: 7.42 us -> 2.54 us
  blocking collectives: 46.4 us -> 50 us
  matrix products: 3.1 us -> 0.39 us
  local copies, waits for them, and re-layouts: 8.38 us -> 6.65 us
    all_to_all x5 -> x4, waiting for transfers between devices: 38.4 us -> 15.2 us  [exchange(): lax.all_to_all(values, axis, split_axis=0, concat_axis=0, tiled=False)]
    ppermute x1 -> x5, starting transfers between devices: 8.21 us -> 18.6 us  [the longest x3 8.51 us: local(): pieces.append(lax.ppermute(part_b[k * n_rows:(k + 1) * n_rows], 'x', perm))]
    ppermute x1 -> x5, waiting for transfers between devices: 0.01 us -> 7.93 us  [the longest x3 5.4 us: local(): pieces.append(lax.ppermute(part_b[k * n_rows:(k + 1) * n_rows], 'x', perm))]
    pallas_call x0 -> x2, Pallas kernels: none -> 7.02 us  [the longest x1 5.23 us: tile(): pl.pallas_call(functools.partial(tile_kernel, nz, ny, nc, nx), out_shape=...]
    all_to_all x5 -> x4, starting transfers between devices: 22.5 us -> 18.3 us  [exchange(): lax.all_to_all(values, axis, split_axis=0, concat_axis=0, tiled=False)]
    all_to_all x3 -> x2, blocking collectives: 46.4 us -> 50 us  [exchange(): lax.all_to_all(values, axis, split_axis=0, concat_axis=0, tiled=False)]
    convert_element_type x4 -> x2, other arithmetic: 3.09 us -> 0.05 us  [the longest x1 0.04 us: local(): sum_b = sum((p.astype(f32) for p in pieces)).astype(bf16)]
    dot_general x5 -> x1, matrix products: 3.1 us -> 0.39 us  [dot(): lax.dot_general(left, right, (contract, ((), ())), preferred_element_type...]
  transfers between devices with their start and end apart: 6 -> 9, of which waited for: 5 -> 6; matrix products, arithmetic and copies ran while one was open for 4% -> 2% of each run, Pallas kernels for 0% -> 1%
where the time goes in v4:
time: 129 us; the launch traced here: 128 us
  blocking collectives  50 us (39%)
  starting transfers between devices  36.9 us (29%)
  waiting for transfers between devices  23.2 us (18%)
  Pallas kernels  7.02 us (5%)
  local copies, waits for them, and re-layouts  6.65 us (5%)
  other arithmetic  2.54 us (2%)
    all_to_all x2, blocking collectives, exchange(): lax.all_to_all(values, axis, split_axis=0, concat_axis=0, tiled=False)  50 us
    all_to_all x4, starting transfers between devices, exchange(): lax.all_to_all(values, axis, split_axis=0, concat_axis=0, tiled=False)  18.3 us
    all_to_all x4, waiting for transfers between devices, exchange(): lax.all_to_all(values, axis, split_axis=0, concat_axis=0, tiled=False)  15.2 us
    ppermute x3, starting transfers between devices, local(): pieces.append(lax.ppermute(part_b[k * n_rows:(k + 1) * n_rows], 'x', perm))  8.51 us
    ppermute x1, starting transfers between devices, local(): other = lax.ppermute(sum_b, 'zh', SWAP)  8.22 us
    ppermute x3, waiting for transfers between devices, local(): pieces.append(lax.ppermute(part_b[k * n_rows:(k + 1) * n_rows], 'x', perm))  5.4 us
    pallas_call x1, Pallas kernels, tile(): pl.pallas_call(functools.partial(tile_kernel, nz, ny, nc, nx), out_shape=...  5.23 us
  transfers between devices with their start and end apart: 9, of which 6 were waited for; matrix products, arithmetic and copies ran while one was open for 2% of the time, Pallas kernels for 1%

profile of v4, /device:TPU:32, one launch (start us, length us, event | category | flops | bytes accessed | tf_op | source)
XLA Modules:
  0.0 127.6 jit_solution(14770767177124919235)
XLA Ops:
  0.6 0.8 constant_dynamic-slice_fusion
  1.5 0.8 broadcast_in_dim.14
  2.3 31.3 %all_to_all.30 = bf16[8,8,2560]{2,1,0:T(8,128)(2,1)S(1)} all-to-all(bf16[8,8,2560]{2,1,0:T(8,128)(2,1)S(1)} %pad_maximum_fusion.1), channel_id=1, replica_groups=mesh['zl'=8,'y'=4,'c'=2,'zh'=2,'x'=4] {'zl'}, dimensions={0} | all-to-all | bytes 655360 | tf_op jit(solution)/shard_map/gather_z/all_to_all | solution.py:21
  33.7 0.1 broadcast_in_dim.15
  33.8 0.1 pad_maximum_fusion
  33.9 18.6 %all_to_all.31 = bf16[4,64,2176]{2,1,0:T(8,128)(2,1)S(1)} all-to-all(bf16[4,64,2176]{2,1,0:T(8,128)(2,1)S(1)} %pad_maximum_fusion), channel_id=1, replica_groups=mesh['zl'=8,'y'=4,'c'=2,'zh'=2,'x'=4] {'y'}, dimensions={0} | all-to-all | bytes 2228224 | tf_op jit(solution)/shard_map/gather_y/all_to_all | solution.py:21
  52.6 1.9 %collective-permute-start = (bf16[256,2176]{1,0:T(8,128)(2,1)S(1)}, bf16[256,2176]{1,0:T(8,128)(2,1)S(1)}, u32[]{:S(2)}, u32[]{:S(2)}) collective-permute-start(bf16[256,2176]{1,0:T(8,128)(2,1)S(1)} %bitcast.42), channel_id=1, source_target_pairs={{0,8},{8,0},{1,9},{9,1},{2,10},{10,2},{3,11},{11,3},{4,12},{12,4},... | collective-permute-start | bytes 3342344 | tf_op jit(solution)/shard_map/gather_core_x/ppermute | solution.py:219
  54.5 0.9 broadcast_in_dim.16
  55.4 4.4 %all-to-all-start.2 = ((bf16[8,256,128]{2,1,0:T(8,128)(2,1)}), bf16[8,256,128]{2,1,0:T(8,128)(2,1)}, u32[]{:S(2)}, u32[]{:S(2)}) async-start(bf16[8,256,128]{2,1,0:T(8,128)(2,1)} %broadcast_in_dim.16), calls=%async_computation.2 | async-start | bytes 1048576 | tf_op jit(solution)/shard_map/gather_core_x/all_to_all | solution.py:21
  59.8 0.1 pad_add_fusion.idx
  59.9 0.0 collective-permute-done.other_ref
  59.9 0.0 copy-start
  59.9 1.0 copy-done
  60.8 0.0 copy-start.1
  60.9 1.2 copy-done.1
  62.1 1.8 %standardize_a.1 = (bf16[512,2048]{1,0:T(8,128)(2,1)S(1)}, f32[8,2048]{1,0:T(8,128)S(1)}) custom-call(s32[4]{0:T(128)S(1)} %pad_add_fusion.idx, bf16[256,2176]{1,0:T(8,128)(2,1)S(1)} %bitcast.44, bf16[256,2176]{1,0:T(8,128)(2,1)S(1)} %copy-done.1), custom_call_target="tpu_custom_call" | custom-call | flops 10485760 | bytes 4194304 | tf_op jit(solution)/shard_map/standardize_a/pallas_call | solution.py:75
  63.9 5.7 %all-to-all-done.2 = bf16[8,256,128]{2,1,0:T(8,128)(2,1)} async-done(((bf16[8,256,128]{2,1,0:T(8,128)(2,1)}), bf16[8,256,128]{2,1,0:T(8,128)(2,1)}, u32[]{:S(2)}, u32[]{:S(2)}) %all-to-all-start.2) | async-done | bytes 524320 | tf_op jit(solution)/shard_map/gather_core_x/all_to_all | solution.py:21
  69.6 5.2 %tile.1 = (f32[2048,256]{1,0:T(8,128)}, bf16[512,256]{1,0:T(8,128)(2,1)S(1)}, bf16[8,16,768]{2,1,0:T(8,128)(2,1)}) custom-call(s32[4]{0:T(128)S(1)} %pad_add_fusion.idx, bf16[512,2048]{1,0:T(8,128)(2,1)S(1)} %get-tuple-element.13.a_ref, bf16[2,2,2,256,128]{4,3,2,1,0:T(8,128)(2,1)} %bitcast.10.b_ref), custom_call_target="tpu_custom_call" | custom-call | flops 1610612736 | bytes 4194304 | tf_op jit(solution)/shard_map/tile/pallas_call | solution.py:167
  74.8 0.0 copy-start.2
  74.8 7.1 %all-to-all-start.3 = ((bf16[8,16,768]{2,1,0:T(8,128)(2,1)}), bf16[8,16,768]{2,1,0:T(8,128)(2,1)S(1)}, u32[]{:S(2)}, u32[]{:S(2)}) async-start(bf16[8,16,768]{2,1,0:T(8,128)(2,1)} %get-tuple-element.17), calls=%async_computation.3 | async-start | bytes 393216 | tf_op jit(solution)/shard_map/reduce_z/all_to_all | solution.py:21
  81.9 3.7 %collective-permute-start.3 = (bf16[128,256]{1,0:T(8,128)(2,1)S(1)}, bf16[128,256]{1,0:T(8,128)(2,1)S(1)}, u32[]{:S(2)}, u32[]{:S(2)}) collective-permute-start(bf16[128,256]{1,0:T(8,128)(2,1)S(1)} %get-tuple-element.22), channel_id=1, source_target_pairs={{0,3},{1,0},{2,1},{3,2},{4,7},{5,4},{6,5},{7,6},{8,11},{9,8},{10,9... | collective-permute-start | bytes 196616 | tf_op jit(solution)/shard_map/sum_b_x/ppermute | solution.py:238
  85.6 2.9 %collective-permute-start.2 = (bf16[128,256]{1,0:T(8,128)(2,1)S(1)}, bf16[128,256]{1,0:T(8,128)(2,1)S(1)}, u32[]{:S(2)}, u32[]{:S(2)}) collective-permute-start(bf16[128,256]{1,0:T(8,128)(2,1)S(1)} %get-tuple-element.23), channel_id=1, source_target_pairs={{0,2},{1,3},{2,0},{3,1},{4,6},{5,7},{6,4},{7,5},{8,10},{9,11},{10,... | collective-permute-start | bytes 196616 | tf_op jit(solution)/shard_map/sum_b_x/ppermute | solution.py:238
  88.5 1.9 %collective-permute-start.1 = (bf16[128,256]{1,0:T(8,128)(2,1)S(1)}, bf16[128,256]{1,0:T(8,128)(2,1)S(1)}, u32[]{:S(2)}, u32[]{:S(2)}) collective-permute-start(bf16[128,256]{1,0:T(8,128)(2,1)S(1)} %get-tuple-element.21), channel_id=1, source_target_pairs={{0,1},{1,2},{2,3},{3,0},{4,5},{5,6},{6,7},{7,4},{8,9},{9,10},{10,1... | collective-permute-start | bytes 196616 | tf_op jit(solution)/shard_map/sum_b_x/ppermute | solution.py:238
  90.5 0.0 collective-permute-done.3
  90.5 2.8 %collective-permute-done.2 = bf16[128,256]{1,0:T(8,128)(2,1)S(1)} collective-permute-done((bf16[128,256]{1,0:T(8,128)(2,1)S(1)}, bf16[128,256]{1,0:T(8,128)(2,1)S(1)}, u32[]{:S(2)}, u32[]{:S(2)}) %collective-permute-start.2) | collective-permute-done | bytes 65568 | tf_op jit(solution)/shard_map/sum_b_x/ppermute | solution.py:238
  93.3 2.6 %collective-permute-done.1 = bf16[128,256]{1,0:T(8,128)(2,1)S(1)} collective-permute-done((bf16[128,256]{1,0:T(8,128)(2,1)S(1)}, bf16[128,256]{1,0:T(8,128)(2,1)S(1)}, u32[]{:S(2)}, u32[]{:S(2)}) %collective-permute-start.1) | collective-permute-done | bytes 65568 | tf_op jit(solution)/shard_map/sum_b_x/ppermute | solution.py:238
  95.9 8.2 %collective-permute-start.4 = (bf16[128,256]{1,0:T(8,128)(2,1)S(1)}, bf16[128,256]{1,0:T(8,128)(2,1)S(1)}, u32[]{:S(2)}, u32[]{:S(2)}) collective-permute-start(bf16[128,256]{1,0:T(8,128)(2,1)S(1)} %add_convert_fusion.1), channel_id=1, source_target_pairs={{0,4},{4,0},{1,5},{5,1},{2,6},{6,2},{3,7},{7,3},{8,12},{12,8},{9,1... | collective-permute-start | bytes 196616 | tf_op jit(solution)/shard_map/sum_b_x/ppermute | solution.py:240
  104.2 0.0 all-to-all-done.3
  104.3 0.7 maximum_maximum_fusion
  105.0 3.4 %all-to-all-start.4 = ((f32[8,8,512]{2,1,0:T(8,128)}), f32[8,8,512]{2,1,0:T(8,128)S(1)}, u32[]{:S(2)}, u32[]{:S(2)}) async-start(f32[8,8,512]{2,1,0:T(8,128)} %maximum_maximum_fusion), calls=%async_computation.4 | async-start | bytes 262144 | tf_op jit(solution)/shard_map/reduce_yc/all_to_all | solution.py:21
  108.4 2.5 %collective-permute-done.4 = bf16[128,256]{1,0:T(8,128)(2,1)S(1)} collective-permute-done((bf16[128,256]{1,0:T(8,128)(2,1)S(1)}, bf16[128,256]{1,0:T(8,128)(2,1)S(1)}, u32[]{:S(2)}, u32[]{:S(2)}) %collective-permute-start.4) | collective-permute-done | bytes 65568 | tf_op jit(solution)/shard_map/sum_b_x/ppermute | solution.py:240
  110.9 3.5 %all-to-all-done.4 = f32[8,8,512]{2,1,0:T(8,128)S(1)} async-done(((f32[8,8,512]{2,1,0:T(8,128)}), f32[8,8,512]{2,1,0:T(8,128)S(1)}, u32[]{:S(2)}, u32[]{:S(2)}) %all-to-all-start.4) | async-done | bytes 131104 | tf_op jit(solution)/shard_map/reduce_yc/all_to_all | solution.py:21
  114.5 0.7 broadcast_in_dim.19
  115.3 3.5 %all-to-all-start.5 = ((bf16[4,136,256]{2,1,0:T(8,128)(2,1)}), bf16[4,136,256]{2,1,0:T(8,128)(2,1)S(1)}, u32[]{:S(2)}, u32[]{:S(2)}) async-start(bf16[4,136,256]{2,1,0:T(8,128)(2,1)} %broadcast_in_dim.19), calls=%async_computation.5 | async-start | bytes 557056 | tf_op jit(solution)/shard_map/gather_b_x/all_to_all | solution.py:21
  118.8 0.0 copy-done.2
  118.8 0.8 subtract_multiply_fusion
  119.6 6.0 %all-to-all-done.5 = bf16[4,136,256]{2,1,0:T(8,128)(2,1)S(1)} async-done(((bf16[4,136,256]{2,1,0:T(8,128)(2,1)}), bf16[4,136,256]{2,1,0:T(8,128)(2,1)S(1)}, u32[]{:S(2)}, u32[]{:S(2)}) %all-to-all-start.5) | async-done | bytes 278560 | tf_op jit(solution)/shard_map/gather_b_x/all_to_all | solution.py:21
  125.7 0.4 fusion.10
  126.1 0.9 copy.13
  127.0 0.6 fusion.1
  (35 shorter events, 0.5 us)
Async XLA Ops:
  52.6 7.3 %collective-permute-start = (bf16[256,2176]{1,0:T(8,128)(2,1)S(1)}, bf16[256,2176]{1,0:T(8,128)(2,1)S(1)}, u32[]{:S(2)}, u32[]{:S(2)}) collective-permute-start(bf16[256,2176]{1,0:T(8,128)(2,1)S(1)} %bitcast.42), channel_id=1, source_target_pairs={{0,8},{8,0},{1,9},{9,1},{2,10},{10,2},{3,11},{11,3},{4,12},{12,4},... | collective-permute-start | bytes 3342344 | tf_op jit(solution)/shard_map/gather_core_x/ppermute | solution.py:219
  55.4 14.2 %all-to-all-start.2 = ((bf16[8,256,128]{2,1,0:T(8,128)(2,1)}), bf16[8,256,128]{2,1,0:T(8,128)(2,1)}, u32[]{:S(2)}, u32[]{:S(2)}) async-start(bf16[8,256,128]{2,1,0:T(8,128)(2,1)} %broadcast_in_dim.16), calls=%async_computation.2 | async-start | bytes 1048576 | tf_op jit(solution)/shard_map/gather_core_x/all_to_all | solution.py:21
  59.9 1.0 copy-start
  60.8 1.2 copy-start.1
  74.8 43.9 %copy-start.2 = (bf16[8,2048]{1,0:T(8,128)(2,1)S(1)}, bf16[8,2048]{1,0:T(8,128)(2,1)}, u32[]{:S(2)}) copy-start(bf16[8,2048]{1,0:T(8,128)(2,1)} %param.2) | copy-start | bytes 98308
  74.8 29.3 %all-to-all-start.3 = ((bf16[8,16,768]{2,1,0:T(8,128)(2,1)}), bf16[8,16,768]{2,1,0:T(8,128)(2,1)S(1)}, u32[]{:S(2)}, u32[]{:S(2)}) async-start(bf16[8,16,768]{2,1,0:T(8,128)(2,1)} %get-tuple-element.17), calls=%async_computation.3 | async-start | bytes 393216 | tf_op jit(solution)/shard_map/reduce_z/all_to_all | solution.py:21
  81.9 8.6 %collective-permute-start.3 = (bf16[128,256]{1,0:T(8,128)(2,1)S(1)}, bf16[128,256]{1,0:T(8,128)(2,1)S(1)}, u32[]{:S(2)}, u32[]{:S(2)}) collective-permute-start(bf16[128,256]{1,0:T(8,128)(2,1)S(1)} %get-tuple-element.22), channel_id=1, source_target_pairs={{0,3},{1,0},{2,1},{3,2},{4,7},{5,4},{6,5},{7,6},{8,11},{9,8},{10,9... | collective-permute-start | bytes 196616 | tf_op jit(solution)/shard_map/sum_b_x/ppermute | solution.py:238
  85.6 7.7 %collective-permute-start.2 = (bf16[128,256]{1,0:T(8,128)(2,1)S(1)}, bf16[128,256]{1,0:T(8,128)(2,1)S(1)}, u32[]{:S(2)}, u32[]{:S(2)}) collective-permute-start(bf16[128,256]{1,0:T(8,128)(2,1)S(1)} %get-tuple-element.23), channel_id=1, source_target_pairs={{0,2},{1,3},{2,0},{3,1},{4,6},{5,7},{6,4},{7,5},{8,10},{9,11},{10,... | collective-permute-start | bytes 196616 | tf_op jit(solution)/shard_map/sum_b_x/ppermute | solution.py:238
  88.5 7.4 %collective-permute-start.1 = (bf16[128,256]{1,0:T(8,128)(2,1)S(1)}, bf16[128,256]{1,0:T(8,128)(2,1)S(1)}, u32[]{:S(2)}, u32[]{:S(2)}) collective-permute-start(bf16[128,256]{1,0:T(8,128)(2,1)S(1)} %get-tuple-element.21), channel_id=1, source_target_pairs={{0,1},{1,2},{2,3},{3,0},{4,5},{5,6},{6,7},{7,4},{8,9},{9,10},{10,1... | collective-permute-start | bytes 196616 | tf_op jit(solution)/shard_map/sum_b_x/ppermute | solution.py:238
  95.9 15.0 %collective-permute-start.4 = (bf16[128,256]{1,0:T(8,128)(2,1)S(1)}, bf16[128,256]{1,0:T(8,128)(2,1)S(1)}, u32[]{:S(2)}, u32[]{:S(2)}) collective-permute-start(bf16[128,256]{1,0:T(8,128)(2,1)S(1)} %add_convert_fusion.1), channel_id=1, source_target_pairs={{0,4},{4,0},{1,5},{5,1},{2,6},{6,2},{3,7},{7,3},{8,12},{12,8},{9,1... | collective-permute-start | bytes 196616 | tf_op jit(solution)/shard_map/sum_b_x/ppermute | solution.py:240
  105.0 9.4 %all-to-all-start.4 = ((f32[8,8,512]{2,1,0:T(8,128)}), f32[8,8,512]{2,1,0:T(8,128)S(1)}, u32[]{:S(2)}, u32[]{:S(2)}) async-start(f32[8,8,512]{2,1,0:T(8,128)} %maximum_maximum_fusion), calls=%async_computation.4 | async-start | bytes 262144 | tf_op jit(solution)/shard_map/reduce_yc/all_to_all | solution.py:21
  115.3 10.4 %all-to-all-start.5 = ((bf16[4,136,256]{2,1,0:T(8,128)(2,1)}), bf16[4,136,256]{2,1,0:T(8,128)(2,1)S(1)}, u32[]{:S(2)}, u32[]{:S(2)}) async-start(bf16[4,136,256]{2,1,0:T(8,128)(2,1)} %broadcast_in_dim.19), calls=%async_computation.5 | async-start | bytes 557056 | tf_op jit(solution)/shard_map/gather_b_x/all_to_all | solution.py:21

commit v5 on v4

--- a/solution.py
+++ b/solution.py
@@ -14,7 +14,7 @@
 DP = ("zl", "y", "c")
 FEAT = ("zh", "x")
 SWAP = [(0, 1), (1, 0)]
-VMEM_LIMIT = 40 * 1024 * 1024
+VMEM_LIMIT = 14 * 1024 * 1024
 
 
 def exchange(values, axis):
@@ -45,6 +45,52 @@
 def statistics(total, square, images):
     mean = total / images
     return mean, lax.rsqrt(square / images - mean * mean + epsilon)
+
+
+def pack_kernel(ny, nc, idx, a_hbm, b_hbm, send_ref, a_ref, b_ref, sems):
+    nz, rows, _ = send_ref.shape
+    cols_a = a_ref.shape[1]
+    copy_a = pltpu.make_async_copy(a_hbm, a_ref, sems.at[0])
+    copy_b = pltpu.make_async_copy(b_hbm, b_ref, sems.at[1])
+    copy_b.start()
+    copy_a.start()
+    copy_a.wait()
+    values = a_ref[...]
+    for z in range(nz):
+        send_ref[z, :, :cols_a] = values
+    copy_b.wait()
+    lanes = (send_ref.shape[2] - cols_a) // ny
+    upper = idx[1] < 2
+    column = (idx[1] & 1) * lanes
+    keep = (lax.broadcasted_iota(jnp.int32, (rows, lanes), 0) < rows // 2) == upper
+    for z in range(nz):
+        for y in range(ny):
+            pair = []
+            for c in range(nc):
+                first = ((z * ny + y) * nc + c) * 2 * lanes
+                first = pl.multiple_of(first + column, lanes)
+                pair.append(b_ref[:, pl.ds(first, lanes)].astype(f32))
+            moved = pltpu.roll(jnp.where(upper, pair[1], pair[0]), rows // 2, 0)
+            mixed = jnp.where(keep, jnp.where(upper, pair[0], pair[1]), moved)
+            send_ref[z, :, cols_a + y * lanes : cols_a + (y + 1) * lanes] = mixed.astype(bf16)
+
+
+def pack(idx, view_a, view_b, sizes):
+    nz, ny, nc, nx = sizes
+    rows, cols_a = view_a.shape
+    lanes = view_b.shape[1] // (nz * ny * nc * 2)
+    return pl.pallas_call(
+        functools.partial(pack_kernel, ny, nc),
+        out_shape=jax.ShapeDtypeStruct((nz, rows, cols_a + ny * lanes), bf16),
+        in_specs=[pl.BlockSpec(memory_space=pltpu.SMEM)] + [pl.BlockSpec(memory_space=pl.ANY)] * 2,
+        out_specs=in_vmem(1)[0],
+        scratch_shapes=[
+            pltpu.VMEM(view_a.shape, bf16),
+            pltpu.VMEM(view_b.shape, bf16),
+            pltpu.SemaphoreType.DMA((2,)),
+        ],
+        compiler_params=pltpu.CompilerParams(vmem_limit_bytes=VMEM_LIMIT),
+    )(idx, view_a, view_b)
 
 
 def standardize_kernel(idx, own_ref, other_ref, norm_ref, stat_ref):
@@ -87,38 +133,108 @@
     )(idx, own, other)
 
 
-def tile_kernel(nz, ny, nc, nx, idx, a_ref, b_ref, corr_ref, part_ref, send_ref, norm_ref, high, low, tail):
+def tile_kernel(
+    nz, ny, nc, nx, idx, a_ref, b_ref, out_ref, part_ref, norm_ref, tail, corr_ref, high, sems
+):
     images, cols = norm_ref.shape
     cols_a = a_ref.shape[1]
-    half, lanes = b_ref.shape[-2:]
+    part, lanes = b_ref.shape[-2:]
+    parts = b_ref.shape[1]
+    half = part * parts
     rows = images // (nz * ny * nc)
-    take = rows // nx
-
+
+    deep = part // rows
+    keep = lax.broadcasted_iota(jnp.int32, (deep, rows, lanes), 1) < rows // 2
     for h in range(cols // lanes):
         span = slice(h * lanes, (h + 1) * lanes)
-        values = [b_ref[c, idx[0], h].astype(f32) for c in range(nc)]
+        values = [b_ref[c, k, h].astype(f32) for c in range(nc) for k in range(parts)]
         total = sum(jnp.sum(v, 0, keepdims=True) for v in values)
         square = sum(jnp.sum(v * v, 0, keepdims=True) for v in values)
         mean, inverse = statistics(total, square, images)
+        values = [((v - mean) * inverse).reshape(deep, rows, lanes) for v in values]
         for c in range(nc):
-            norm_ref[c * half : (c + 1) * half, span] = ((values[c] - mean) * inverse).astype(bf16)
-        for k, part in enumerate(kernel_terms(mean, 3) + kernel_terms(inverse, 3)):
-            tail[8 + k : 9 + k, span] = part
+            first, second = values[2 * c], values[2 * c + 1]
+            even = jnp.where(keep, first, pltpu.roll(second, rows // 2, 1))
+            odd = jnp.where(keep, pltpu.roll(first, rows // 2, 1), second)
+            norm_ref[c * half : (c + 1) * half, span] = jnp.stack([even, odd], 1).reshape(half, lanes).astype(bf16)
+        for k, term in enumerate(kernel_terms(mean, 3) + kernel_terms(inverse, 3)):
+            tail[8 + k : 9 + k, span] = term
         tail[16:17, span] = inverse
 
     norm = norm_ref[...]
     ones = jnp.ones((8, cols), bf16)
+    copies = []
     for j in range(cols_a // cols):
         span = slice(j * cols, (j + 1) * cols)
         corr = dot(a_ref[:, span], norm, ((0,), (0,))) / images
         corr_ref[span, :] = corr
+        place = pl.ds(j * cols, cols)
+        copies.append(pltpu.make_async_copy(corr_ref.at[place], out_ref.at[place], sems.at[j]))
+        copies[-1].start()
         upper, lower = (v.astype(bf16) for v in kernel_terms(corr * corr, 2))
         sums = dot(ones, upper, ((1,), (1,))) + dot(ones, lower, ((1,), (1,)))
         tail[j : j + 1, :] = sums[0:1]
-        upper, lower = kernel_terms(2.0 * off_weight * corr, 2)
-        high[span, :] = upper.astype(bf16)
-        low[span, :] = lower.astype(bf16)
-
+        high[span, :] = corr.astype(bf16)
+
+    place = pl.multiple_of(idx[2] * cols, cols)
+    corr = corr_ref[pl.ds(place, cols), :]
+    row = lax.broadcasted_iota(jnp.int32, corr.shape, 0)
+    col = lax.broadcasted_iota(jnp.int32, corr.shape, 1)
+    diagonal = jnp.sum(jnp.where(row == col, corr, 0.0), 0, keepdims=True)
+    for k, part in enumerate(kernel_terms(diagonal, 2)):
+        tail[14 + k : 15 + k, :] = part
+    shift = -2.0 * (1.0 - diagonal) - 2.0 * off_weight * diagonal
+    shift = jnp.where(idx[3] == 1, shift, 0.0)
+    chunk = images // nx
+    totals = []
+    for k in range(nx):
+        span = slice(k * chunk, (k + 1) * chunk)
+        total = dot(a_ref[span, :], high[...], ((1,), (0,))) * (2.0 * off_weight)
+        totals.append(total + a_ref[span, pl.ds(place, cols)].astype(f32) * shift)
+    along = 0.0
+    for k in range(nx):
+        along += jnp.sum(totals[k] * norm_ref[k * chunk : (k + 1) * chunk, :].astype(f32), 0, keepdims=True)
+    along = along / images
+    for k in range(nx):
+        total = totals[k] - norm_ref[k * chunk : (k + 1) * chunk, :].astype(f32) * along
+        to = k ^ idx[1]
+        to = to ^ (to >> 1)
+        part_ref[pl.ds(pl.multiple_of(to * chunk, chunk), chunk), :] = (total * tail[16:17, :]).astype(bf16)
+    for copy in copies:
+        copy.wait()
+
+
+def tile(idx, norm_a, parts, sizes):
+    nz, ny, nc, nx = sizes
+    images, cols_a = norm_a.shape
+    cols = parts.shape[2] * parts.shape[4]
+    return pl.pallas_call(
+        functools.partial(tile_kernel, nz, ny, nc, nx),
+        out_shape=(
+            jax.ShapeDtypeStruct((cols_a, cols), f32),
+            jax.ShapeDtypeStruct((images, cols), bf16),
+            jax.ShapeDtypeStruct((images, cols), bf16),
+            jax.ShapeDtypeStruct((24, cols), f32),
+        ),
+        in_specs=[pl.BlockSpec(memory_space=pltpu.SMEM)] + in_vmem(2),
+        out_specs=[pl.BlockSpec(memory_space=pl.ANY)] + in_vmem(3),
+        scratch_shapes=[
+            pltpu.VMEM((cols_a, cols), f32),
+            pltpu.VMEM((cols_a, cols), bf16),
+            pltpu.SemaphoreType.DMA((cols_a // cols,)),
+        ],
+        compiler_params=pltpu.CompilerParams(vmem_limit_bytes=VMEM_LIMIT),
+        cost_estimate=pl.CostEstimate(
+            flops=6 * images * cols_a * cols, bytes_accessed=4 * images * cols_a, transcendentals=0
+        ),
+    )(idx, norm_a, parts)
+
+
+def gram_kernel(nz, ny, nc, nx, idx, norm_ref, tail, send_ref):
+    images, cols = norm_ref.shape
+    rows = images // (nz * ny * nc)
+    take = rows // nx
+    norm = norm_ref[...]
     picks = nz * ny * nc * take
     out = lax.broadcasted_iota(jnp.int32, (picks, images), 0)
     image = lax.broadcasted_iota(jnp.int32, (picks, images), 1)
@@ -130,60 +246,24 @@
     for z in range(nz):
         send_ref[z, :, :images] = gram[z * 16 : z * 16 + 16].astype(bf16)
 
-    place = pl.multiple_of(idx[2] * cols, cols)
-    corr = corr_ref[pl.ds(place, cols), :]
-    row = lax.broadcasted_iota(jnp.int32, corr.shape, 0)
-    col = lax.broadcasted_iota(jnp.int32, corr.shape, 1)
-    diagonal = jnp.sum(jnp.where(row == col, corr, 0.0), 0, keepdims=True)
-    for k, part in enumerate(kernel_terms(diagonal, 2)):
-        tail[14 + k : 15 + k, :] = part
     values = tail[0:16, :].astype(bf16)
     for z in range(nz):
         send_ref[z, :, images:] = values
 
-    shift = -2.0 * (1.0 - diagonal) - 2.0 * off_weight * diagonal
-    shift = jnp.where(idx[3] == 1, shift, 0.0)
-    chunk = images // nx
-    totals = []
-    for k in range(nx):
-        span = slice(k * chunk, (k + 1) * chunk)
-        total = dot(a_ref[span, :], high[...], ((1,), (0,))) + dot(a_ref[span, :], low[...], ((1,), (0,)))
-        totals.append(total + a_ref[span, pl.ds(place, cols)].astype(f32) * shift)
-    along = 0.0
-    for k in range(nx):
-        along += jnp.sum(totals[k] * norm_ref[k * chunk : (k + 1) * chunk, :].astype(f32), 0, keepdims=True)
-    along = along / images
-    for k in range(nx):
-        total = totals[k] - norm_ref[k * chunk : (k + 1) * chunk, :].astype(f32) * along
-        to = lax.rem(k + nx - idx[1], nx)
-        part_ref[pl.ds(pl.multiple_of(to * chunk, chunk), chunk), :] = (total * tail[16:17, :]).astype(bf16)
-
-
-def tile(idx, norm_a, parts, sizes):
-    nz, ny, nc, nx = sizes
-    images, cols_a = norm_a.shape
-    halves, half, lanes = parts.shape[2:]
-    cols = halves * lanes
+
+def gram_part(idx, norm_b, tail, sizes):
+    nz = sizes[0]
+    images, cols = norm_b.shape
     return pl.pallas_call(
-        functools.partial(tile_kernel, nz, ny, nc, nx),
-        out_shape=(
-            jax.ShapeDtypeStruct((cols_a, cols), f32),
-            jax.ShapeDtypeStruct((images, cols), bf16),
-            jax.ShapeDtypeStruct((nz, 16, images + cols), bf16),
-        ),
+        functools.partial(gram_kernel, *sizes),
+        out_shape=jax.ShapeDtypeStruct((nz, 16, images + cols), bf16),
         in_specs=[pl.BlockSpec(memory_space=pltpu.SMEM)] + in_vmem(2),
-        out_specs=in_vmem(3),
-        scratch_shapes=[
-            pltpu.VMEM((images, cols), bf16),
-            pltpu.VMEM((cols_a, cols), bf16),
-            pltpu.VMEM((cols_a, cols), bf16),
-            pltpu.VMEM((24, cols), f32),
-        ],
+        out_specs=in_vmem(1)[0],
         compiler_params=pltpu.CompilerParams(vmem_limit_bytes=VMEM_LIMIT),
         cost_estimate=pl.CostEstimate(
-            flops=6 * images * cols_a * cols, bytes_accessed=4 * images * cols_a, transcendentals=0
-        ),
-    )(idx, norm_a, parts)
+            flops=8 * images * images * cols, bytes_accessed=16 * images * cols, transcendentals=0
+        ),
+    )(idx, norm_b, tail)
 
 
 def local(view_a, view_b):
@@ -199,12 +279,9 @@
     n_yc = ny * nc
 
     with jax.named_scope("gather_z"):
-        lanes = cols_b // (nx // nc)
-        quarter = view_b.reshape(rows, nz * ny, nx, lanes)
-        quarter = lax.dynamic_index_in_dim(quarter, ix, 2, False).reshape(rows, nz, ny * lanes)
-        send = jnp.concatenate(
-            [jnp.broadcast_to(view_a[None], (nz, rows, cols_a)), quarter.transpose(1, 0, 2)], 2
-        )
+        lanes = cols_b // 2
+        idx = jnp.stack([ic, ix, iy * nc + ic, (feat == iz).astype(jnp.int32)]).astype(jnp.int32)
+        send = pack(idx, view_a, view_b, (nz, ny, nc, nx))
         got = exchange(send, "zl").reshape(nz * rows, cols_a + ny * lanes)
     with jax.named_scope("gather_y"):
         send = jnp.concatenate(
@@ -218,26 +295,25 @@
     with jax.named_scope("gather_core_x"):
         got_other = lax.ppermute(got, "c", SWAP)
         half = images // nc
-        parts = exchange(jnp.broadcast_to(got[None, :, cols_a:], (nc * nx, half, lanes)), ("c", "x"))
-        parts = parts.reshape(nc, nc, nx // nc, half, lanes)
+        parts = got[:, cols_a:].reshape(half // rows, nc, rows // nc, lanes).transpose(1, 0, 2, 3)
+        parts = parts.reshape(nc, 1, half // nc, lanes)
+        parts = jnp.broadcast_to(parts, (nc, nx, half // nc, lanes)).reshape(nc * nx, half // nc, lanes)
+        parts = exchange(parts, ("c", "x")).reshape(nc, nx // 2, 2, half // nc, lanes)
     with jax.named_scope("standardize_a"):
-        idx = jnp.stack([ic, ix, iy * nc + ic, (feat == iz).astype(jnp.int32)]).astype(jnp.int32)
         norm_a, stat_a = standardize_a(idx, got, got_other, cols_a)
         norm_a, parts = lax.optimization_barrier((norm_a, parts))
         mean_a, inverse_a = stat_a[0], stat_a[1]
     with jax.named_scope("tile"):
-        correlation, part_b, send = tile(idx, norm_a, parts, (nz, ny, nc, nx))
-
-    with jax.named_scope("reduce_z"):
+        correlation, part_b, norm_b, tail = tile(idx, norm_a, parts, (nz, ny, nc, nx))
+
+    with jax.named_scope("sum_b_x_reduce_z"):
+        n_rows = images // nx
+        came = lax.ppermute(part_b[2 * n_rows :], "x", [(i, i ^ 3) for i in range(nx)])
+        send = gram_part(idx, norm_b, tail, (nz, ny, nc, nx))
         got = exchange(send, "zl")
-    with jax.named_scope("sum_b_x"):
-        n_rows = images // nx
-        pieces = [part_b[:n_rows]]
-        for k in range(1, nx):
-            perm = [(i, (i + k) % nx) for i in range(nx)]
-            pieces.append(lax.ppermute(part_b[k * n_rows : (k + 1) * n_rows], "x", perm))
-        sum_b = sum(p.astype(f32) for p in pieces).astype(bf16)
-        other = lax.ppermute(sum_b, "zh", SWAP)
+        sum_b = part_b[: 2 * n_rows].astype(f32) + came.astype(f32)
+        came = lax.ppermute(sum_b[n_rows:].astype(bf16), "x", [(i, i ^ 1) for i in range(nx)])
+        sum_b = (sum_b[:n_rows] + came.astype(f32)).astype(bf16)
     with jax.named_scope("reduce_yc"):
         take = rows // nx
         total = jnp.sum(got[:, :, :images].astype(f32), 0).reshape(n_yc, take * images // cols_b, cols_b)
@@ -246,6 +322,7 @@
         aux = jnp.stack([aux[0] + aux[1] + aux[2], aux[3] + aux[4] + aux[5], aux[6] + aux[7], aux[7]])
         right = jnp.concatenate([total, jnp.broadcast_to(aux[None], (n_yc, 4, cols_b))], 1)
         send = jnp.concatenate([jnp.broadcast_to(squares[None], (n_yc, 8, cols_b)), right], 2)
+        other = lax.ppermute(sum_b, "zh", SWAP)
         got = exchange(send, ("y", "c"))
         squares = jnp.sum(got[:, :, :cols_b], 0).reshape(cols_a)
         gram = jnp.sum(got[:, :4, cols_b:], 0)

time: 129 us -> 126 us (0.977)
  starting transfers between devices: 36.9 us -> 34 us
    ppermute x3 -> x2, waiting for transfers between devices: 5.4 us -> 8.59 us  [the longest x1 4.37 us: local(): lax.ppermute(part_b[2 * n_rows:], 'x', [(i, i ^ 3) for i in range(nx)])]
    ppermute x3 -> x2, starting transfers between devices: 8.51 us -> 5.62 us  [the longest x1 3.7 us: local(): lax.ppermute(part_b[2 * n_rows:], 'x', [(i, i ^ 3) for i in range(nx)])]
    all_to_all x4, waiting for transfers between devices: 15.2 us -> 12.5 us  [exchange(): lax.all_to_all(values, axis, split_axis=0, concat_axis=0, tiled=False)]
    pallas_call x1, Pallas kernels: 5.23 us -> 2.95 us  [tile(): pl.pallas_call(functools.partial(tile_kernel, nz, ny, nc, nx), out_shape=...]
    pallas_call x0 -> x2, Pallas kernels: none -> 2.26 us  [the longest x1 1.54 us: gram_part(): pl.pallas_call(functools.partial(gram_kernel, *sizes), out_shape=jax.Shap...]
    unnamed x7 -> x11, local copies, waits for them, and re-layouts: 2.25 us -> 3.95 us
  transfers between devices with their start and end apart: 9 -> 8, of which waited for: 6 -> 6; matrix products, arithmetic and copies ran while one was open for 2% -> 2% of each run, Pallas kernels for 1% -> 1%
where the time goes in v5:
time: 126 us; the launch traced here: 125 us
  blocking collectives  50 us (40%)
  starting transfers between devices  34 us (27%)
  waiting for transfers between devices  23.5 us (19%)
  Pallas kernels  7 us (6%)
  local copies, waits for them, and re-layouts  6.63 us (5%)
  other arithmetic  2.52 us (2%)
    all_to_all x2, blocking collectives, exchange(): lax.all_to_all(values, axis, split_axis=0, concat_axis=0, tiled=False)  50 us
    all_to_all x4, starting transfers between devices, exchange(): lax.all_to_all(values, axis, split_axis=0, concat_axis=0, tiled=False)  18.3 us
    all_to_all x4, waiting for transfers between devices, exchange(): lax.all_to_all(values, axis, split_axis=0, concat_axis=0, tiled=False)  12.5 us
    ppermute x1, starting transfers between devices, local(): other = lax.ppermute(sum_b, 'zh', SWAP)  8.22 us
    ppermute x1, waiting for transfers between devices, local(): lax.ppermute(part_b[2 * n_rows:], 'x', [(i, i ^ 3) for i in range(nx)])  4.37 us
    ppermute x1, waiting for transfers between devices, local(): lax.ppermute(sum_b[n_rows:].astype(bf16), 'x', [(i, i ^ 1) for i in range...  4.22 us
    unnamed x11, local copies, waits for them, and re-layouts  3.95 us
    ppermute x1, starting transfers between devices, local(): lax.ppermute(part_b[2 * n_rows:], 'x', [(i, i ^ 3) for i in range(nx)])  3.7 us
  transfers between devices with their start and end apart: 8, of which 6 were waited for; matrix products, arithmetic and copies ran while one was open for 2% of the time, Pallas kernels for 1%

profile of v5, /device:TPU:32, one launch (start us, length us, event | category | flops | bytes accessed | tf_op | source)
XLA Modules:
  0.0 125.1 jit_solution(7157909952026930527)
XLA Ops:
  0.6 0.1 pad_add_fusion.idx
  0.7 0.0 copy-start.2
  0.7 0.9 copy-done.2
  1.7 0.0 copy-start.3
  1.7 0.8 copy-done.3
  2.4 0.7 gather_z.1
  3.2 31.3 %all_to_all.30 = bf16[8,8,2560]{2,1,0:T(8,128)(2,1)S(1)} all-to-all(bf16[8,8,2560]{2,1,0:T(8,128)(2,1)S(1)} %gather_z.1), channel_id=1, replica_groups=mesh['zl'=8,'y'=4,'c'=2,'zh'=2,'x'=4] {'zl'}, dimensions={0} | all-to-all | bytes 655360 | tf_op jit(solution)/shard_map/gather_z/all_to_all | solution.py:21
  34.6 0.1 broadcast_in_dim.14
  34.7 0.1 pad_maximum_fusion
  34.8 18.6 %all_to_all.31 = bf16[4,64,2176]{2,1,0:T(8,128)(2,1)S(1)} all-to-all(bf16[4,64,2176]{2,1,0:T(8,128)(2,1)S(1)} %pad_maximum_fusion), channel_id=1, replica_groups=mesh['zl'=8,'y'=4,'c'=2,'zh'=2,'x'=4] {'y'}, dimensions={0} | all-to-all | bytes 2228224 | tf_op jit(solution)/shard_map/gather_y/all_to_all | solution.py:21
  53.4 1.9 %collective-permute-start = (bf16[256,2176]{1,0:T(8,128)(2,1)S(1)}, bf16[256,2176]{1,0:T(8,128)(2,1)S(1)}, u32[]{:S(2)}, u32[]{:S(2)}) collective-permute-start(bf16[256,2176]{1,0:T(8,128)(2,1)S(1)} %bitcast.43), channel_id=1, source_target_pairs={{0,8},{8,0},{1,9},{9,1},{2,10},{10,2},{3,11},{11,3},{4,12},{12,4},... | collective-permute-start | bytes 3342344 | tf_op jit(solution)/shard_map/gather_core_x/ppermute | solution.py:296
  55.4 0.7 broadcast_in_dim.16
  56.1 4.4 %all-to-all-start.2 = ((bf16[8,128,128]{2,1,0:T(8,128)(2,1)}), bf16[8,128,128]{2,1,0:T(8,128)(2,1)S(1)}, u32[]{:S(2)}, u32[]{:S(2)}) async-start(bf16[8,128,128]{2,1,0:T(8,128)(2,1)} %bitcast.10), calls=%async_computation.2 | async-start | bytes 524288 | tf_op jit(solution)/shard_map/gather_core_x/all_to_all | solution.py:21
  60.5 0.0 collective-permute-done.other_ref
  60.5 0.0 copy-start
  60.6 1.0 copy-done
  61.5 0.0 copy-start.1
  61.5 1.2 copy-done.1
  62.8 1.8 %standardize_a.1 = (bf16[512,2048]{1,0:T(8,128)(2,1)S(1)}, f32[8,2048]{1,0:T(8,128)S(1)}) custom-call(s32[4]{0:T(128)S(1)} %pad_add_fusion.idx, bf16[256,2176]{1,0:T(8,128)(2,1)S(1)} %bitcast.45, bf16[256,2176]{1,0:T(8,128)(2,1)S(1)} %copy-done.1), custom_call_target="tpu_custom_call" | custom-call | flops 10485760 | bytes 4194304 | tf_op jit(solution)/shard_map/standardize_a/pallas_call | solution.py:121
  64.6 2.9 %all-to-all-done.2 = bf16[8,128,128]{2,1,0:T(8,128)(2,1)S(1)} async-done(((bf16[8,128,128]{2,1,0:T(8,128)(2,1)}), bf16[8,128,128]{2,1,0:T(8,128)(2,1)S(1)}, u32[]{:S(2)}, u32[]{:S(2)}) %all-to-all-start.2) | async-done | bytes 262176 | tf_op jit(solution)/shard_map/gather_core_x/all_to_all | solution.py:21
  67.5 3.0 %tile.1 = (f32[2048,256]{1,0:T(8,128)}, bf16[512,256]{1,0:T(8,128)(2,1)S(1)}, bf16[512,256]{1,0:T(8,128)(2,1)S(1)}, f32[24,256]{1,0:T(8,128)S(1)}) custom-call(s32[4]{0:T(128)S(1)} %pad_add_fusion.idx, bf16[512,2048]{1,0:T(8,128)(2,1)S(1)} %get-tuple-element.14.a_ref, bf16[2,2,2,128,128]{4,3,2,1,0:T(8,128)(2,1)S(1)} %bitcast.46), custom_call_target="tpu_custom_call" | custom-call | flops 1610612736 | bytes 4194304 | tf_op jit(solution)/shard_map/tile/pallas_call | solution.py:211
  70.4 1.5 %sum_b_x_reduce_z.1 = bf16[8,16,768]{2,1,0:T(8,128)(2,1)} custom-call(s32[4]{0:T(128)S(1)} %pad_add_fusion.idx, bf16[512,256]{1,0:T(8,128)(2,1)S(1)} %get-tuple-element.18.norm_ref, f32[24,256]{1,0:T(8,128)S(1)} %get-tuple-element.19.tail), custom_call_target="tpu_custom_call" | custom-call | flops 536870912 | bytes 2097152 | tf_op jit(solution)/shard_map/sum_b_x_reduce_z/pallas_call | solution.py:257
  72.0 0.0 copy-start.4
  72.0 7.1 %all-to-all-start.3 = ((bf16[8,16,768]{2,1,0:T(8,128)(2,1)}), bf16[8,16,768]{2,1,0:T(8,128)(2,1)S(1)}, u32[]{:S(2)}, u32[]{:S(2)}) async-start(bf16[8,16,768]{2,1,0:T(8,128)(2,1)} %sum_b_x_reduce_z.1), calls=%async_computation.3 | async-start | bytes 393216 | tf_op jit(solution)/shard_map/sum_b_x_reduce_z/all_to_all | solution.py:21
  79.0 3.7 %collective-permute-start.1 = (bf16[256,256]{1,0:T(8,128)(2,1)S(1)}, bf16[256,256]{1,0:T(8,128)(2,1)S(1)}, u32[]{:S(2)}, u32[]{:S(2)}) collective-permute-start(bf16[256,256]{1,0:T(8,128)(2,1)S(1)} %slice.105), channel_id=1, source_target_pairs={{0,3},{1,2},{2,1},{3,0},{4,7},{5,6},{6,5},{7,4},{8,11},{9,10},{10,... | collective-permute-start | bytes 393224 | tf_op jit(solution)/shard_map/sum_b_x_reduce_z/ppermute | solution.py:311
  82.8 4.4 %collective-permute-done.1 = bf16[256,256]{1,0:T(8,128)(2,1)S(1)} collective-permute-done((bf16[256,256]{1,0:T(8,128)(2,1)S(1)}, bf16[256,256]{1,0:T(8,128)(2,1)S(1)}, u32[]{:S(2)}, u32[]{:S(2)}) %collective-permute-start.1) | collective-permute-done | bytes 131104 | tf_op jit(solution)/shard_map/sum_b_x_reduce_z/ppermute | solution.py:311
  87.2 1.9 %collective-permute-start.2 = (bf16[128,256]{1,0:T(8,128)(2,1)S(1)}, bf16[128,256]{1,0:T(8,128)(2,1)S(1)}, u32[]{:S(2)}, u32[]{:S(2)}) collective-permute-start(bf16[128,256]{1,0:T(8,128)(2,1)S(1)} %slice.192), channel_id=1, source_target_pairs={{0,1},{1,0},{2,3},{3,2},{4,5},{5,4},{6,7},{7,6},{8,9},{9,8},{10,11... | collective-permute-start | bytes 196616 | tf_op jit(solution)/shard_map/sum_b_x_reduce_z/ppermute | solution.py:315
  89.1 4.2 %collective-permute-done.2 = bf16[128,256]{1,0:T(8,128)(2,1)S(1)} collective-permute-done((bf16[128,256]{1,0:T(8,128)(2,1)S(1)}, bf16[128,256]{1,0:T(8,128)(2,1)S(1)}, u32[]{:S(2)}, u32[]{:S(2)}) %collective-permute-start.2) | collective-permute-done | bytes 65568 | tf_op jit(solution)/shard_map/sum_b_x_reduce_z/ppermute | solution.py:315
  93.4 8.2 %collective-permute-start.3 = (bf16[128,256]{1,0:T(8,128)(2,1)S(1)}, bf16[128,256]{1,0:T(8,128)(2,1)S(1)}, u32[]{:S(2)}, u32[]{:S(2)}) collective-permute-start(bf16[128,256]{1,0:T(8,128)(2,1)S(1)} %fusion), channel_id=1, source_target_pairs={{0,4},{4,0},{1,5},{5,1},{2,6},{6,2},{3,7},{7,3},{8,12},{12,8},{9,1... | collective-permute-start | bytes 196616 | tf_op jit(solution)/shard_map/reduce_yc/ppermute | solution.py:325
  101.6 0.0 all-to-all-done.3
  101.8 0.7 maximum_maximum_fusion
  102.4 3.4 %all-to-all-start.4 = ((f32[8,8,512]{2,1,0:T(8,128)}), f32[8,8,512]{2,1,0:T(8,128)S(1)}, u32[]{:S(2)}, u32[]{:S(2)}) async-start(f32[8,8,512]{2,1,0:T(8,128)} %maximum_maximum_fusion), calls=%async_computation.4 | async-start | bytes 262144 | tf_op jit(solution)/shard_map/reduce_yc/all_to_all | solution.py:21
  105.8 2.5 %collective-permute-done.3 = bf16[128,256]{1,0:T(8,128)(2,1)S(1)} collective-permute-done((bf16[128,256]{1,0:T(8,128)(2,1)S(1)}, bf16[128,256]{1,0:T(8,128)(2,1)S(1)}, u32[]{:S(2)}, u32[]{:S(2)}) %collective-permute-start.3) | collective-permute-done | bytes 65568 | tf_op jit(solution)/shard_map/reduce_yc/ppermute | solution.py:325
  108.3 3.6 %all-to-all-done.4 = f32[8,8,512]{2,1,0:T(8,128)S(1)} async-done(((f32[8,8,512]{2,1,0:T(8,128)}), f32[8,8,512]{2,1,0:T(8,128)S(1)}, u32[]{:S(2)}, u32[]{:S(2)}) %all-to-all-start.4) | async-done | bytes 131104 | tf_op jit(solution)/shard_map/reduce_yc/all_to_all | solution.py:21
  112.0 0.7 broadcast_in_dim.19
  112.7 3.5 %all-to-all-start.5 = ((bf16[4,136,256]{2,1,0:T(8,128)(2,1)}), bf16[4,136,256]{2,1,0:T(8,128)(2,1)S(1)}, u32[]{:S(2)}, u32[]{:S(2)}) async-start(bf16[4,136,256]{2,1,0:T(8,128)(2,1)} %broadcast_in_dim.19), calls=%async_computation.5 | async-start | bytes 557056 | tf_op jit(solution)/shard_map/gather_b_x/all_to_all | solution.py:21
  116.2 0.0 copy-done.4
  116.2 0.8 subtract_multiply_fusion
  117.0 6.0 %all-to-all-done.5 = bf16[4,136,256]{2,1,0:T(8,128)(2,1)S(1)} async-done(((bf16[4,136,256]{2,1,0:T(8,128)(2,1)}), bf16[4,136,256]{2,1,0:T(8,128)(2,1)S(1)}, u32[]{:S(2)}, u32[]{:S(2)}) %all-to-all-start.5) | async-done | bytes 278560 | tf_op jit(solution)/shard_map/gather_b_x/all_to_all | solution.py:21
  123.1 0.4 fusion.10
  123.6 0.9 copy.16
  124.4 0.6 fusion.2
  (37 shorter events, 0.5 us)
Async XLA Ops:
  0.7 1.0 copy-start.2
  1.7 0.8 copy-start.3
  53.4 7.1 %collective-permute-start = (bf16[256,2176]{1,0:T(8,128)(2,1)S(1)}, bf16[256,2176]{1,0:T(8,128)(2,1)S(1)}, u32[]{:S(2)}, u32[]{:S(2)}) collective-permute-start(bf16[256,2176]{1,0:T(8,128)(2,1)S(1)} %bitcast.43), channel_id=1, source_target_pairs={{0,8},{8,0},{1,9},{9,1},{2,10},{10,2},{3,11},{11,3},{4,12},{12,4},... | collective-permute-start | bytes 3342344 | tf_op jit(solution)/shard_map/gather_core_x/ppermute | solution.py:296
  56.1 11.3 %all-to-all-start.2 = ((bf16[8,128,128]{2,1,0:T(8,128)(2,1)}), bf16[8,128,128]{2,1,0:T(8,128)(2,1)S(1)}, u32[]{:S(2)}, u32[]{:S(2)}) async-start(bf16[8,128,128]{2,1,0:T(8,128)(2,1)} %bitcast.10), calls=%async_computation.2 | async-start | bytes 524288 | tf_op jit(solution)/shard_map/gather_core_x/all_to_all | solution.py:21
  60.5 1.0 copy-start
  61.5 1.2 copy-start.1
  72.0 44.2 %copy-start.4 = (bf16[8,2048]{1,0:T(8,128)(2,1)S(1)}, bf16[8,2048]{1,0:T(8,128)(2,1)}, u32[]{:S(2)}) copy-start(bf16[8,2048]{1,0:T(8,128)(2,1)} %a_hbm.1) | copy-start | bytes 98308
  72.0 29.6 %all-to-all-start.3 = ((bf16[8,16,768]{2,1,0:T(8,128)(2,1)}), bf16[8,16,768]{2,1,0:T(8,128)(2,1)S(1)}, u32[]{:S(2)}, u32[]{:S(2)}) async-start(bf16[8,16,768]{2,1,0:T(8,128)(2,1)} %sum_b_x_reduce_z.1), calls=%async_computation.3 | async-start | bytes 393216 | tf_op jit(solution)/shard_map/sum_b_x_reduce_z/all_to_all | solution.py:21
  79.0 8.1 %collective-permute-start.1 = (bf16[256,256]{1,0:T(8,128)(2,1)S(1)}, bf16[256,256]{1,0:T(8,128)(2,1)S(1)}, u32[]{:S(2)}, u32[]{:S(2)}) collective-permute-start(bf16[256,256]{1,0:T(8,128)(2,1)S(1)} %slice.105), channel_id=1, source_target_pairs={{0,3},{1,2},{2,1},{3,0},{4,7},{5,6},{6,5},{7,4},{8,11},{9,10},{10,... | collective-permute-start | bytes 393224 | tf_op jit(solution)/shard_map/sum_b_x_reduce_z/ppermute | solution.py:311
  87.2 6.2 %collective-permute-start.2 = (bf16[128,256]{1,0:T(8,128)(2,1)S(1)}, bf16[128,256]{1,0:T(8,128)(2,1)S(1)}, u32[]{:S(2)}, u32[]{:S(2)}) collective-permute-start(bf16[128,256]{1,0:T(8,128)(2,1)S(1)} %slice.192), channel_id=1, source_target_pairs={{0,1},{1,0},{2,3},{3,2},{4,5},{5,4},{6,7},{7,6},{8,9},{9,8},{10,11... | collective-permute-start | bytes 196616 | tf_op jit(solution)/shard_map/sum_b_x_reduce_z/ppermute | solution.py:315
  93.4 14.9 %collective-permute-start.3 = (bf16[128,256]{1,0:T(8,128)(2,1)S(1)}, bf16[128,256]{1,0:T(8,128)(2,1)S(1)}, u32[]{:S(2)}, u32[]{:S(2)}) collective-permute-start(bf16[128,256]{1,0:T(8,128)(2,1)S(1)} %fusion), channel_id=1, source_target_pairs={{0,4},{4,0},{1,5},{5,1},{2,6},{6,2},{3,7},{7,3},{8,12},{12,8},{9,1... | collective-permute-start | bytes 196616 | tf_op jit(solution)/shard_map/reduce_yc/ppermute | solution.py:325
  102.4 9.4 %all-to-all-start.4 = ((f32[8,8,512]{2,1,0:T(8,128)}), f32[8,8,512]{2,1,0:T(8,128)S(1)}, u32[]{:S(2)}, u32[]{:S(2)}) async-start(f32[8,8,512]{2,1,0:T(8,128)} %maximum_maximum_fusion), calls=%async_computation.4 | async-start | bytes 262144 | tf_op jit(solution)/shard_map/reduce_yc/all_to_all | solution.py:21
  112.7 10.4 %all-to-all-start.5 = ((bf16[4,136,256]{2,1,0:T(8,128)(2,1)}), bf16[4,136,256]{2,1,0:T(8,128)(2,1)S(1)}, u32[]{:S(2)}, u32[]{:S(2)}) async-start(bf16[4,136,256]{2,1,0:T(8,128)(2,1)} %broadcast_in_dim.19), calls=%async_computation.5 | async-start | bytes 557056 | tf_op jit(solution)/shard_map/gather_b_x/all_to_all | solution.py:21

commit v6 on v5

--- a/solution.py
+++ b/solution.py
@@ -321,9 +321,10 @@
         aux = lax.dynamic_index_in_dim(got[:, 8:, images:], feat, 0, False).astype(f32)
         aux = jnp.stack([aux[0] + aux[1] + aux[2], aux[3] + aux[4] + aux[5], aux[6] + aux[7], aux[7]])
         right = jnp.concatenate([total, jnp.broadcast_to(aux[None], (n_yc, 4, cols_b))], 1)
-        send = jnp.concatenate([jnp.broadcast_to(squares[None], (n_yc, 8, cols_b)), right], 2)
+        left = jnp.broadcast_to(squares[None], (n_yc, 8, cols_b))
+        send = jnp.concatenate([left, right, jnp.zeros((n_yc, 8, 2 * cols_b), f32)], 2)
         other = lax.ppermute(sum_b, "zh", SWAP)
-        got = exchange(send, ("y", "c"))
+        got = exchange(send, ("y", "c"))[:, :, : 2 * cols_b]
         squares = jnp.sum(got[:, :, :cols_b], 0).reshape(cols_a)
         gram = jnp.sum(got[:, :4, cols_b:], 0)
         mean_f, inverse_f, diag_f = (got[:, 4 + k, cols_b:].reshape(cols_a) for k in range(3))

time: 126 us -> 123 us (0.976)
  waiting for transfers between devices: 23.5 us -> 20.4 us
    ppermute x1, waiting for transfers between devices: 4.37 us -> 0.01 us  [local(): lax.ppermute(part_b[2 * n_rows:], 'x', [(i, i ^ 3) for i in range(nx)])]
    all_to_all x4, waiting for transfers between devices: 12.5 us -> 13.7 us  [exchange(): lax.all_to_all(values, axis, split_axis=0, concat_axis=0, tiled=False)]
  transfers between devices with their start and end apart: 8 -> 8, of which waited for: 6 -> 5; matrix products, arithmetic and copies ran while one was open for 2% -> 2% of each run, Pallas kernels for 1% -> 3%
where the time goes in v6:
time: 123 us; the launch traced here: 122 us
  blocking collectives  50 us (41%)
  starting transfers between devices  34.1 us (28%)
  waiting for transfers between devices  20.4 us (17%)
  Pallas kernels  7 us (6%)
  local copies, waits for them, and re-layouts  6.64 us (5%)
  other arithmetic  2.58 us (2%)
    all_to_all x2, blocking collectives, exchange(): lax.all_to_all(values, axis, split_axis=0, concat_axis=0, tiled=False)  50 us
    all_to_all x4, starting transfers between devices, exchange(): lax.all_to_all(values, axis, split_axis=0, concat_axis=0, tiled=False)  18.3 us
    all_to_all x4, waiting for transfers between devices, exchange(): lax.all_to_all(values, axis, split_axis=0, concat_axis=0, tiled=False)  13.7 us
    ppermute x1, starting transfers between devices, local(): other = lax.ppermute(sum_b, 'zh', SWAP)  8.22 us
    ppermute x1, waiting for transfers between devices, local(): lax.ppermute(sum_b[n_rows:].astype(bf16), 'x', [(i, i ^ 1) for i in range...  4.21 us
    unnamed x11, local copies, waits for them, and re-layouts  3.95 us
    ppermute x1, starting transfers between devices, local(): lax.ppermute(part_b[2 * n_rows:], 'x', [(i, i ^ 3) for i in range(nx)])  3.7 us
    pallas_call x1, Pallas kernels, tile(): pl.pallas_call(functools.partial(tile_kernel, nz, ny, nc, nx), out_shape=...  2.95 us
  transfers between devices with their start and end apart: 8, of which 5 were waited for; matrix products, arithmetic and copies ran while one was open for 2% of the time, Pallas kernels for 3%

profile of v6, /device:TPU:32, one launch (start us, length us, event | category | flops | bytes accessed | tf_op | source)
XLA Modules:
  0.0 122.1 jit_solution(10631540793548731825)
XLA Ops:
  0.6 0.1 pad_add_fusion.idx
  0.7 0.0 copy-start.2
  0.7 0.9 copy-done.2
  1.7 0.0 copy-start.3
  1.7 0.8 copy-done.3
  2.4 0.7 gather_z.1
  3.2 31.3 %all_to_all.30 = bf16[8,8,2560]{2,1,0:T(8,128)(2,1)S(1)} all-to-all(bf16[8,8,2560]{2,1,0:T(8,128)(2,1)S(1)} %gather_z.1), channel_id=1, replica_groups=mesh['zl'=8,'y'=4,'c'=2,'zh'=2,'x'=4] {'zl'}, dimensions={0} | all-to-all | bytes 655360 | tf_op jit(solution)/shard_map/gather_z/all_to_all | solution.py:21
  34.6 0.1 broadcast_in_dim.16
  34.7 0.1 pad_maximum_fusion
  34.8 18.6 %all_to_all.31 = bf16[4,64,2176]{2,1,0:T(8,128)(2,1)S(1)} all-to-all(bf16[4,64,2176]{2,1,0:T(8,128)(2,1)S(1)} %pad_maximum_fusion), channel_id=1, replica_groups=mesh['zl'=8,'y'=4,'c'=2,'zh'=2,'x'=4] {'y'}, dimensions={0} | all-to-all | bytes 2228224 | tf_op jit(solution)/shard_map/gather_y/all_to_all | solution.py:21
  53.4 1.9 %collective-permute-start = (bf16[256,2176]{1,0:T(8,128)(2,1)S(1)}, bf16[256,2176]{1,0:T(8,128)(2,1)S(1)}, u32[]{:S(2)}, u32[]{:S(2)}) collective-permute-start(bf16[256,2176]{1,0:T(8,128)(2,1)S(1)} %bitcast.43), channel_id=1, source_target_pairs={{0,8},{8,0},{1,9},{9,1},{2,10},{10,2},{3,11},{11,3},{4,12},{12,4},... | collective-permute-start | bytes 3342344 | tf_op jit(solution)/shard_map/gather_core_x/ppermute | solution.py:296
  55.4 0.7 broadcast_in_dim.18
  56.1 4.4 %all-to-all-start.2 = ((bf16[8,128,128]{2,1,0:T(8,128)(2,1)}), bf16[8,128,128]{2,1,0:T(8,128)(2,1)S(1)}, u32[]{:S(2)}, u32[]{:S(2)}) async-start(bf16[8,128,128]{2,1,0:T(8,128)(2,1)} %bitcast.10), calls=%async_computation.2 | async-start | bytes 524288 | tf_op jit(solution)/shard_map/gather_core_x/all_to_all | solution.py:21
  60.5 0.0 collective-permute-done.other_ref
  60.5 0.0 copy-start
  60.6 1.0 copy-done
  61.5 0.0 copy-start.1
  61.5 1.2 %copy-done.1 = bf16[256,2176]{1,0:T(8,128)(2,1)S(1)} copy-done((bf16[256,2176]{1,0:T(8,128)(2,1)S(1)}, bf16[256,2176]{1,0:T(8,128)(2,1)}, u32[]{:S(2)}) %copy-start.1) | copy-done | bytes 1114136
  62.8 1.8 %standardize_a.1 = (bf16[512,2048]{1,0:T(8,128)(2,1)S(1)}, f32[8,2048]{1,0:T(8,128)S(1)}) custom-call(s32[4]{0:T(128)S(1)} %pad_add_fusion.idx, bf16[256,2176]{1,0:T(8,128)(2,1)S(1)} %bitcast.45, bf16[256,2176]{1,0:T(8,128)(2,1)S(1)} %copy-done.1), custom_call_target="tpu_custom_call" | custom-call | flops 10485760 | bytes 4194304 | tf_op jit(solution)/shard_map/standardize_a/pallas_call | solution.py:121
  64.6 2.9 %all-to-all-done.2 = bf16[8,128,128]{2,1,0:T(8,128)(2,1)S(1)} async-done(((bf16[8,128,128]{2,1,0:T(8,128)(2,1)}), bf16[8,128,128]{2,1,0:T(8,128)(2,1)S(1)}, u32[]{:S(2)}, u32[]{:S(2)}) %all-to-all-start.2) | async-done | bytes 262176 | tf_op jit(solution)/shard_map/gather_core_x/all_to_all | solution.py:21
  67.5 2.9 %tile.1 = (f32[2048,256]{1,0:T(8,128)}, bf16[512,256]{1,0:T(8,128)(2,1)S(1)}, bf16[512,256]{1,0:T(8,128)(2,1)S(1)}, f32[24,256]{1,0:T(8,128)S(1)}) custom-call(s32[4]{0:T(128)S(1)} %pad_add_fusion.idx, bf16[512,2048]{1,0:T(8,128)(2,1)S(1)} %get-tuple-element.14.a_ref, bf16[2,2,2,128,128]{4,3,2,1,0:T(8,128)(2,1)S(1)} %bitcast.46), custom_call_target="tpu_custom_call" | custom-call | flops 1610612736 | bytes 4194304 | tf_op jit(solution)/shard_map/tile/pallas_call | solution.py:211
  70.4 3.7 %collective-permute-start.1 = (bf16[256,256]{1,0:T(8,128)(2,1)S(1)}, bf16[256,256]{1,0:T(8,128)(2,1)S(1)}, u32[]{:S(2)}, u32[]{:S(2)}) collective-permute-start(bf16[256,256]{1,0:T(8,128)(2,1)S(1)} %slice.111), channel_id=1, source_target_pairs={{0,3},{1,2},{2,1},{3,0},{4,7},{5,6},{6,5},{7,4},{8,11},{9,10},{10,... | collective-permute-start | bytes 393224 | tf_op jit(solution)/shard_map/sum_b_x_reduce_z/ppermute | solution.py:311
  74.2 1.5 %sum_b_x_reduce_z.1 = bf16[8,16,768]{2,1,0:T(8,128)(2,1)} custom-call(s32[4]{0:T(128)S(1)} %pad_add_fusion.idx, bf16[512,256]{1,0:T(8,128)(2,1)S(1)} %get-tuple-element.18.norm_ref, f32[24,256]{1,0:T(8,128)S(1)} %get-tuple-element.19.tail), custom_call_target="tpu_custom_call" | custom-call | flops 536870912 | bytes 2097152 | tf_op jit(solution)/shard_map/sum_b_x_reduce_z/pallas_call | solution.py:257
  75.7 0.0 copy-start.4
  75.7 7.1 %all-to-all-start.3 = ((bf16[8,16,768]{2,1,0:T(8,128)(2,1)}), bf16[8,16,768]{2,1,0:T(8,128)(2,1)S(1)}, u32[]{:S(2)}, u32[]{:S(2)}) async-start(bf16[8,16,768]{2,1,0:T(8,128)(2,1)} %sum_b_x_reduce_z.1), calls=%async_computation.3 | async-start | bytes 393216 | tf_op jit(solution)/shard_map/sum_b_x_reduce_z/all_to_all | solution.py:21
  82.8 0.0 collective-permute-done.1
  82.8 1.9 %collective-permute-start.2 = (bf16[128,256]{1,0:T(8,128)(2,1)S(1)}, bf16[128,256]{1,0:T(8,128)(2,1)S(1)}, u32[]{:S(2)}, u32[]{:S(2)}) collective-permute-start(bf16[128,256]{1,0:T(8,128)(2,1)S(1)} %slice.198), channel_id=1, source_target_pairs={{0,1},{1,0},{2,3},{3,2},{4,5},{5,4},{6,7},{7,6},{8,9},{9,8},{10,11... | collective-permute-start | bytes 196616 | tf_op jit(solution)/shard_map/sum_b_x_reduce_z/ppermute | solution.py:315
  84.8 4.2 %collective-permute-done.2 = bf16[128,256]{1,0:T(8,128)(2,1)S(1)} collective-permute-done((bf16[128,256]{1,0:T(8,128)(2,1)S(1)}, bf16[128,256]{1,0:T(8,128)(2,1)S(1)}, u32[]{:S(2)}, u32[]{:S(2)}) %collective-permute-start.2) | collective-permute-done | bytes 65568 | tf_op jit(solution)/shard_map/sum_b_x_reduce_z/ppermute | solution.py:315
  89.0 8.2 %collective-permute-start.3 = (bf16[128,256]{1,0:T(8,128)(2,1)S(1)}, bf16[128,256]{1,0:T(8,128)(2,1)S(1)}, u32[]{:S(2)}, u32[]{:S(2)}) collective-permute-start(bf16[128,256]{1,0:T(8,128)(2,1)S(1)} %fusion), channel_id=1, source_target_pairs={{0,4},{4,0},{1,5},{5,1},{2,6},{6,2},{3,7},{7,3},{8,12},{12,8},{9,1... | collective-permute-start | bytes 196616 | tf_op jit(solution)/shard_map/reduce_yc/ppermute | solution.py:326
  97.2 0.0 all-to-all-done.3
  97.4 0.7 maximum_maximum_fusion
  98.2 3.4 %all-to-all-start.4 = ((f32[8,8,1024]{2,1,0:T(8,128)}), f32[8,8,1024]{2,1,0:T(8,128)S(1)}, u32[]{:S(2)}, u32[]{:S(2)}) async-start(f32[8,8,1024]{2,1,0:T(8,128)} %maximum_maximum_fusion), calls=%async_computation.4 | async-start | bytes 524288 | tf_op jit(solution)/shard_map/reduce_yc/all_to_all | solution.py:21
  101.6 2.4 %collective-permute-done.3 = bf16[128,256]{1,0:T(8,128)(2,1)S(1)} collective-permute-done((bf16[128,256]{1,0:T(8,128)(2,1)S(1)}, bf16[128,256]{1,0:T(8,128)(2,1)S(1)}, u32[]{:S(2)}, u32[]{:S(2)}) %collective-permute-start.3) | collective-permute-done | bytes 65568 | tf_op jit(solution)/shard_map/reduce_yc/ppermute | solution.py:326
  104.0 5.0 %all-to-all-done.4 = f32[8,8,1024]{2,1,0:T(8,128)S(1)} async-done(((f32[8,8,1024]{2,1,0:T(8,128)}), f32[8,8,1024]{2,1,0:T(8,128)S(1)}, u32[]{:S(2)}, u32[]{:S(2)}) %all-to-all-start.4) | async-done | bytes 262176 | tf_op jit(solution)/shard_map/reduce_yc/all_to_all | solution.py:21
  109.1 0.7 broadcast_in_dim.22
  109.8 3.5 %all-to-all-start.5 = ((bf16[4,136,256]{2,1,0:T(8,128)(2,1)}), bf16[4,136,256]{2,1,0:T(8,128)(2,1)S(1)}, u32[]{:S(2)}, u32[]{:S(2)}) async-start(bf16[4,136,256]{2,1,0:T(8,128)(2,1)} %broadcast_in_dim.22), calls=%async_computation.5 | async-start | bytes 557056 | tf_op jit(solution)/shard_map/gather_b_x/all_to_all | solution.py:21
  113.3 0.0 copy-done.4
  113.4 0.8 subtract_multiply_fusion
  114.2 5.9 %all-to-all-done.5 = bf16[4,136,256]{2,1,0:T(8,128)(2,1)S(1)} async-done(((bf16[4,136,256]{2,1,0:T(8,128)(2,1)}), bf16[4,136,256]{2,1,0:T(8,128)(2,1)S(1)}, u32[]{:S(2)}, u32[]{:S(2)}) %all-to-all-start.5) | async-done | bytes 278560 | tf_op jit(solution)/shard_map/gather_b_x/all_to_all | solution.py:21
  120.1 0.4 fusion.10
  120.6 0.9 copy.16
  121.4 0.6 fusion.2
  (39 shorter events, 0.5 us)
Async XLA Ops:
  0.7 1.0 copy-start.2
  1.7 0.8 copy-start.3
  53.4 7.1 %collective-permute-start = (bf16[256,2176]{1,0:T(8,128)(2,1)S(1)}, bf16[256,2176]{1,0:T(8,128)(2,1)S(1)}, u32[]{:S(2)}, u32[]{:S(2)}) collective-permute-start(bf16[256,2176]{1,0:T(8,128)(2,1)S(1)} %bitcast.43), channel_id=1, source_target_pairs={{0,8},{8,0},{1,9},{9,1},{2,10},{10,2},{3,11},{11,3},{4,12},{12,4},... | collective-permute-start | bytes 3342344 | tf_op jit(solution)/shard_map/gather_core_x/ppermute | solution.py:296
  56.1 11.3 %all-to-all-start.2 = ((bf16[8,128,128]{2,1,0:T(8,128)(2,1)}), bf16[8,128,128]{2,1,0:T(8,128)(2,1)S(1)}, u32[]{:S(2)}, u32[]{:S(2)}) async-start(bf16[8,128,128]{2,1,0:T(8,128)(2,1)} %bitcast.10), calls=%async_computation.2 | async-start | bytes 524288 | tf_op jit(solution)/shard_map/gather_core_x/all_to_all | solution.py:21
  60.5 1.0 copy-start
  61.5 1.2 %copy-start.1 = (bf16[256,2176]{1,0:T(8,128)(2,1)S(1)}, bf16[256,2176]{1,0:T(8,128)(2,1)}, u32[]{:S(2)}) copy-start(bf16[256,2176]{1,0:T(8,128)(2,1)} %copy-done) | copy-start | bytes 3342340
  70.4 12.3 %collective-permute-start.1 = (bf16[256,256]{1,0:T(8,128)(2,1)S(1)}, bf16[256,256]{1,0:T(8,128)(2,1)S(1)}, u32[]{:S(2)}, u32[]{:S(2)}) collective-permute-start(bf16[256,256]{1,0:T(8,128)(2,1)S(1)} %slice.111), channel_id=1, source_target_pairs={{0,3},{1,2},{2,1},{3,0},{4,7},{5,6},{6,5},{7,4},{8,11},{9,10},{10,... | collective-permute-start | bytes 393224 | tf_op jit(solution)/shard_map/sum_b_x_reduce_z/ppermute | solution.py:311
  75.7 37.6 %copy-start.4 = (bf16[8,2048]{1,0:T(8,128)(2,1)S(1)}, bf16[8,2048]{1,0:T(8,128)(2,1)}, u32[]{:S(2)}) copy-start(bf16[8,2048]{1,0:T(8,128)(2,1)} %a_hbm.1) | copy-start | bytes 98308
  75.7 21.5 %all-to-all-start.3 = ((bf16[8,16,768]{2,1,0:T(8,128)(2,1)}), bf16[8,16,768]{2,1,0:T(8,128)(2,1)S(1)}, u32[]{:S(2)}, u32[]{:S(2)}) async-start(bf16[8,16,768]{2,1,0:T(8,128)(2,1)} %sum_b_x_reduce_z.1), calls=%async_computation.3 | async-start | bytes 393216 | tf_op jit(solution)/shard_map/sum_b_x_reduce_z/all_to_all | solution.py:21
  82.8 6.2 %collective-permute-start.2 = (bf16[128,256]{1,0:T(8,128)(2,1)S(1)}, bf16[128,256]{1,0:T(8,128)(2,1)S(1)}, u32[]{:S(2)}, u32[]{:S(2)}) collective-permute-start(bf16[128,256]{1,0:T(8,128)(2,1)S(1)} %slice.198), channel_id=1, source_target_pairs={{0,1},{1,0},{2,3},{3,2},{4,5},{5,4},{6,7},{7,6},{8,9},{9,8},{10,11... | collective-permute-start | bytes 196616 | tf_op jit(solution)/shard_map/sum_b_x_reduce_z/ppermute | solution.py:315
  89.0 15.0 %collective-permute-start.3 = (bf16[128,256]{1,0:T(8,128)(2,1)S(1)}, bf16[128,256]{1,0:T(8,128)(2,1)S(1)}, u32[]{:S(2)}, u32[]{:S(2)}) collective-permute-start(bf16[128,256]{1,0:T(8,128)(2,1)S(1)} %fusion), channel_id=1, source_target_pairs={{0,4},{4,0},{1,5},{5,1},{2,6},{6,2},{3,7},{7,3},{8,12},{12,8},{9,1... | collective-permute-start | bytes 196616 | tf_op jit(solution)/shard_map/reduce_yc/ppermute | solution.py:326
  98.2 10.9 %all-to-all-start.4 = ((f32[8,8,1024]{2,1,0:T(8,128)}), f32[8,8,1024]{2,1,0:T(8,128)S(1)}, u32[]{:S(2)}, u32[]{:S(2)}) async-start(f32[8,8,1024]{2,1,0:T(8,128)} %maximum_maximum_fusion), calls=%async_computation.4 | async-start | bytes 524288 | tf_op jit(solution)/shard_map/reduce_yc/all_to_all | solution.py:21
  109.8 10.2 %all-to-all-start.5 = ((bf16[4,136,256]{2,1,0:T(8,128)(2,1)}), bf16[4,136,256]{2,1,0:T(8,128)(2,1)S(1)}, u32[]{:S(2)}, u32[]{:S(2)}) async-start(bf16[4,136,256]{2,1,0:T(8,128)(2,1)} %broadcast_in_dim.22), calls=%async_computation.5 | async-start | bytes 557056 | tf_op jit(solution)/shard_map/gather_b_x/all_to_all | solution.py:21

commit v7 on v6

--- a/solution.py
+++ b/solution.py
@@ -264,6 +264,48 @@
             flops=8 * images * images * cols, bytes_accessed=16 * images * cols, transcendentals=0
         ),
     )(idx, norm_b, tail)
+
+
+def finish_kernel(nz, ny, nc, got_ref, norm_ref, shifted_ref, scale_ref, grad_a_ref, grad_b_ref, gram):
+    nx, rows_x, cols = got_ref.shape
+    images = norm_ref.shape[0]
+    rows = shifted_ref.shape[0]
+    n_rows = images // nx
+    wide = images // cols
+    take = rows // nx
+    for x in range(nx):
+        values = got_ref[x, n_rows:, :].astype(f32)
+        for part in range(2):
+            for t in range(take):
+                for w in range(wide):
+                    line = (part * take + t) * wide + w
+                    to = part * rows + x * take + t
+                    gram[to : to + 1, w * cols : (w + 1) * cols] = values[line : line + 1]
+    both = dot(gram[...].astype(bf16), norm_ref[...], ((1,), (0,)))
+    grad_a_ref[...] = (both[:rows] + both[rows:]) * scale_ref[...] + shifted_ref[...]
+    for x in range(nx):
+        values = got_ref[x, :n_rows, :].astype(f32)
+        for k in range(n_rows // rows):
+            block = x * (n_rows // rows) + k
+            c, y, z = block // (ny * nz), block // nz % ny, block % nz
+            to = ((z * ny + y) * nc + c) * rows
+            grad_b_ref[to : to + rows, :] = values[k * rows : (k + 1) * rows]
+
+
+def finish(got, norm_a, shifted, scale, sizes):
+    images, cols_a = norm_a.shape
+    rows, cols = shifted.shape[0], got.shape[2]
+    return pl.pallas_call(
+        functools.partial(finish_kernel, *sizes[:3]),
+        out_shape=(
+            jax.ShapeDtypeStruct((rows, cols_a), f32),
+            jax.ShapeDtypeStruct((images, cols), f32),
+        ),
+        in_specs=in_vmem(4),
+        out_specs=in_vmem(2),
+        scratch_shapes=[pltpu.VMEM((2 * rows, images), f32)],
+        compiler_params=pltpu.CompilerParams(vmem_limit_bytes=VMEM_LIMIT),
+    )(got, norm_a, shifted, scale)
 
 
 def local(view_a, view_b):
@@ -342,12 +384,8 @@
         own = jnp.concatenate([sum_b, upper, lower], 0)
         shifted, scale = lax.optimization_barrier((shifted, scale))
         got = exchange(jnp.broadcast_to(own[None], (nx,) + own.shape), "x")
-        grad_b = got[:, :n_rows].reshape(nc, ny, nz, rows, cols_b).transpose(2, 1, 0, 3, 4)
-        grad_b = grad_b.reshape(images, cols_b).astype(f32)
-        gram = got[:, n_rows:].reshape(nx, 2, take, images).transpose(1, 0, 2, 3).reshape(2 * rows, images)
-    with jax.named_scope("grad_a"):
-        both = dot(gram, norm_a, ((1,), (0,)))
-        grad_a = (both[:rows] + both[rows:]) * scale + shifted
+    with jax.named_scope("finish"):
+        grad_a, grad_b = finish(got, norm_a, shifted, scale, (nz, ny, nc, nx))
     return correlation, grad_a, grad_b
 
 

time: 123 us -> 122 us (level)
  no operation moved by 1% of the time
where the time goes in v7:
time: 122 us; the launch traced here: 121 us
  blocking collectives  50 us (41%)
  starting transfers between devices  34.1 us (28%)
  waiting for transfers between devices  20.3 us (17%)
  Pallas kernels  8.16 us (7%)
  local copies, waits for them, and re-layouts  5.71 us (5%)
  other arithmetic  1.91 us (2%)
    all_to_all x2, blocking collectives, exchange(): lax.all_to_all(values, axis, split_axis=0, concat_axis=0, tiled=False)  50 us
    all_to_all x4, starting transfers between devices, exchange(): lax.all_to_all(values, axis, split_axis=0, concat_axis=0, tiled=False)  18.3 us
    all_to_all x4, waiting for transfers between devices, exchange(): lax.all_to_all(values, axis, split_axis=0, concat_axis=0, tiled=False)  13.8 us
    ppermute x1, starting transfers between devices, local(): other = lax.ppermute(sum_b, 'zh', SWAP)  8.22 us
    ppermute x1, waiting for transfers between devices, local(): lax.ppermute(sum_b[n_rows:].astype(bf16), 'x', [(i, i ^ 1) for i in range...  4.21 us
    unnamed x11, local copies, waits for them, and re-layouts  3.95 us
    ppermute x1, starting transfers between devices, local(): lax.ppermute(part_b[2 * n_rows:], 'x', [(i, i ^ 3) for i in range(nx)])  3.7 us
    pallas_call x1, Pallas kernels, tile(): pl.pallas_call(functools.partial(tile_kernel, nz, ny, nc, nx), out_shape=...  2.95 us
  transfers between devices with their start and end apart: 8, of which 5 were waited for; matrix products, arithmetic and copies ran while one was open for 2% of the time, Pallas kernels for 3%

profile of v7, /device:TPU:32, one launch (start us, length us, event | category | flops | bytes accessed | tf_op | source)
XLA Modules:
  0.0 121.1 jit_solution(15025534177355112153)
XLA Ops:
  0.6 0.1 pad_add_fusion.idx
  0.7 0.0 copy-start.2
  0.7 0.9 copy-done.2
  1.7 0.0 copy-start.3
  1.7 0.8 copy-done.3
  2.4 0.7 gather_z.1
  3.2 31.3 %all_to_all.30 = bf16[8,8,2560]{2,1,0:T(8,128)(2,1)S(1)} all-to-all(bf16[8,8,2560]{2,1,0:T(8,128)(2,1)S(1)} %gather_z.1), channel_id=1, replica_groups=mesh['zl'=8,'y'=4,'c'=2,'zh'=2,'x'=4] {'zl'}, dimensions={0} | all-to-all | bytes 655360 | tf_op jit(solution)/shard_map/gather_z/all_to_all | solution.py:21
  34.6 0.1 broadcast_in_dim.16
  34.7 0.1 pad_maximum_fusion
  34.8 18.6 %all_to_all.31 = bf16[4,64,2176]{2,1,0:T(8,128)(2,1)S(1)} all-to-all(bf16[4,64,2176]{2,1,0:T(8,128)(2,1)S(1)} %pad_maximum_fusion), channel_id=1, replica_groups=mesh['zl'=8,'y'=4,'c'=2,'zh'=2,'x'=4] {'y'}, dimensions={0} | all-to-all | bytes 2228224 | tf_op jit(solution)/shard_map/gather_y/all_to_all | solution.py:21
  53.4 1.9 %collective-permute-start = (bf16[256,2176]{1,0:T(8,128)(2,1)S(1)}, bf16[256,2176]{1,0:T(8,128)(2,1)S(1)}, u32[]{:S(2)}, u32[]{:S(2)}) collective-permute-start(bf16[256,2176]{1,0:T(8,128)(2,1)S(1)} %bitcast.33), channel_id=1, source_target_pairs={{0,8},{8,0},{1,9},{9,1},{2,10},{10,2},{3,11},{11,3},{4,12},{12,4},... | collective-permute-start | bytes 3342344 | tf_op jit(solution)/shard_map/gather_core_x/ppermute | solution.py:338
  55.4 0.7 broadcast_in_dim.18
  56.1 4.4 %all-to-all-start.2 = ((bf16[8,128,128]{2,1,0:T(8,128)(2,1)}), bf16[8,128,128]{2,1,0:T(8,128)(2,1)S(1)}, u32[]{:S(2)}, u32[]{:S(2)}) async-start(bf16[8,128,128]{2,1,0:T(8,128)(2,1)} %bitcast.10), calls=%async_computation.2 | async-start | bytes 524288 | tf_op jit(solution)/shard_map/gather_core_x/all_to_all | solution.py:21
  60.5 0.0 collective-permute-done.other_ref
  60.5 0.0 copy-start
  60.6 1.0 copy-done
  61.5 0.0 copy-start.1
  61.5 1.2 %copy-done.1 = bf16[256,2176]{1,0:T(8,128)(2,1)S(1)} copy-done((bf16[256,2176]{1,0:T(8,128)(2,1)S(1)}, bf16[256,2176]{1,0:T(8,128)(2,1)}, u32[]{:S(2)}) %copy-start.1) | copy-done | bytes 1114136
  62.8 1.8 %standardize_a.1 = (bf16[512,2048]{1,0:T(8,128)(2,1)S(1)}, f32[8,2048]{1,0:T(8,128)S(1)}) custom-call(s32[4]{0:T(128)S(1)} %pad_add_fusion.idx, bf16[256,2176]{1,0:T(8,128)(2,1)S(1)} %bitcast.35, bf16[256,2176]{1,0:T(8,128)(2,1)S(1)} %copy-done.1), custom_call_target="tpu_custom_call" | custom-call | flops 10485760 | bytes 4194304 | tf_op jit(solution)/shard_map/standardize_a/pallas_call | solution.py:121
  64.6 2.9 %all-to-all-done.2 = bf16[8,128,128]{2,1,0:T(8,128)(2,1)S(1)} async-done(((bf16[8,128,128]{2,1,0:T(8,128)(2,1)}), bf16[8,128,128]{2,1,0:T(8,128)(2,1)S(1)}, u32[]{:S(2)}, u32[]{:S(2)}) %all-to-all-start.2) | async-done | bytes 262176 | tf_op jit(solution)/shard_map/gather_core_x/all_to_all | solution.py:21
  67.5 2.9 %tile.1 = (f32[2048,256]{1,0:T(8,128)}, bf16[512,256]{1,0:T(8,128)(2,1)S(1)}, bf16[512,256]{1,0:T(8,128)(2,1)S(1)}, f32[24,256]{1,0:T(8,128)S(1)}) custom-call(s32[4]{0:T(128)S(1)} %pad_add_fusion.idx, bf16[512,2048]{1,0:T(8,128)(2,1)S(1)} %get-tuple-element.16.a_ref.norm_ref, bf16[2,2,2,128,128]{4,3,2,1,0:T(8,128)(2,1)S(1)} %bitcast.36), custom_call_target="tpu_custom_call" | custom-call | flops 1610612736 | bytes 4194304 | tf_op jit(solution)/shard_map/tile/pallas_call | solution.py:211
  70.4 3.7 %collective-permute-start.1 = (bf16[256,256]{1,0:T(8,128)(2,1)S(1)}, bf16[256,256]{1,0:T(8,128)(2,1)S(1)}, u32[]{:S(2)}, u32[]{:S(2)}) collective-permute-start(bf16[256,256]{1,0:T(8,128)(2,1)S(1)} %slice.99), channel_id=1, source_target_pairs={{0,3},{1,2},{2,1},{3,0},{4,7},{5,6},{6,5},{7,4},{8,11},{9,10},{10,... | collective-permute-start | bytes 393224 | tf_op jit(solution)/shard_map/sum_b_x_reduce_z/ppermute | solution.py:353
  74.2 1.5 %sum_b_x_reduce_z.1 = bf16[8,16,768]{2,1,0:T(8,128)(2,1)} custom-call(s32[4]{0:T(128)S(1)} %pad_add_fusion.idx, bf16[512,256]{1,0:T(8,128)(2,1)S(1)} %get-tuple-element.20.norm_ref, f32[24,256]{1,0:T(8,128)S(1)} %get-tuple-element.21.tail), custom_call_target="tpu_custom_call" | custom-call | flops 536870912 | bytes 2097152 | tf_op jit(solution)/shard_map/sum_b_x_reduce_z/pallas_call | solution.py:257
  75.7 6.9 %all-to-all-start.3 = ((bf16[8,16,768]{2,1,0:T(8,128)(2,1)}), bf16[8,16,768]{2,1,0:T(8,128)(2,1)S(1)}, u32[]{:S(2)}, u32[]{:S(2)}) async-start(bf16[8,16,768]{2,1,0:T(8,128)(2,1)} %sum_b_x_reduce_z.1), calls=%async_computation.3 | async-start | bytes 393216 | tf_op jit(solution)/shard_map/sum_b_x_reduce_z/all_to_all | solution.py:21
  82.6 0.0 collective-permute-done.1
  82.7 1.9 %collective-permute-start.2 = (bf16[128,256]{1,0:T(8,128)(2,1)S(1)}, bf16[128,256]{1,0:T(8,128)(2,1)S(1)}, u32[]{:S(2)}, u32[]{:S(2)}) collective-permute-start(bf16[128,256]{1,0:T(8,128)(2,1)S(1)} %slice.172), channel_id=1, source_target_pairs={{0,1},{1,0},{2,3},{3,2},{4,5},{5,4},{6,7},{7,6},{8,9},{9,8},{10,11... | collective-permute-start | bytes 196616 | tf_op jit(solution)/shard_map/sum_b_x_reduce_z/ppermute | solution.py:357
  84.7 4.2 %collective-permute-done.2 = bf16[128,256]{1,0:T(8,128)(2,1)S(1)} collective-permute-done((bf16[128,256]{1,0:T(8,128)(2,1)S(1)}, bf16[128,256]{1,0:T(8,128)(2,1)S(1)}, u32[]{:S(2)}, u32[]{:S(2)}) %collective-permute-start.2) | collective-permute-done | bytes 65568 | tf_op jit(solution)/shard_map/sum_b_x_reduce_z/ppermute | solution.py:357
  88.9 8.2 %collective-permute-start.3 = (bf16[128,256]{1,0:T(8,128)(2,1)S(1)}, bf16[128,256]{1,0:T(8,128)(2,1)S(1)}, u32[]{:S(2)}, u32[]{:S(2)}) collective-permute-start(bf16[128,256]{1,0:T(8,128)(2,1)S(1)} %fusion), channel_id=1, source_target_pairs={{0,4},{4,0},{1,5},{5,1},{2,6},{6,2},{3,7},{7,3},{8,12},{12,8},{9,1... | collective-permute-start | bytes 196616 | tf_op jit(solution)/shard_map/reduce_yc/ppermute | solution.py:368
  97.1 0.0 all-to-all-done.3
  97.3 0.7 maximum_maximum_fusion
  98.0 0.0 copy-start.4
  98.0 3.5 %all-to-all-start.4 = ((f32[8,8,1024]{2,1,0:T(8,128)}), f32[8,8,1024]{2,1,0:T(8,128)S(1)}, u32[]{:S(2)}, u32[]{:S(2)}) async-start(f32[8,8,1024]{2,1,0:T(8,128)} %maximum_maximum_fusion), calls=%async_computation.4 | async-start | bytes 524288 | tf_op jit(solution)/shard_map/reduce_yc/all_to_all | solution.py:21
  101.6 2.3 %collective-permute-done.3 = bf16[128,256]{1,0:T(8,128)(2,1)S(1)} collective-permute-done((bf16[128,256]{1,0:T(8,128)(2,1)S(1)}, bf16[128,256]{1,0:T(8,128)(2,1)S(1)}, u32[]{:S(2)}, u32[]{:S(2)}) %collective-permute-start.3) | collective-permute-done | bytes 65568 | tf_op jit(solution)/shard_map/reduce_yc/ppermute | solution.py:368
  103.9 5.2 %all-to-all-done.4 = f32[8,8,1024]{2,1,0:T(8,128)S(1)} async-done(((f32[8,8,1024]{2,1,0:T(8,128)}), f32[8,8,1024]{2,1,0:T(8,128)S(1)}, u32[]{:S(2)}, u32[]{:S(2)}) %all-to-all-start.4) | async-done | bytes 262176 | tf_op jit(solution)/shard_map/reduce_yc/all_to_all | solution.py:21
  109.1 0.7 broadcast_in_dim.22
  109.8 3.5 %all-to-all-start.5 = ((bf16[4,136,256]{2,1,0:T(8,128)(2,1)}), bf16[4,136,256]{2,1,0:T(8,128)(2,1)S(1)}, u32[]{:S(2)}, u32[]{:S(2)}) async-start(bf16[4,136,256]{2,1,0:T(8,128)(2,1)} %broadcast_in_dim.22), calls=%async_computation.5 | async-start | bytes 557056 | tf_op jit(solution)/shard_map/gather_b_x/all_to_all | solution.py:21
  113.3 0.0 copy-done.4
  113.4 0.8 subtract_multiply_fusion.shifted_ref
  114.2 5.8 %all-to-all-done.5.got_ref = bf16[4,136,256]{2,1,0:T(8,128)(2,1)S(1)} async-done(((bf16[4,136,256]{2,1,0:T(8,128)(2,1)}), bf16[4,136,256]{2,1,0:T(8,128)(2,1)S(1)}, u32[]{:S(2)}, u32[]{:S(2)}) %all-to-all-start.5) | async-done | bytes 278560 | tf_op jit(solution)/shard_map/gather_b_x/all_to_all | solution.py:21
  120.0 1.2 finish.1
  (33 shorter events, 0.4 us)
Async XLA Ops:
  0.7 1.0 copy-start.2
  1.7 0.8 copy-start.3
  53.4 7.1 %collective-permute-start = (bf16[256,2176]{1,0:T(8,128)(2,1)S(1)}, bf16[256,2176]{1,0:T(8,128)(2,1)S(1)}, u32[]{:S(2)}, u32[]{:S(2)}) collective-permute-start(bf16[256,2176]{1,0:T(8,128)(2,1)S(1)} %bitcast.33), channel_id=1, source_target_pairs={{0,8},{8,0},{1,9},{9,1},{2,10},{10,2},{3,11},{11,3},{4,12},{12,4},... | collective-permute-start | bytes 3342344 | tf_op jit(solution)/shard_map/gather_core_x/ppermute | solution.py:338
  56.1 11.3 %all-to-all-start.2 = ((bf16[8,128,128]{2,1,0:T(8,128)(2,1)}), bf16[8,128,128]{2,1,0:T(8,128)(2,1)S(1)}, u32[]{:S(2)}, u32[]{:S(2)}) async-start(bf16[8,128,128]{2,1,0:T(8,128)(2,1)} %bitcast.10), calls=%async_computation.2 | async-start | bytes 524288 | tf_op jit(solution)/shard_map/gather_core_x/all_to_all | solution.py:21
  60.5 1.0 copy-start
  61.5 1.2 %copy-start.1 = (bf16[256,2176]{1,0:T(8,128)(2,1)S(1)}, bf16[256,2176]{1,0:T(8,128)(2,1)}, u32[]{:S(2)}) copy-start(bf16[256,2176]{1,0:T(8,128)(2,1)} %copy-done) | copy-start | bytes 3342340
  70.4 12.2 %collective-permute-start.1 = (bf16[256,256]{1,0:T(8,128)(2,1)S(1)}, bf16[256,256]{1,0:T(8,128)(2,1)S(1)}, u32[]{:S(2)}, u32[]{:S(2)}) collective-permute-start(bf16[256,256]{1,0:T(8,128)(2,1)S(1)} %slice.99), channel_id=1, source_target_pairs={{0,3},{1,2},{2,1},{3,0},{4,7},{5,6},{6,5},{7,4},{8,11},{9,10},{10,... | collective-permute-start | bytes 393224 | tf_op jit(solution)/shard_map/sum_b_x_reduce_z/ppermute | solution.py:353
  75.7 21.4 %all-to-all-start.3 = ((bf16[8,16,768]{2,1,0:T(8,128)(2,1)}), bf16[8,16,768]{2,1,0:T(8,128)(2,1)S(1)}, u32[]{:S(2)}, u32[]{:S(2)}) async-start(bf16[8,16,768]{2,1,0:T(8,128)(2,1)} %sum_b_x_reduce_z.1), calls=%async_computation.3 | async-start | bytes 393216 | tf_op jit(solution)/shard_map/sum_b_x_reduce_z/all_to_all | solution.py:21
  82.7 6.2 %collective-permute-start.2 = (bf16[128,256]{1,0:T(8,128)(2,1)S(1)}, bf16[128,256]{1,0:T(8,128)(2,1)S(1)}, u32[]{:S(2)}, u32[]{:S(2)}) collective-permute-start(bf16[128,256]{1,0:T(8,128)(2,1)S(1)} %slice.172), channel_id=1, source_target_pairs={{0,1},{1,0},{2,3},{3,2},{4,5},{5,4},{6,7},{7,6},{8,9},{9,8},{10,11... | collective-permute-start | bytes 196616 | tf_op jit(solution)/shard_map/sum_b_x_reduce_z/ppermute | solution.py:357
  88.9 15.0 %collective-permute-start.3 = (bf16[128,256]{1,0:T(8,128)(2,1)S(1)}, bf16[128,256]{1,0:T(8,128)(2,1)S(1)}, u32[]{:S(2)}, u32[]{:S(2)}) collective-permute-start(bf16[128,256]{1,0:T(8,128)(2,1)S(1)} %fusion), channel_id=1, source_target_pairs={{0,4},{4,0},{1,5},{5,1},{2,6},{6,2},{3,7},{7,3},{8,12},{12,8},{9,1... | collective-permute-start | bytes 196616 | tf_op jit(solution)/shard_map/reduce_yc/ppermute | solution.py:368
  98.0 15.3 %copy-start.4 = (bf16[8,2048]{1,0:T(8,128)(2,1)S(1)}, bf16[8,2048]{1,0:T(8,128)(2,1)}, u32[]{:S(2)}) copy-start(bf16[8,2048]{1,0:T(8,128)(2,1)} %a_hbm.1) | copy-start | bytes 98308
  98.0 11.0 %all-to-all-start.4 = ((f32[8,8,1024]{2,1,0:T(8,128)}), f32[8,8,1024]{2,1,0:T(8,128)S(1)}, u32[]{:S(2)}, u32[]{:S(2)}) async-start(f32[8,8,1024]{2,1,0:T(8,128)} %maximum_maximum_fusion), calls=%async_computation.4 | async-start | bytes 524288 | tf_op jit(solution)/shard_map/reduce_yc/all_to_all | solution.py:21
  109.8 10.2 %all-to-all-start.5 = ((bf16[4,136,256]{2,1,0:T(8,128)(2,1)}), bf16[4,136,256]{2,1,0:T(8,128)(2,1)S(1)}, u32[]{:S(2)}, u32[]{:S(2)}) async-start(bf16[4,136,256]{2,1,0:T(8,128)(2,1)} %broadcast_in_dim.22), calls=%async_computation.5 | async-start | bytes 557056 | tf_op jit(solution)/shard_map/gather_b_x/all_to_all | solution.py:21

commit v8 on v7

--- a/solution.py
+++ b/solution.py
@@ -45,52 +45,6 @@
 def statistics(total, square, images):
     mean = total / images
     return mean, lax.rsqrt(square / images - mean * mean + epsilon)
-
-
-def pack_kernel(ny, nc, idx, a_hbm, b_hbm, send_ref, a_ref, b_ref, sems):
-    nz, rows, _ = send_ref.shape
-    cols_a = a_ref.shape[1]
-    copy_a = pltpu.make_async_copy(a_hbm, a_ref, sems.at[0])
-    copy_b = pltpu.make_async_copy(b_hbm, b_ref, sems.at[1])
-    copy_b.start()
-    copy_a.start()
-    copy_a.wait()
-    values = a_ref[...]
-    for z in range(nz):
-        send_ref[z, :, :cols_a] = values
-    copy_b.wait()
-    lanes = (send_ref.shape[2] - cols_a) // ny
-    upper = idx[1] < 2
-    column = (idx[1] & 1) * lanes
-    keep = (lax.broadcasted_iota(jnp.int32, (rows, lanes), 0) < rows // 2) == upper
-    for z in range(nz):
-        for y in range(ny):
-            pair = []
-            for c in range(nc):
-                first = ((z * ny + y) * nc + c) * 2 * lanes
-                first = pl.multiple_of(first + column, lanes)
-                pair.append(b_ref[:, pl.ds(first, lanes)].astype(f32))
-            moved = pltpu.roll(jnp.where(upper, pair[1], pair[0]), rows // 2, 0)
-            mixed = jnp.where(keep, jnp.where(upper, pair[0], pair[1]), moved)
-            send_ref[z, :, cols_a + y * lanes : cols_a + (y + 1) * lanes] = mixed.astype(bf16)
-
-
-def pack(idx, view_a, view_b, sizes):
-    nz, ny, nc, nx = sizes
-    rows, cols_a = view_a.shape
-    lanes = view_b.shape[1] // (nz * ny * nc * 2)
-    return pl.pallas_call(
-        functools.partial(pack_kernel, ny, nc),
-        out_shape=jax.ShapeDtypeStruct((nz, rows, cols_a + ny * lanes), bf16),
-        in_specs=[pl.BlockSpec(memory_space=pltpu.SMEM)] + [pl.BlockSpec(memory_space=pl.ANY)] * 2,
-        out_specs=in_vmem(1)[0],
-        scratch_shapes=[
-            pltpu.VMEM(view_a.shape, bf16),
-            pltpu.VMEM(view_b.shape, bf16),
-            pltpu.SemaphoreType.DMA((2,)),
-        ],
-        compiler_params=pltpu.CompilerParams(vmem_limit_bytes=VMEM_LIMIT),
-    )(idx, view_a, view_b)
 
 
 def standardize_kernel(idx, own_ref, other_ref, norm_ref, stat_ref):
@@ -323,7 +277,11 @@
     with jax.named_scope("gather_z"):
         lanes = cols_b // 2
         idx = jnp.stack([ic, ix, iy * nc + ic, (feat == iz).astype(jnp.int32)]).astype(jnp.int32)
-        send = pack(idx, view_a, view_b, (nz, ny, nc, nx))
+        quarter = view_b.reshape(2, rows // 2, nz * ny, nc, 2, lanes)
+        quarter = lax.dynamic_index_in_dim(quarter, ix // 2, 0, False)
+        quarter = lax.dynamic_index_in_dim(quarter, ix % 2, 3, False)
+        quarter = quarter.transpose(2, 0, 1, 3).reshape(rows, nz, ny * lanes).transpose(1, 0, 2)
+        send = jnp.concatenate([jnp.broadcast_to(view_a[None], (nz, rows, cols_a)), quarter], 2)
         got = exchange(send, "zl").reshape(nz * rows, cols_a + ny * lanes)
     with jax.named_scope("gather_y"):
         send = jnp.concatenate(
@@ -381,7 +339,7 @@
     with jax.named_scope("gather_b_x"):
         sum_b = (sum_b.astype(f32) + other.astype(f32)).astype(bf16)
         upper, lower = terms(gram, 2)
-        own = jnp.concatenate([sum_b, upper, lower], 0)
+        own = jnp.concatenate([sum_b, upper, lower, jnp.zeros((8, cols_b), bf16)], 0)
         shifted, scale = lax.optimization_barrier((shifted, scale))
         got = exchange(jnp.broadcast_to(own[None], (nx,) + own.shape), "x")
     with jax.named_scope("finish"):

time: 122 us -> 121 us (level)
    unnamed x11 -> x9, local copies, waits for them, and re-layouts: 3.95 us -> 2.26 us
where the time goes in v8:
time: 121 us; the launch traced here: 120 us
  blocking collectives  50 us (41%)
  starting transfers between devices  34.1 us (28%)
  waiting for transfers between devices  20.4 us (17%)
  Pallas kernels  7.44 us (6%)
  local copies, waits for them, and re-layouts  5.48 us (5%)
  other arithmetic  2 us (2%)
    all_to_all x2, blocking collectives, exchange(): lax.all_to_all(values, axis, split_axis=0, concat_axis=0, tiled=False)  50 us
    all_to_all x4, starting transfers between devices, exchange(): lax.all_to_all(values, axis, split_axis=0, concat_axis=0, tiled=False)  18.3 us
    all_to_all x4, waiting for transfers between devices, exchange(): lax.all_to_all(values, axis, split_axis=0, concat_axis=0, tiled=False)  13.9 us
    ppermute x1, starting transfers between devices, local(): other = lax.ppermute(sum_b, 'zh', SWAP)  8.22 us
    ppermute x1, waiting for transfers between devices, local(): lax.ppermute(sum_b[n_rows:].astype(bf16), 'x', [(i, i ^ 1) for i in range...  4.21 us
    ppermute x1, starting transfers between devices, local(): lax.ppermute(part_b[2 * n_rows:], 'x', [(i, i ^ 3) for i in range(nx)])  3.7 us
    pallas_call x1, Pallas kernels, tile(): pl.pallas_call(functools.partial(tile_kernel, nz, ny, nc, nx), out_shape=...  2.95 us
  transfers between devices with their start and end apart: 8, of which 5 were waited for; matrix products, arithmetic and copies ran while one was open for 2% of the time, Pallas kernels for 3%

profile of v8, /device:TPU:32, one launch (start us, length us, event | category | flops | bytes accessed | tf_op | source)
XLA Modules:
  0.0 120.5 jit_solution(17606261826579705324)
XLA Ops:
  0.6 0.0 copy-start.2
  0.7 1.1 reshape.86
  1.8 0.1 constant_dynamic-slice_fusion
  2.0 0.1 reshape.87
  2.1 0.0 copy-done.2
  2.1 31.3 %all_to_all.30 = bf16[8,8,2560]{2,1,0:T(8,128)(2,1)S(1)} all-to-all(bf16[8,8,2560]{2,1,0:T(8,128)(2,1)S(1)} %pad_maximum_fusion.1), channel_id=1, replica_groups=mesh['zl'=8,'y'=4,'c'=2,'zh'=2,'x'=4] {'zl'}, dimensions={0} | all-to-all | bytes 655360 | tf_op jit(solution)/shard_map/gather_z/all_to_all | solution.py:21
  33.5 0.1 broadcast_in_dim.21
  33.7 0.1 pad_maximum_fusion
  33.8 18.6 %all_to_all.31 = bf16[4,64,2176]{2,1,0:T(8,128)(2,1)S(1)} all-to-all(bf16[4,64,2176]{2,1,0:T(8,128)(2,1)S(1)} %pad_maximum_fusion), channel_id=1, replica_groups=mesh['zl'=8,'y'=4,'c'=2,'zh'=2,'x'=4] {'y'}, dimensions={0} | all-to-all | bytes 2228224 | tf_op jit(solution)/shard_map/gather_y/all_to_all | solution.py:21
  52.4 1.9 %collective-permute-start = (bf16[256,2176]{1,0:T(8,128)(2,1)S(1)}, bf16[256,2176]{1,0:T(8,128)(2,1)S(1)}, u32[]{:S(2)}, u32[]{:S(2)}) collective-permute-start(bf16[256,2176]{1,0:T(8,128)(2,1)S(1)} %bitcast.41), channel_id=1, source_target_pairs={{0,8},{8,0},{1,9},{9,1},{2,10},{10,2},{3,11},{11,3},{4,12},{12,4},... | collective-permute-start | bytes 3342344 | tf_op jit(solution)/shard_map/gather_core_x/ppermute | solution.py:296
  54.4 0.7 broadcast_in_dim.23
  55.1 4.4 %all-to-all-start.2 = ((bf16[8,128,128]{2,1,0:T(8,128)(2,1)}), bf16[8,128,128]{2,1,0:T(8,128)(2,1)S(1)}, u32[]{:S(2)}, u32[]{:S(2)}) async-start(bf16[8,128,128]{2,1,0:T(8,128)(2,1)} %bitcast.14), calls=%async_computation.2 | async-start | bytes 524288 | tf_op jit(solution)/shard_map/gather_core_x/all_to_all | solution.py:21
  59.5 0.1 pad_add_fusion.idx
  59.6 0.0 collective-permute-done.other_ref
  59.6 0.0 copy-start
  59.6 1.0 copy-done
  60.6 0.0 copy-start.1
  60.6 1.2 %copy-done.1 = bf16[256,2176]{1,0:T(8,128)(2,1)S(1)} copy-done((bf16[256,2176]{1,0:T(8,128)(2,1)S(1)}, bf16[256,2176]{1,0:T(8,128)(2,1)}, u32[]{:S(2)}) %copy-start.1) | copy-done | bytes 1114136
  61.8 1.8 %standardize_a.1 = (bf16[512,2048]{1,0:T(8,128)(2,1)S(1)}, f32[8,2048]{1,0:T(8,128)S(1)}) custom-call(s32[4]{0:T(128)S(1)} %pad_add_fusion.idx, bf16[256,2176]{1,0:T(8,128)(2,1)S(1)} %bitcast.43, bf16[256,2176]{1,0:T(8,128)(2,1)S(1)} %copy-done.1), custom_call_target="tpu_custom_call" | custom-call | flops 10485760 | bytes 4194304 | tf_op jit(solution)/shard_map/standardize_a/pallas_call | solution.py:75
  63.7 2.8 %all-to-all-done.2 = bf16[8,128,128]{2,1,0:T(8,128)(2,1)S(1)} async-done(((bf16[8,128,128]{2,1,0:T(8,128)(2,1)}), bf16[8,128,128]{2,1,0:T(8,128)(2,1)S(1)}, u32[]{:S(2)}, u32[]{:S(2)}) %all-to-all-start.2) | async-done | bytes 262176 | tf_op jit(solution)/shard_map/gather_core_x/all_to_all | solution.py:21
  66.4 2.9 %tile.1 = (f32[2048,256]{1,0:T(8,128)}, bf16[512,256]{1,0:T(8,128)(2,1)S(1)}, bf16[512,256]{1,0:T(8,128)(2,1)S(1)}, f32[24,256]{1,0:T(8,128)S(1)}) custom-call(s32[4]{0:T(128)S(1)} %pad_add_fusion.idx, bf16[512,2048]{1,0:T(8,128)(2,1)S(1)} %get-tuple-element.16.a_ref.norm_ref, bf16[2,2,2,128,128]{4,3,2,1,0:T(8,128)(2,1)S(1)} %bitcast.44), custom_call_target="tpu_custom_call" | custom-call | flops 1610612736 | bytes 4194304 | tf_op jit(solution)/shard_map/tile/pallas_call | solution.py:165
  69.4 3.7 %collective-permute-start.1 = (bf16[256,256]{1,0:T(8,128)(2,1)S(1)}, bf16[256,256]{1,0:T(8,128)(2,1)S(1)}, u32[]{:S(2)}, u32[]{:S(2)}) collective-permute-start(bf16[256,256]{1,0:T(8,128)(2,1)S(1)} %slice.99), channel_id=1, source_target_pairs={{0,3},{1,2},{2,1},{3,0},{4,7},{5,6},{6,5},{7,4},{8,11},{9,10},{10,... | collective-permute-start | bytes 393224 | tf_op jit(solution)/shard_map/sum_b_x_reduce_z/ppermute | solution.py:311
  73.2 0.1 pad.3.clone
  73.2 1.5 %sum_b_x_reduce_z.1 = bf16[8,16,768]{2,1,0:T(8,128)(2,1)} custom-call(s32[4]{0:T(128)S(1)} %pad_add_fusion.idx, bf16[512,256]{1,0:T(8,128)(2,1)S(1)} %get-tuple-element.20.norm_ref, f32[24,256]{1,0:T(8,128)S(1)} %get-tuple-element.21.tail), custom_call_target="tpu_custom_call" | custom-call | flops 536870912 | bytes 2097152 | tf_op jit(solution)/shard_map/sum_b_x_reduce_z/pallas_call | solution.py:211
  74.8 6.9 %all-to-all-start.3 = ((bf16[8,16,768]{2,1,0:T(8,128)(2,1)}), bf16[8,16,768]{2,1,0:T(8,128)(2,1)S(1)}, u32[]{:S(2)}, u32[]{:S(2)}) async-start(bf16[8,16,768]{2,1,0:T(8,128)(2,1)} %sum_b_x_reduce_z.1), calls=%async_computation.3 | async-start | bytes 393216 | tf_op jit(solution)/shard_map/sum_b_x_reduce_z/all_to_all | solution.py:21
  81.7 0.0 collective-permute-done.1
  81.8 1.9 %collective-permute-start.2 = (bf16[128,256]{1,0:T(8,128)(2,1)S(1)}, bf16[128,256]{1,0:T(8,128)(2,1)S(1)}, u32[]{:S(2)}, u32[]{:S(2)}) collective-permute-start(bf16[128,256]{1,0:T(8,128)(2,1)S(1)} %slice.172), channel_id=1, source_target_pairs={{0,1},{1,0},{2,3},{3,2},{4,5},{5,4},{6,7},{7,6},{8,9},{9,8},{10,11... | collective-permute-start | bytes 196616 | tf_op jit(solution)/shard_map/sum_b_x_reduce_z/ppermute | solution.py:315
  83.7 4.2 %collective-permute-done.2 = bf16[128,256]{1,0:T(8,128)(2,1)S(1)} collective-permute-done((bf16[128,256]{1,0:T(8,128)(2,1)S(1)}, bf16[128,256]{1,0:T(8,128)(2,1)S(1)}, u32[]{:S(2)}, u32[]{:S(2)}) %collective-permute-start.2) | collective-permute-done | bytes 65568 | tf_op jit(solution)/shard_map/sum_b_x_reduce_z/ppermute | solution.py:315
  88.0 8.2 %collective-permute-start.3 = (bf16[128,256]{1,0:T(8,128)(2,1)S(1)}, bf16[128,256]{1,0:T(8,128)(2,1)S(1)}, u32[]{:S(2)}, u32[]{:S(2)}) collective-permute-start(bf16[128,256]{1,0:T(8,128)(2,1)S(1)} %fusion), channel_id=1, source_target_pairs={{0,4},{4,0},{1,5},{5,1},{2,6},{6,2},{3,7},{7,3},{8,12},{12,8},{9,1... | collective-permute-start | bytes 196616 | tf_op jit(solution)/shard_map/reduce_yc/ppermute | solution.py:326
  96.2 0.0 all-to-all-done.3
  96.4 0.7 maximum_maximum_fusion
  97.1 0.0 copy-start.3
  97.1 3.5 %all-to-all-start.4 = ((f32[8,8,1024]{2,1,0:T(8,128)}), f32[8,8,1024]{2,1,0:T(8,128)S(1)}, u32[]{:S(2)}, u32[]{:S(2)}) async-start(f32[8,8,1024]{2,1,0:T(8,128)} %maximum_maximum_fusion), calls=%async_computation.4 | async-start | bytes 524288 | tf_op jit(solution)/shard_map/reduce_yc/all_to_all | solution.py:21
  100.7 2.3 %collective-permute-done.3 = bf16[128,256]{1,0:T(8,128)(2,1)S(1)} collective-permute-done((bf16[128,256]{1,0:T(8,128)(2,1)S(1)}, bf16[128,256]{1,0:T(8,128)(2,1)S(1)}, u32[]{:S(2)}, u32[]{:S(2)}) %collective-permute-start.3) | collective-permute-done | bytes 65568 | tf_op jit(solution)/shard_map/reduce_yc/ppermute | solution.py:326
  103.0 5.2 %all-to-all-done.4 = f32[8,8,1024]{2,1,0:T(8,128)S(1)} async-done(((f32[8,8,1024]{2,1,0:T(8,128)}), f32[8,8,1024]{2,1,0:T(8,128)S(1)}, u32[]{:S(2)}, u32[]{:S(2)}) %all-to-all-start.4) | async-done | bytes 262176 | tf_op jit(solution)/shard_map/reduce_yc/all_to_all | solution.py:21
  108.1 0.1 maximum_maximum_fusion.1
  108.2 0.7 broadcast_in_dim.56
  109.0 3.5 %all-to-all-start.5 = ((bf16[4,144,256]{2,1,0:T(8,128)(2,1)}), bf16[4,144,256]{2,1,0:T(8,128)(2,1)S(1)}, u32[]{:S(2)}, u32[]{:S(2)}) async-start(bf16[4,144,256]{2,1,0:T(8,128)(2,1)} %broadcast_in_dim.56), calls=%async_computation.5 | async-start | bytes 589824 | tf_op jit(solution)/shard_map/gather_b_x/all_to_all | solution.py:21
  112.5 0.0 copy-done.3
  112.5 0.8 subtract_multiply_fusion.shifted_ref
  113.3 6.0 %all-to-all-done.5.got_ref = bf16[4,144,256]{2,1,0:T(8,128)(2,1)S(1)} async-done(((bf16[4,144,256]{2,1,0:T(8,128)(2,1)}), bf16[4,144,256]{2,1,0:T(8,128)(2,1)S(1)}, u32[]{:S(2)}, u32[]{:S(2)}) %all-to-all-start.5) | async-done | bytes 294944 | tf_op jit(solution)/shard_map/gather_b_x/all_to_all | solution.py:21
  119.3 1.2 finish.1
  (37 shorter events, 0.5 us)
Async XLA Ops:
  0.6 1.4 %copy-start.2 = (bf16[8,2048]{1,0:T(8,128)(2,1)S(1)}, bf16[8,2048]{1,0:T(8,128)(2,1)}, u32[]{:S(2)}) copy-start(bf16[8,2048]{1,0:T(8,128)(2,1)} %param.2) | copy-start | bytes 98308
  52.4 7.2 %collective-permute-start = (bf16[256,2176]{1,0:T(8,128)(2,1)S(1)}, bf16[256,2176]{1,0:T(8,128)(2,1)S(1)}, u32[]{:S(2)}, u32[]{:S(2)}) collective-permute-start(bf16[256,2176]{1,0:T(8,128)(2,1)S(1)} %bitcast.41), channel_id=1, source_target_pairs={{0,8},{8,0},{1,9},{9,1},{2,10},{10,2},{3,11},{11,3},{4,12},{12,4},... | collective-permute-start | bytes 3342344 | tf_op jit(solution)/shard_map/gather_core_x/ppermute | solution.py:296
  55.1 11.3 %all-to-all-start.2 = ((bf16[8,128,128]{2,1,0:T(8,128)(2,1)}), bf16[8,128,128]{2,1,0:T(8,128)(2,1)S(1)}, u32[]{:S(2)}, u32[]{:S(2)}) async-start(bf16[8,128,128]{2,1,0:T(8,128)(2,1)} %bitcast.14), calls=%async_computation.2 | async-start | bytes 524288 | tf_op jit(solution)/shard_map/gather_core_x/all_to_all | solution.py:21
  59.6 1.0 copy-start
  60.6 1.2 %copy-start.1 = (bf16[256,2176]{1,0:T(8,128)(2,1)S(1)}, bf16[256,2176]{1,0:T(8,128)(2,1)}, u32[]{:S(2)}) copy-start(bf16[256,2176]{1,0:T(8,128)(2,1)} %copy-done) | copy-start | bytes 3342340
  69.4 12.3 %collective-permute-start.1 = (bf16[256,256]{1,0:T(8,128)(2,1)S(1)}, bf16[256,256]{1,0:T(8,128)(2,1)S(1)}, u32[]{:S(2)}, u32[]{:S(2)}) collective-permute-start(bf16[256,256]{1,0:T(8,128)(2,1)S(1)} %slice.99), channel_id=1, source_target_pairs={{0,3},{1,2},{2,1},{3,0},{4,7},{5,6},{6,5},{7,4},{8,11},{9,10},{10,... | collective-permute-start | bytes 393224 | tf_op jit(solution)/shard_map/sum_b_x_reduce_z/ppermute | solution.py:311
  74.8 21.4 %all-to-all-start.3 = ((bf16[8,16,768]{2,1,0:T(8,128)(2,1)}), bf16[8,16,768]{2,1,0:T(8,128)(2,1)S(1)}, u32[]{:S(2)}, u32[]{:S(2)}) async-start(bf16[8,16,768]{2,1,0:T(8,128)(2,1)} %sum_b_x_reduce_z.1), calls=%async_computation.3 | async-start | bytes 393216 | tf_op jit(solution)/shard_map/sum_b_x_reduce_z/all_to_all | solution.py:21
  81.8 6.2 %collective-permute-start.2 = (bf16[128,256]{1,0:T(8,128)(2,1)S(1)}, bf16[128,256]{1,0:T(8,128)(2,1)S(1)}, u32[]{:S(2)}, u32[]{:S(2)}) collective-permute-start(bf16[128,256]{1,0:T(8,128)(2,1)S(1)} %slice.172), channel_id=1, source_target_pairs={{0,1},{1,0},{2,3},{3,2},{4,5},{5,4},{6,7},{7,6},{8,9},{9,8},{10,11... | collective-permute-start | bytes 196616 | tf_op jit(solution)/shard_map/sum_b_x_reduce_z/ppermute | solution.py:315
  88.0 15.0 %collective-permute-start.3 = (bf16[128,256]{1,0:T(8,128)(2,1)S(1)}, bf16[128,256]{1,0:T(8,128)(2,1)S(1)}, u32[]{:S(2)}, u32[]{:S(2)}) collective-permute-start(bf16[128,256]{1,0:T(8,128)(2,1)S(1)} %fusion), channel_id=1, source_target_pairs={{0,4},{4,0},{1,5},{5,1},{2,6},{6,2},{3,7},{7,3},{8,12},{12,8},{9,1... | collective-permute-start | bytes 196616 | tf_op jit(solution)/shard_map/reduce_yc/ppermute | solution.py:326
  97.1 15.4 %copy-start.3 = (bf16[8,2048]{1,0:T(8,128)(2,1)S(1)}, bf16[8,2048]{1,0:T(8,128)(2,1)}, u32[]{:S(2)}) copy-start(bf16[8,2048]{1,0:T(8,128)(2,1)} %param.2) | copy-start | bytes 98308
  97.1 11.0 %all-to-all-start.4 = ((f32[8,8,1024]{2,1,0:T(8,128)}), f32[8,8,1024]{2,1,0:T(8,128)S(1)}, u32[]{:S(2)}, u32[]{:S(2)}) async-start(f32[8,8,1024]{2,1,0:T(8,128)} %maximum_maximum_fusion), calls=%async_computation.4 | async-start | bytes 524288 | tf_op jit(solution)/shard_map/reduce_yc/all_to_all | solution.py:21
  109.0 10.4 %all-to-all-start.5 = ((bf16[4,144,256]{2,1,0:T(8,128)(2,1)}), bf16[4,144,256]{2,1,0:T(8,128)(2,1)S(1)}, u32[]{:S(2)}, u32[]{:S(2)}) async-start(bf16[4,144,256]{2,1,0:T(8,128)(2,1)} %broadcast_in_dim.56), calls=%async_computation.5 | async-start | bytes 589824 | tf_op jit(solution)/shard_map/gather_b_x/all_to_all | solution.py:21

commit v9 on v8

--- a/solution.py
+++ b/solution.py
@@ -116,7 +116,6 @@
         tail[16:17, span] = inverse
 
     norm = norm_ref[...]
-    ones = jnp.ones((8, cols), bf16)
     copies = []
     for j in range(cols_a // cols):
         span = slice(j * cols, (j + 1) * cols)
@@ -125,9 +124,7 @@
         place = pl.ds(j * cols, cols)
         copies.append(pltpu.make_async_copy(corr_ref.at[place], out_ref.at[place], sems.at[j]))
         copies[-1].start()
-        upper, lower = (v.astype(bf16) for v in kernel_terms(corr * corr, 2))
-        sums = dot(ones, upper, ((1,), (1,))) + dot(ones, lower, ((1,), (1,)))
-        tail[j : j + 1, :] = sums[0:1]
+        tail[j : j + 1, :] = jnp.sum(corr * corr, 1)[None, :]
         high[span, :] = corr.astype(bf16)
 
     place = pl.multiple_of(idx[2] * cols, cols)

time: 121 us -> 121 us (level)
  no operation moved by 1% of the time
where the time goes in v9:
time: 121 us; the launch traced here: 120 us
  blocking collectives  50 us (41%)
  starting transfers between devices  34.1 us (28%)
  waiting for transfers between devices  20.4 us (17%)
  Pallas kernels  7 us (6%)
  local copies, waits for them, and re-layouts  5.48 us (5%)
  other arithmetic  2 us (2%)
    all_to_all x2, blocking collectives, exchange(): lax.all_to_all(values, axis, split_axis=0, concat_axis=0, tiled=False)  50 us
    all_to_all x4, starting transfers between devices, exchange(): lax.all_to_all(values, axis, split_axis=0, concat_axis=0, tiled=False)  18.3 us
    all_to_all x4, waiting for transfers between devices, exchange(): lax.all_to_all(values, axis, split_axis=0, concat_axis=0, tiled=False)  13.9 us
    ppermute x1, starting transfers between devices, local(): other = lax.ppermute(sum_b, 'zh', SWAP)  8.21 us
    ppermute x1, waiting for transfers between devices, local(): lax.ppermute(sum_b[n_rows:].astype(bf16), 'x', [(i, i ^ 1) for i in range...  4.21 us
    ppermute x1, starting transfers between devices, local(): lax.ppermute(part_b[2 * n_rows:], 'x', [(i, i ^ 3) for i in range(nx)])  3.69 us
    pallas_call x1, Pallas kernels, tile(): pl.pallas_call(functools.partial(tile_kernel, nz, ny, nc, nx), out_shape=...  2.5 us
  transfers between devices with their start and end apart: 8, of which 5 were waited for; matrix products, arithmetic and copies ran while one was open for 2% of the time, Pallas kernels for 3%

profile of v9, /device:TPU:32, one launch (start us, length us, event | category | flops | bytes accessed | tf_op | source)
XLA Modules:
  0.0 120.0 jit_solution(4003054866165226927)
XLA Ops:
  0.6 0.0 copy-start.2
  0.7 1.1 reshape.86
  1.8 0.1 constant_dynamic-slice_fusion
  2.0 0.1 reshape.87
  2.1 0.0 copy-done.2
  2.1 31.3 %all_to_all.30 = bf16[8,8,2560]{2,1,0:T(8,128)(2,1)S(1)} all-to-all(bf16[8,8,2560]{2,1,0:T(8,128)(2,1)S(1)} %pad_maximum_fusion.1), channel_id=1, replica_groups=mesh['zl'=8,'y'=4,'c'=2,'zh'=2,'x'=4] {'zl'}, dimensions={0} | all-to-all | bytes 655360 | tf_op jit(solution)/shard_map/gather_z/all_to_all | solution.py:21
  33.5 0.1 broadcast_in_dim.21
  33.7 0.1 pad_maximum_fusion
  33.8 18.6 %all_to_all.31 = bf16[4,64,2176]{2,1,0:T(8,128)(2,1)S(1)} all-to-all(bf16[4,64,2176]{2,1,0:T(8,128)(2,1)S(1)} %pad_maximum_fusion), channel_id=1, replica_groups=mesh['zl'=8,'y'=4,'c'=2,'zh'=2,'x'=4] {'y'}, dimensions={0} | all-to-all | bytes 2228224 | tf_op jit(solution)/shard_map/gather_y/all_to_all | solution.py:21
  52.4 1.9 %collective-permute-start = (bf16[256,2176]{1,0:T(8,128)(2,1)S(1)}, bf16[256,2176]{1,0:T(8,128)(2,1)S(1)}, u32[]{:S(2)}, u32[]{:S(2)}) collective-permute-start(bf16[256,2176]{1,0:T(8,128)(2,1)S(1)} %bitcast.41), channel_id=1, source_target_pairs={{0,8},{8,0},{1,9},{9,1},{2,10},{10,2},{3,11},{11,3},{4,12},{12,4},... | collective-permute-start | bytes 3342344 | tf_op jit(solution)/shard_map/gather_core_x/ppermute | solution.py:293
  54.4 0.7 broadcast_in_dim.23
  55.1 4.4 %all-to-all-start.2 = ((bf16[8,128,128]{2,1,0:T(8,128)(2,1)}), bf16[8,128,128]{2,1,0:T(8,128)(2,1)S(1)}, u32[]{:S(2)}, u32[]{:S(2)}) async-start(bf16[8,128,128]{2,1,0:T(8,128)(2,1)} %bitcast.14), calls=%async_computation.2 | async-start | bytes 524288 | tf_op jit(solution)/shard_map/gather_core_x/all_to_all | solution.py:21
  59.5 0.1 pad_add_fusion.idx
  59.6 0.0 collective-permute-done.other_ref
  59.6 0.0 copy-start
  59.6 1.0 copy-done
  60.6 0.0 copy-start.1
  60.6 1.2 %copy-done.1 = bf16[256,2176]{1,0:T(8,128)(2,1)S(1)} copy-done((bf16[256,2176]{1,0:T(8,128)(2,1)S(1)}, bf16[256,2176]{1,0:T(8,128)(2,1)}, u32[]{:S(2)}) %copy-start.1) | copy-done | bytes 1114136
  61.8 1.8 %standardize_a.1 = (bf16[512,2048]{1,0:T(8,128)(2,1)S(1)}, f32[8,2048]{1,0:T(8,128)S(1)}) custom-call(s32[4]{0:T(128)S(1)} %pad_add_fusion.idx, bf16[256,2176]{1,0:T(8,128)(2,1)S(1)} %bitcast.43, bf16[256,2176]{1,0:T(8,128)(2,1)S(1)} %copy-done.1), custom_call_target="tpu_custom_call" | custom-call | flops 10485760 | bytes 4194304 | tf_op jit(solution)/shard_map/standardize_a/pallas_call | solution.py:75
  63.7 2.8 %all-to-all-done.2 = bf16[8,128,128]{2,1,0:T(8,128)(2,1)S(1)} async-done(((bf16[8,128,128]{2,1,0:T(8,128)(2,1)}), bf16[8,128,128]{2,1,0:T(8,128)(2,1)S(1)}, u32[]{:S(2)}, u32[]{:S(2)}) %all-to-all-start.2) | async-done | bytes 262176 | tf_op jit(solution)/shard_map/gather_core_x/all_to_all | solution.py:21
  66.4 2.5 %tile.1 = (f32[2048,256]{1,0:T(8,128)}, bf16[512,256]{1,0:T(8,128)(2,1)S(1)}, bf16[512,256]{1,0:T(8,128)(2,1)S(1)}, f32[24,256]{1,0:T(8,128)S(1)}) custom-call(s32[4]{0:T(128)S(1)} %pad_add_fusion.idx, bf16[512,2048]{1,0:T(8,128)(2,1)S(1)} %get-tuple-element.16.a_ref.norm_ref, bf16[2,2,2,128,128]{4,3,2,1,0:T(8,128)(2,1)S(1)} %bitcast.44), custom_call_target="tpu_custom_call" | custom-call | flops 1610612736 | bytes 4194304 | tf_op jit(solution)/shard_map/tile/pallas_call | solution.py:162
  69.0 3.7 %collective-permute-start.1 = (bf16[256,256]{1,0:T(8,128)(2,1)S(1)}, bf16[256,256]{1,0:T(8,128)(2,1)S(1)}, u32[]{:S(2)}, u32[]{:S(2)}) collective-permute-start(bf16[256,256]{1,0:T(8,128)(2,1)S(1)} %slice.99), channel_id=1, source_target_pairs={{0,3},{1,2},{2,1},{3,0},{4,7},{5,6},{6,5},{7,4},{8,11},{9,10},{10,... | collective-permute-start | bytes 393224 | tf_op jit(solution)/shard_map/sum_b_x_reduce_z/ppermute | solution.py:308
  72.7 0.1 pad.3.clone
  72.8 1.5 %sum_b_x_reduce_z.1 = bf16[8,16,768]{2,1,0:T(8,128)(2,1)} custom-call(s32[4]{0:T(128)S(1)} %pad_add_fusion.idx, bf16[512,256]{1,0:T(8,128)(2,1)S(1)} %get-tuple-element.20.norm_ref, f32[24,256]{1,0:T(8,128)S(1)} %get-tuple-element.21.tail), custom_call_target="tpu_custom_call" | custom-call | flops 536870912 | bytes 2097152 | tf_op jit(solution)/shard_map/sum_b_x_reduce_z/pallas_call | solution.py:208
  74.3 6.9 %all-to-all-start.3 = ((bf16[8,16,768]{2,1,0:T(8,128)(2,1)}), bf16[8,16,768]{2,1,0:T(8,128)(2,1)S(1)}, u32[]{:S(2)}, u32[]{:S(2)}) async-start(bf16[8,16,768]{2,1,0:T(8,128)(2,1)} %sum_b_x_reduce_z.1), calls=%async_computation.3 | async-start | bytes 393216 | tf_op jit(solution)/shard_map/sum_b_x_reduce_z/all_to_all | solution.py:21
  81.3 0.0 collective-permute-done.1
  81.3 1.9 %collective-permute-start.2 = (bf16[128,256]{1,0:T(8,128)(2,1)S(1)}, bf16[128,256]{1,0:T(8,128)(2,1)S(1)}, u32[]{:S(2)}, u32[]{:S(2)}) collective-permute-start(bf16[128,256]{1,0:T(8,128)(2,1)S(1)} %slice.172), channel_id=1, source_target_pairs={{0,1},{1,0},{2,3},{3,2},{4,5},{5,4},{6,7},{7,6},{8,9},{9,8},{10,11... | collective-permute-start | bytes 196616 | tf_op jit(solution)/shard_map/sum_b_x_reduce_z/ppermute | solution.py:312
  83.3 4.2 %collective-permute-done.2 = bf16[128,256]{1,0:T(8,128)(2,1)S(1)} collective-permute-done((bf16[128,256]{1,0:T(8,128)(2,1)S(1)}, bf16[128,256]{1,0:T(8,128)(2,1)S(1)}, u32[]{:S(2)}, u32[]{:S(2)}) %collective-permute-start.2) | collective-permute-done | bytes 65568 | tf_op jit(solution)/shard_map/sum_b_x_reduce_z/ppermute | solution.py:312
  87.5 8.2 %collective-permute-start.3 = (bf16[128,256]{1,0:T(8,128)(2,1)S(1)}, bf16[128,256]{1,0:T(8,128)(2,1)S(1)}, u32[]{:S(2)}, u32[]{:S(2)}) collective-permute-start(bf16[128,256]{1,0:T(8,128)(2,1)S(1)} %fusion), channel_id=1, source_target_pairs={{0,4},{4,0},{1,5},{5,1},{2,6},{6,2},{3,7},{7,3},{8,12},{12,8},{9,1... | collective-permute-start | bytes 196616 | tf_op jit(solution)/shard_map/reduce_yc/ppermute | solution.py:323
  95.7 0.0 all-to-all-done.3
  95.9 0.7 maximum_maximum_fusion
  96.6 0.0 copy-start.3
  96.6 3.5 %all-to-all-start.4 = ((f32[8,8,1024]{2,1,0:T(8,128)}), f32[8,8,1024]{2,1,0:T(8,128)S(1)}, u32[]{:S(2)}, u32[]{:S(2)}) async-start(f32[8,8,1024]{2,1,0:T(8,128)} %maximum_maximum_fusion), calls=%async_computation.4 | async-start | bytes 524288 | tf_op jit(solution)/shard_map/reduce_yc/all_to_all | solution.py:21
  100.2 2.3 %collective-permute-done.3 = bf16[128,256]{1,0:T(8,128)(2,1)S(1)} collective-permute-done((bf16[128,256]{1,0:T(8,128)(2,1)S(1)}, bf16[128,256]{1,0:T(8,128)(2,1)S(1)}, u32[]{:S(2)}, u32[]{:S(2)}) %collective-permute-start.3) | collective-permute-done | bytes 65568 | tf_op jit(solution)/shard_map/reduce_yc/ppermute | solution.py:323
  102.5 5.1 %all-to-all-done.4 = f32[8,8,1024]{2,1,0:T(8,128)S(1)} async-done(((f32[8,8,1024]{2,1,0:T(8,128)}), f32[8,8,1024]{2,1,0:T(8,128)S(1)}, u32[]{:S(2)}, u32[]{:S(2)}) %all-to-all-start.4) | async-done | bytes 262176 | tf_op jit(solution)/shard_map/reduce_yc/all_to_all | solution.py:21
  107.7 0.1 maximum_maximum_fusion.1
  107.8 0.7 broadcast_in_dim.56
  108.5 3.5 %all-to-all-start.5 = ((bf16[4,144,256]{2,1,0:T(8,128)(2,1)}), bf16[4,144,256]{2,1,0:T(8,128)(2,1)S(1)}, u32[]{:S(2)}, u32[]{:S(2)}) async-start(bf16[4,144,256]{2,1,0:T(8,128)(2,1)} %broadcast_in_dim.56), calls=%async_computation.5 | async-start | bytes 589824 | tf_op jit(solution)/shard_map/gather_b_x/all_to_all | solution.py:21
  112.0 0.0 copy-done.3
  112.1 0.8 subtract_multiply_fusion.shifted_ref
  112.9 6.0 %all-to-all-done.5.got_ref = bf16[4,144,256]{2,1,0:T(8,128)(2,1)S(1)} async-done(((bf16[4,144,256]{2,1,0:T(8,128)(2,1)}), bf16[4,144,256]{2,1,0:T(8,128)(2,1)S(1)}, u32[]{:S(2)}, u32[]{:S(2)}) %all-to-all-start.5) | async-done | bytes 294944 | tf_op jit(solution)/shard_map/gather_b_x/all_to_all | solution.py:21
  118.9 1.2 finish.1
  (37 shorter events, 0.5 us)
Async XLA Ops:
  0.6 1.4 %copy-start.2 = (bf16[8,2048]{1,0:T(8,128)(2,1)S(1)}, bf16[8,2048]{1,0:T(8,128)(2,1)}, u32[]{:S(2)}) copy-start(bf16[8,2048]{1,0:T(8,128)(2,1)} %param.2) | copy-start | bytes 98308
  52.4 7.2 %collective-permute-start = (bf16[256,2176]{1,0:T(8,128)(2,1)S(1)}, bf16[256,2176]{1,0:T(8,128)(2,1)S(1)}, u32[]{:S(2)}, u32[]{:S(2)}) collective-permute-start(bf16[256,2176]{1,0:T(8,128)(2,1)S(1)} %bitcast.41), channel_id=1, source_target_pairs={{0,8},{8,0},{1,9},{9,1},{2,10},{10,2},{3,11},{11,3},{4,12},{12,4},... | collective-permute-start | bytes 3342344 | tf_op jit(solution)/shard_map/gather_core_x/ppermute | solution.py:293
  55.1 11.3 %all-to-all-start.2 = ((bf16[8,128,128]{2,1,0:T(8,128)(2,1)}), bf16[8,128,128]{2,1,0:T(8,128)(2,1)S(1)}, u32[]{:S(2)}, u32[]{:S(2)}) async-start(bf16[8,128,128]{2,1,0:T(8,128)(2,1)} %bitcast.14), calls=%async_computation.2 | async-start | bytes 524288 | tf_op jit(solution)/shard_map/gather_core_x/all_to_all | solution.py:21
  59.6 1.0 copy-start
  60.6 1.2 %copy-start.1 = (bf16[256,2176]{1,0:T(8,128)(2,1)S(1)}, bf16[256,2176]{1,0:T(8,128)(2,1)}, u32[]{:S(2)}) copy-start(bf16[256,2176]{1,0:T(8,128)(2,1)} %copy-done) | copy-start | bytes 3342340
  69.0 12.3 %collective-permute-start.1 = (bf16[256,256]{1,0:T(8,128)(2,1)S(1)}, bf16[256,256]{1,0:T(8,128)(2,1)S(1)}, u32[]{:S(2)}, u32[]{:S(2)}) collective-permute-start(bf16[256,256]{1,0:T(8,128)(2,1)S(1)} %slice.99), channel_id=1, source_target_pairs={{0,3},{1,2},{2,1},{3,0},{4,7},{5,6},{6,5},{7,4},{8,11},{9,10},{10,... | collective-permute-start | bytes 393224 | tf_op jit(solution)/shard_map/sum_b_x_reduce_z/ppermute | solution.py:308
  74.3 21.4 %all-to-all-start.3 = ((bf16[8,16,768]{2,1,0:T(8,128)(2,1)}), bf16[8,16,768]{2,1,0:T(8,128)(2,1)S(1)}, u32[]{:S(2)}, u32[]{:S(2)}) async-start(bf16[8,16,768]{2,1,0:T(8,128)(2,1)} %sum_b_x_reduce_z.1), calls=%async_computation.3 | async-start | bytes 393216 | tf_op jit(solution)/shard_map/sum_b_x_reduce_z/all_to_all | solution.py:21
  81.3 6.2 %collective-permute-start.2 = (bf16[128,256]{1,0:T(8,128)(2,1)S(1)}, bf16[128,256]{1,0:T(8,128)(2,1)S(1)}, u32[]{:S(2)}, u32[]{:S(2)}) collective-permute-start(bf16[128,256]{1,0:T(8,128)(2,1)S(1)} %slice.172), channel_id=1, source_target_pairs={{0,1},{1,0},{2,3},{3,2},{4,5},{5,4},{6,7},{7,6},{8,9},{9,8},{10,11... | collective-permute-start | bytes 196616 | tf_op jit(solution)/shard_map/sum_b_x_reduce_z/ppermute | solution.py:312
  87.5 15.0 %collective-permute-start.3 = (bf16[128,256]{1,0:T(8,128)(2,1)S(1)}, bf16[128,256]{1,0:T(8,128)(2,1)S(1)}, u32[]{:S(2)}, u32[]{:S(2)}) collective-permute-start(bf16[128,256]{1,0:T(8,128)(2,1)S(1)} %fusion), channel_id=1, source_target_pairs={{0,4},{4,0},{1,5},{5,1},{2,6},{6,2},{3,7},{7,3},{8,12},{12,8},{9,1... | collective-permute-start | bytes 196616 | tf_op jit(solution)/shard_map/reduce_yc/ppermute | solution.py:323
  96.6 15.4 %copy-start.3 = (bf16[8,2048]{1,0:T(8,128)(2,1)S(1)}, bf16[8,2048]{1,0:T(8,128)(2,1)}, u32[]{:S(2)}) copy-start(bf16[8,2048]{1,0:T(8,128)(2,1)} %param.2) | copy-start | bytes 98308
  96.6 11.0 %all-to-all-start.4 = ((f32[8,8,1024]{2,1,0:T(8,128)}), f32[8,8,1024]{2,1,0:T(8,128)S(1)}, u32[]{:S(2)}, u32[]{:S(2)}) async-start(f32[8,8,1024]{2,1,0:T(8,128)} %maximum_maximum_fusion), calls=%async_computation.4 | async-start | bytes 524288 | tf_op jit(solution)/shard_map/reduce_yc/all_to_all | solution.py:21
  108.5 10.4 %all-to-all-start.5 = ((bf16[4,144,256]{2,1,0:T(8,128)(2,1)}), bf16[4,144,256]{2,1,0:T(8,128)(2,1)S(1)}, u32[]{:S(2)}, u32[]{:S(2)}) async-start(bf16[4,144,256]{2,1,0:T(8,128)(2,1)} %broadcast_in_dim.56), calls=%async_computation.5 | async-start | bytes 589824 | tf_op jit(solution)/shard_map/gather_b_x/all_to_all | solution.py:21
